TPU v7x, 32 devices: a whole 2x2x4 slice. The times are simulated.
32 devices in a mesh: gx: 16 (over z, y, core), gy: 2 (over x).
Axes of the slice: x: 2, y: 2, z: 4, core: 2. Of those that a mesh axis runs over, the one named last changes fastest.
Arguments:
- features: bfloat16 [8192, 8, 8, 256], P('gx', 'gy'), may hold values from -6 to 6
- spectral_weight: bfloat16 [16, 2, 256, 256], replicated, may hold values from -6 to 6
- conv_taps: float32 [3, 256], replicated, may hold values from -3 to 3
- w_in: bfloat16 [256, 1024], replicated, may hold values from -0.375 to 0.375
- bias_in: float32 [1024], replicated, may hold values from -3 to 3
- w_out: bfloat16 [1024, 256], replicated, may hold values from -0.1875 to 0.1875
- bias_out: float32 [256], replicated, may hold values from -3 to 3
Outputs:
- layer_out: bfloat16 [8192, 8, 8, 256], P('gx', 'gy')
All inputs are finite; a program needn't handle non-finite values.
Results may differ from a plain program's by a relative error of at most 0.0065.
Values may be sent and summed in bfloat16 or wider, within the bound.
No kernel may reach another device: no remote copies, remote signals or barrier semaphores. Data moves between devices by JAX's collectives and lax.ppermute only.
A program may use at most 128 MiB of HBM per device.

v0:
```python
import math

import jax
import jax.numpy as jnp
from jax import lax
from jax.sharding import PartitionSpec as P


def with_halo(cells, sides, width):
    for axis, dim in sides:
        count = lax.axis_size(axis)
        ends = count - 1
        head = lax.slice_in_dim(cells, 0, width, axis=dim)
        tail = lax.slice_in_dim(cells, cells.shape[dim] - width, cells.shape[dim], axis=dim)
        cells = jnp.concatenate(
            [
                lax.ppermute(tail, axis, [(i, (i + 1) % count) for i in range(ends)]),
                cells,
                lax.ppermute(head, axis, [((i + 1) % count, i) for i in range(ends)]),
            ],
            axis=dim,
        )
    return cells


def make_tables(positions, total, mode_count):
    waves = jnp.arange(mode_count, dtype=jnp.int32)
    product = waves[:, None] * positions[None, :] % total
    angles = 2.0 * math.pi / total * product.astype(jnp.float32)
    scale = 1.0 / math.sqrt(total)
    cosines = jnp.cos(angles)
    sines = jnp.sin(angles)
    forward = (jnp.concatenate([cosines, -sines], 0) * scale).astype(jnp.bfloat16)
    amplitude = jnp.where(waves == 0, 1.0, 2.0).astype(jnp.float32)[:, None]
    inverse = (jnp.concatenate([amplitude * cosines, -amplitude * sines], 0) * scale).T.astype(
        jnp.bfloat16
    )
    return (forward, inverse)


def local(features, spectral_weight, conv_taps, w_in, bias_in, w_out, bias_out):
    x_rows, y_rows, z_cols, channels = features.shape
    gx_size = lax.axis_size("gx")
    mode_count = spectral_weight.shape[0]
    positions = lax.axis_index("gx") * x_rows + jnp.arange(x_rows, dtype=jnp.int32)
    forward, inverse = make_tables(positions, x_rows * gx_size, mode_count)
    col_count = features.shape[2]
    row_count = y_rows * col_count
    padded = with_halo(features, (("gy", 1),), 1)
    flattened = features.reshape(x_rows, row_count * channels)
    spectrum = jnp.dot(forward, flattened, preferred_element_type=jnp.float32)
    spectrum = spectrum.reshape(2, mode_count * row_count, channels)
    owned = lax.psum_scatter(spectrum, "gx", scatter_dimension=1, tiled=True).astype(jnp.bfloat16)
    per_mode = gx_size // mode_count
    owner_mode = lax.axis_index("gx") // per_mode
    chosen = lax.dynamic_index_in_dim(spectral_weight, owner_mode, 0, keepdims=False)
    mixed_real = jnp.dot(owned[0], chosen[0], preferred_element_type=jnp.float32) - jnp.dot(
        owned[1], chosen[1], preferred_element_type=jnp.float32
    )
    mixed_imag = jnp.dot(owned[0], chosen[1], preferred_element_type=jnp.float32) + jnp.dot(
        owned[1], chosen[0], preferred_element_type=jnp.float32
    )
    mixed_own = jnp.stack([mixed_real, mixed_imag]).astype(jnp.bfloat16)
    mixed = lax.all_gather(mixed_own, "gx", axis=1, tiled=True)
    mixed = mixed.reshape(2 * mode_count, row_count * channels)
    spectral = jnp.dot(inverse, mixed, preferred_element_type=jnp.float32)
    spectral = spectral.reshape(x_rows, y_rows, col_count, channels)
    conv = (
        conv_taps[0] * padded[:, :-2].astype(jnp.float32)
        + conv_taps[1] * padded[:, 1:-1].astype(jnp.float32)
        + conv_taps[2] * padded[:, 2:].astype(jnp.float32)
    )
    joined = (spectral + conv).astype(jnp.bfloat16).reshape(x_rows * row_count, channels)
    hidden = jax.nn.gelu(
        jnp.dot(joined, w_in, preferred_element_type=jnp.float32) + bias_in, approximate=True
    ).astype(jnp.bfloat16)
    result = (
        features.reshape(x_rows * row_count, channels).astype(jnp.float32)
        + jnp.dot(hidden, w_out, preferred_element_type=jnp.float32)
        + bias_out
    )
    return result.astype(jnp.bfloat16).reshape(x_rows, y_rows, col_count, channels)


def solution(mesh):
    return jax.shard_map(
        local,
        mesh=mesh,
        in_specs=(P("gx", "gy", None, None), P(), P(), P(), P(), P(), P()),
        out_specs=P("gx", "gy", None, None),
        check_vma=False,
    )
```

profile of v0, /device:TPU:0, one launch (start us, length us, event | category | flops | bytes accessed | tf_op | source)
XLA Modules:
  0.0 179.0 jit_solution(12710664781945795625)
XLA Ops:
  6.5 0.0 copy-start
  6.5 0.0 reduce-scatter.2.cloned.1.call-start
  6.5 16.7 %copy.22 = bf16[64,8,32,256]{3,1,2,0:T(8,128)(2,1)} copy(bf16[64,8,32,256]{3,2,1,0:T(8,128)(2,1)} %bitcast.45) | data formatting | bytes 16777216
  23.2 0.2 broadcast_multiply_fusion.1
  23.4 4.9 %fusion.36 = f32[32,8192]{1,0:T(8,128)S(1)} fusion(bf16[512,8192]{1,0:T(8,128)(2,1)} %bitcast.44, f32[16,512]{1,0:T(8,128)S(1)} %get-tuple-element.13, f32[16,512]{1,0:T(8,128)S(1)} %get-tuple-element.15), kind=kOutput, calls=%fused_computation.39 | convolution fusion | flops 268484608 | bytes 9502720 | tf_op jit(solution)/shard_map/dot_general | solution.py:51
  28.3 1.2 reshape.43
  29.4 0.0 reduce-scatter.2.cloned.1.call-update
  29.5 10.9 %fusion.62 = (bf16[512,4,8,256]{3,0,2,1:T(8,128)(2,1)S(1)}, f32[512,4,8,256]{3,0,2,1:T(8,128)}) fusion(bf16[512,4,8,256]{3,2,1,0:T(8,128)(2,1)} %param.7), kind=kLoop, calls=%fused_computation.71 | loop fusion | flops 4194304 | bytes 33554432 | tf_op args[0]
  40.3 3.4 %copy-done.1 = bf16[512,4,8,256]{3,0,2,1:T(8,128)(2,1)} copy-done((bf16[512,4,8,256]{3,0,2,1:T(8,128)(2,1)}, bf16[512,4,8,256]{3,0,2,1:T(8,128)(2,1)S(1)}, u32[]{:S(2)}) %copy-start.1) | copy-done | bytes 8388632
  43.7 2.4 %fusion.61 = (bf16[512,1,8,256]{3,0,2,1:T(8,128)(2,1)}, bf16[512,1,8,256]{3,0,2,1:T(8,128)(2,1)}) fusion(bf16[512,4,8,256]{3,0,2,1:T(8,128)(2,1)S(1)} %get-tuple-element.7), kind=kLoop, calls=%fused_computation.70 | loop fusion | bytes 8388608 | tf_op jit(solution)/shard_map/slice | solution.py:14
  46.1 6.3 %collective-permute-start = (bf16[512,1,8,256]{3,0,2,1:T(8,128)(2,1)}, bf16[512,1,8,256]{3,0,2,1:T(8,128)(2,1)}, u32[]{:S(2)}, u32[]{:S(2)}) collective-permute-start(bf16[512,1,8,256]{3,0,2,1:T(8,128)(2,1)} %get-tuple-element.5), channel_id=1, source_target_pairs={{0,1},{2,3},{4,5},{6,7},{8,9},{10,11},{12,13},{14,15},{16,17},{18,... | collective-permute-start | bytes 6291464 | tf_op jit(solution)/shard_map/ppermute | solution.py:17
  52.4 1.3 collective-permute-start.1
  53.7 0.0 copy-start.2
  53.7 17.7 %copy.14 = f32[512,4,8,256]{3,2,1,0:T(8,128)} copy(f32[512,4,8,256]{3,0,2,1:T(8,128)} %get-tuple-element.8) | data formatting | bytes 33554432 | tf_op jit(solution)/shard_map/convert_element_type | solution.py:78
  71.4 0.0 copy-done.2
  71.4 18.3 %reduce-scatter.2.cloned.1.call-done = f32[2,32,256]{2,1,0:T(8,128)} async-done(((f32[2,512,256]{2,1,0:T(8,128)}), f32[2,32,256]{2,1,0:T(8,128)}) %reduce-scatter.2.cloned.1.call-update) | async-done | bytes 65552 | tf_op jit(solution)/shard_map/reduce_scatter | solution.py:53
  89.7 0.8 convert_element_type.43
  90.5 1.0 fusion.30
  91.6 1.1 fusion.23
  92.6 1.1 fusion.29
  93.7 1.1 fusion.24
  94.8 20.8 %all_gather.3 = bf16[2,512,256]{2,1,0:T(8,128)(2,1)S(1)} all-gather(bf16[2,32,256]{2,1,0:T(8,128)(2,1)S(1)} %pad_maximum_fusion.2), channel_id=1, replica_groups=mesh['gx'=16,'gy'=2] {'gx'}, dimensions={1}, use_global_device_ids=true | all-gather | bytes 557056 | tf_op jit(solution)/shard_map/all_gather | solution.py:64
  115.6 0.2 reshape.44
  115.8 0.1 copy.23
  116.0 0.0 collective-permute-done
  116.0 0.0 collective-permute-done.1
  116.0 13.5 %add_convert_fusion = bf16[512,4,8,256]{3,0,2,1:T(8,128)(2,1)} fusion(bf16[512,1,8,256]{3,0,2,1:T(8,128)(2,1)} %collective-permute-done.1, bf16[512,4,8,256]{3,0,2,1:T(8,128)(2,1)} %copy-done.1, bf16[512,1,8,256]{3,0,2,1:T(8,128)(2,1)} %collective-permute-done, f32[256]{0:T(256)S(1)} %bitcast.51, f32[256]{0:T(256)S(1)} %bitcast.52, f32[256]{0:T(256)S(1)} %bitcast.50, ...), kind=kOutput, calls=%fused_computation.13 | convolution fusion | flops 318816256 | bytes 21564416 | tf_op jit(solution)/shard_map/dot_general | solution.py:66
  129.5 11.4 %copy.20 = bf16[512,4,8,256]{3,2,1,0:T(8,128)(2,1)} copy(bf16[512,4,8,256]{3,0,2,1:T(8,128)(2,1)} %add_convert_fusion) | data formatting | bytes 16777216 | tf_op jit(solution)/shard_map/convert_element_type | solution.py:73
  140.9 0.0 copy-done
  140.9 0.0 copy-done.3
  140.9 0.0 copy-done.4
  140.9 31.3 %fusion.16 = bf16[16384,256]{1,0:T(8,128)(2,1)} fusion(f32[16384,256]{1,0:T(8,128)} %bitcast.46, bf16[1024,256]{1,0:T(8,128)(2,1)S(1)} %copy-done, f32[1024]{0:T(1024)S(1)} %copy-done.4, bf16[16384,256]{1,0:T(8,128)(2,1)} %bitcast.47, bf16[256,1024]{1,0:T(8,128)(2,1)S(1)} %copy-done.3, f32[256]{0:T(256)S(1)} %copy-done.5), kind=kOutput, calls=%fused_computation.12 | convolution fusion | flops 17360224256 | bytes 34608128 | tf_op jit(solution)/shard_map/dot_general | solution.py:79
  (9 shorter events, 0.0 us)
Async XLA Ops:
  6.5 134.4 %copy-start = (bf16[1024,256]{1,0:T(8,128)(2,1)S(1)}, bf16[1024,256]{1,0:T(8,128)(2,1)}, u32[]{:S(2)}) copy-start(bf16[1024,256]{1,0:T(8,128)(2,1)} %param.12) | copy-start | bytes 1572868
  6.5 83.2 %reduce-scatter.2.cloned.1.call-start = ((), (), s32[]{:S(2)}) async-start(), calls=%async_computation.1 | async-start | bytes 1114112 | tf_op jit(solution)/shard_map/reduce_scatter | solution.py:53
  40.3 3.4 %copy-start.1 = (bf16[512,4,8,256]{3,0,2,1:T(8,128)(2,1)}, bf16[512,4,8,256]{3,0,2,1:T(8,128)(2,1)S(1)}, u32[]{:S(2)}) copy-start(bf16[512,4,8,256]{3,0,2,1:T(8,128)(2,1)S(1)} %get-tuple-element.7) | copy-start | bytes 25165828
  46.1 69.9 %collective-permute-start = (bf16[512,1,8,256]{3,0,2,1:T(8,128)(2,1)}, bf16[512,1,8,256]{3,0,2,1:T(8,128)(2,1)}, u32[]{:S(2)}, u32[]{:S(2)}) collective-permute-start(bf16[512,1,8,256]{3,0,2,1:T(8,128)(2,1)} %get-tuple-element.5), channel_id=1, source_target_pairs={{0,1},{2,3},{4,5},{6,7},{8,9},{10,11},{12,13},{14,15},{16,17},{18,... | collective-permute-start | bytes 6291464 | tf_op jit(solution)/shard_map/ppermute | solution.py:17
  52.4 63.6 %collective-permute-start.1 = (bf16[512,1,8,256]{3,0,2,1:T(8,128)(2,1)}, bf16[512,1,8,256]{3,0,2,1:T(8,128)(2,1)}, u32[]{:S(2)}, u32[]{:S(2)}) collective-permute-start(bf16[512,1,8,256]{3,0,2,1:T(8,128)(2,1)} %get-tuple-element.6), channel_id=1, source_target_pairs={{1,0},{3,2},{5,4},{7,6},{9,8},{11,10},{13,12},{15,14},{17,16},{19,... | collective-permute-start | bytes 6291464 | tf_op jit(solution)/shard_map/ppermute | solution.py:19
  53.7 17.7 %copy-start.2 = (f32[3,256]{1,0:T(4,128)S(1)}, f32[3,256]{1,0:T(4,128)}, u32[]{:S(2)}) copy-start(f32[3,256]{1,0:T(4,128)} %param.9) | copy-start | bytes 9220
  129.4 11.5 %copy-start.3 = (bf16[256,1024]{1,0:T(8,128)(2,1)S(1)}, bf16[256,1024]{1,0:T(8,128)(2,1)}, u32[]{:S(2)}) copy-start(bf16[256,1024]{1,0:T(8,128)(2,1)} %param.10) | copy-start | bytes 1572868
  129.5 11.5 %copy-start.4 = (f32[1024]{0:T(1024)S(1)}, f32[1024]{0:T(1024)}, u32[]{:S(2)}) copy-start(f32[1024]{0:T(1024)} %param.11) | copy-start | bytes 12292
  129.5 11.5 %copy-start.5 = (f32[256]{0:T(256)S(1)}, f32[256]{0:T(256)}, u32[]{:S(2)}) copy-start(f32[256]{0:T(256)} %param.13) | copy-start | bytes 3076
Sparse Core Ops, SparseCore 0:
  29.6 60.0 reduce-scatter.1
where the time goes:
time: 179 us
  matrix products  53.8 us (30%)
  local copies, waits for them, and re-layouts  53.1 us (30%)
  blocking collectives  20.8 us (12%)
  waiting for transfers between devices  18.3 us (10%)
  between operations  13.5 us (8%)
  other arithmetic  11.9 us (7%)
  starting transfers between devices  7.54 us (4%)
    dot_general x1, matrix products, local(): jnp.dot(hidden, w_out, preferred_element_type=jnp.float32)  31.3 us
    all_gather x1, blocking collectives, local(): mixed = lax.all_gather(mixed_own, 'gx', axis=1, tiled=True)  20.8 us
    unnamed x14, local copies, waits for them, and re-layouts  20.2 us
    reduce_scatter x1, waiting for transfers between devices, local(): lax.psum_scatter(spectrum, 'gx', scatter_dimension=1, tiled=True)  18.3 us
    convert_element_type x1, local copies, waits for them, and re-layouts, local(): features.reshape(x_rows * row_count, channels).astype(jnp.float32)  17.7 us
    dot_general x1, matrix products, local(): spectral = jnp.dot(inverse, mixed, preferred_element_type=jnp.float32)  13.5 us
    convert_element_type x1, local copies, waits for them, and re-layouts, local(): (spectral + conv).astype(jnp.bfloat16).reshape(x_rows * row_count, channels)  11.4 us
    unnamed x1, other arithmetic  10.9 us
  transfers between devices with their start and end apart: 3, of which 1 were waited for; matrix products, arithmetic and copies ran while one was open for 20% of the time, Pallas kernels for 0%

commit v1 on v0

v1 whole, which is shorter than its diff:
```python
import functools
import math

import jax
import jax.numpy as jnp
from jax import lax
from jax.experimental import pallas as pl
from jax.experimental.pallas import tpu as pltpu
from jax.sharding import PartitionSpec as P

F32 = jnp.float32
BF16 = jnp.bfloat16
GELU_A = math.sqrt(2.0 / math.pi)
GELU_B = GELU_A * 0.044715
VMEM_BYTES = 50 * 2**20


def wave_tables(waves, positions, total):
    product = waves[:, None] * positions[None, :] % total
    angles = 2.0 * math.pi / total * product.astype(F32)
    scale = 1.0 / math.sqrt(total)
    cosines = jnp.cos(angles)
    sines = jnp.sin(angles)
    forward = (jnp.stack([cosines, -sines], 1) * scale).astype(BF16)
    amplitude = jnp.where(waves == 0, 1.0, 2.0).astype(F32)[:, None]
    inverse = (jnp.stack([amplitude * cosines, -amplitude * sines], 1) * scale).astype(BF16)
    rows = 2 * waves.shape[0]
    return forward.reshape(rows, -1), inverse.reshape(rows, -1)


def forward_kernel(half, table_ref, inverse_ref, field_ref, send_ref, keep_ref, inv_ref, total_ref):
    step = pl.program_id(0)
    xb, rows, cols, channels = field_ref.shape
    waves = table_ref.shape[1]
    width = xb * cols
    spread = (
        lax.broadcasted_iota(jnp.int32, (xb, width), 1) // cols
        == lax.broadcasted_iota(jnp.int32, (xb, width), 0)
    )
    wide = jnp.dot(table_ref[0], spread.astype(F32).astype(BF16), preferred_element_type=F32)
    same = lax.broadcasted_iota(jnp.int32, (1, cols, width), 2) % cols == lax.broadcasted_iota(
        jnp.int32, (1, cols, width), 1
    )
    wide = jnp.where(same, wide[:, None, :], 0.0).reshape(waves * cols, width).astype(BF16)

    @pl.when(step == 0)
    def _():
        total_ref[...] = jnp.zeros_like(total_ref)

    for row in range(rows):
        block = field_ref[:, row].reshape(width, channels)
        total_ref[row] += jnp.dot(wide, block, preferred_element_type=F32)

    columns = waves * cols
    spread = (
        lax.broadcasted_iota(jnp.int32, (waves, columns), 1) // cols
        == lax.broadcasted_iota(jnp.int32, (waves, columns), 0)
    )
    tall = jnp.dot(inverse_ref[...], spread.astype(F32).astype(BF16), preferred_element_type=F32)
    same = lax.broadcasted_iota(jnp.int32, (1, cols, columns), 2) % cols == lax.broadcasted_iota(
        jnp.int32, (1, cols, columns), 1
    )
    tall = jnp.where(same, tall[:, None, :], 0.0).reshape(width, columns)
    inv_ref[...] = tall.astype(BF16)

    @pl.when(step == pl.num_programs(0) - 1)
    def _():
        for row in range(rows):
            part = total_ref[row].reshape(waves, cols, channels)
            keep_ref[:, row] = part[:half]
            send_ref[:, row] = part[half:].astype(BF16)


def forward_transform(features, table, inverse, xb, half):
    x_rows, y_rows, cols, channels = features.shape
    waves = inverse.shape[1]
    steps = x_rows // xb
    shape = (half, y_rows, cols, channels)
    rest = (waves - half, y_rows, cols, channels)
    whole = lambda i: (0, 0, 0, 0)
    return pl.pallas_call(
        functools.partial(forward_kernel, half),
        grid=(steps,),
        in_specs=[
            pl.BlockSpec((1, waves, xb), lambda i: (i, 0, 0)),
            pl.BlockSpec((xb, waves), lambda i: (i, 0)),
            pl.BlockSpec((xb, y_rows, cols, channels), lambda i: (i, 0, 0, 0)),
        ],
        out_specs=[
            pl.BlockSpec(rest, whole),
            pl.BlockSpec(shape, whole),
            pl.BlockSpec((xb * cols, waves * cols), lambda i: (i, 0)),
        ],
        out_shape=[
            jax.ShapeDtypeStruct(rest, BF16),
            jax.ShapeDtypeStruct(shape, F32),
            jax.ShapeDtypeStruct((x_rows * cols, waves * cols), BF16),
        ],
        scratch_shapes=[pltpu.VMEM((y_rows, waves * cols, channels), F32)],
        compiler_params=pltpu.CompilerParams(vmem_limit_bytes=VMEM_BYTES),
        cost_estimate=pl.CostEstimate(
            flops=2 * x_rows * y_rows * cols * cols * waves * channels,
            bytes_accessed=features.size * 2,
            transcendentals=0,
        ),
        name="forward",
    )(table, inverse, features)


def halve_kernel(half, keep_ref, got_ref, send_ref, next_ref):
    next_ref[...] = keep_ref[:half] + got_ref[:half].astype(F32)
    send_ref[...] = (keep_ref[half:] + got_ref[half:].astype(F32)).astype(BF16)


def halve(keep, got):
    half = keep.shape[0] // 2
    shape = (half,) + keep.shape[1:]
    return pl.pallas_call(
        functools.partial(halve_kernel, half),
        out_shape=[jax.ShapeDtypeStruct(shape, BF16), jax.ShapeDtypeStruct(shape, F32)],
        compiler_params=pltpu.CompilerParams(vmem_limit_bytes=VMEM_BYTES),
        name="halve",
    )(keep, got)


def add_kernel(keep_ref, got_ref, send_ref, next_ref):
    total = keep_ref[...] + got_ref[...].astype(F32)
    next_ref[...] = total
    send_ref[...] = total.astype(BF16)


def add(keep, got):
    return pl.pallas_call(
        add_kernel,
        out_shape=[
            jax.ShapeDtypeStruct(keep.shape, BF16),
            jax.ShapeDtypeStruct(keep.shape, F32),
        ],
        compiler_params=pltpu.CompilerParams(vmem_limit_bytes=VMEM_BYTES),
        name="add",
    )(keep, got)


def mix_kernel(which_ref, keep_ref, got_ref, weight_ref, out_ref):
    modes = weight_ref.shape[0]
    waves, rows, cols, channels = keep_ref.shape
    count = rows * cols
    for mode in range(modes):
        parts = []
        for p in range(2):
            at = 2 * mode + p
            part = keep_ref[at] + got_ref[at].astype(F32)
            parts.append(part.reshape(count, channels).astype(BF16))
        real, imag = parts
        weight_real = weight_ref[mode, 0]
        weight_imag = weight_ref[mode, 1]
        dot = functools.partial(jnp.dot, preferred_element_type=F32)
        mixed_real = dot(real, weight_real) - dot(imag, weight_imag)
        mixed_imag = dot(real, weight_imag) + dot(imag, weight_real)
        out_ref[2 * mode] = mixed_real.reshape(rows, cols, channels).astype(BF16)
        out_ref[2 * mode + 1] = mixed_imag.reshape(rows, cols, channels).astype(BF16)


def mix(keep, got, weight, which):
    waves, rows, cols, channels = keep.shape
    modes = waves // 2
    whole = lambda i, w: (0, 0, 0, 0)
    return pl.pallas_call(
        mix_kernel,
        grid_spec=pltpu.PrefetchScalarGridSpec(
            num_scalar_prefetch=1,
            grid=(1,),
            in_specs=[
                pl.BlockSpec(keep.shape, whole),
                pl.BlockSpec(keep.shape, whole),
                pl.BlockSpec((modes, 2, channels, channels), lambda i, w: (w[0], 0, 0, 0)),
            ],
            out_specs=pl.BlockSpec(keep.shape, whole),
        ),
        out_shape=jax.ShapeDtypeStruct(keep.shape, BF16),
        compiler_params=pltpu.CompilerParams(vmem_limit_bytes=VMEM_BYTES),
        name="mix",
    )(which, keep, got, weight)


def row_kernel(
    pieces, sub, rows_ref, before_ref, here_ref, after_ref, inv_ref, taps_ref,
    w_in_ref, bias_in_ref, w_out_ref, bias_out_ref, *rest
):
    piece_refs = rest[:pieces]
    out_ref, mixed_ref, joined_ref, hidden_ref = rest[-4:]
    xb = here_ref.shape[0]
    cols, channels = here_ref.shape[-2:]
    tokens = xb * cols

    @pl.when(pl.program_id(1) == 0)
    def _():
        at = 0
        for ref in piece_refs:
            count = ref.shape[0] * cols
            piece = ref[...].astype(F32).reshape(count, channels).astype(BF16)
            mixed_ref[at : at + count] = piece
            at += count

    taps = taps_ref[0]

    def load(ref, s):
        part = ref[s * sub // cols : (s + 1) * sub // cols]
        return part.reshape(sub, channels)

    def join(s):
        rows = slice(s * sub, (s + 1) * sub)
        spectral = jnp.dot(inv_ref[rows], mixed_ref[...], preferred_element_type=F32)
        conv = (
            taps[0:1] * load(before_ref, s).astype(F32)
            + taps[1:2] * load(here_ref, s).astype(F32)
            + taps[2:3] * load(after_ref, s).astype(F32)
        )
        joined_ref[rows] = (spectral + conv).astype(BF16)

    def expand(s):
        rows = slice(s * sub, (s + 1) * sub)
        x = jnp.dot(joined_ref[rows], w_in_ref[...], preferred_element_type=F32)
        x = (x + bias_in_ref[...]).astype(BF16)
        u = x * (BF16(GELU_A) + BF16(GELU_B) * (x * x))
        hidden_ref[rows] = x + x * jnp.tanh(u)

    def project(s):
        rows = slice(s * sub, (s + 1) * sub)
        y = jnp.dot(hidden_ref[rows], w_out_ref[...], preferred_element_type=F32)
        y = load(here_ref, s).astype(F32) + (0.5 * y + bias_out_ref[...])
        out_ref[s * sub // cols : (s + 1) * sub // cols] = y.reshape(
            (sub // cols,) + out_ref.shape[1:]
        ).astype(BF16)

    parts = tokens // sub
    for s in range(parts + 2):
        if s < parts:
            join(s)
        if 0 <= s - 1 < parts:
            expand(s - 1)
        if s >= 2:
            project(s - 2)


def rows_of(out, features, inv, taps, rows, w_in, bias_in, w_out, bias_out, pieces, xb, start, count, halo=None):
    x_rows, y_rows, cols, channels = features.shape
    hidden = w_in.shape[1]
    waves_cols = inv.shape[1]
    slots = taps.shape[0]
    block = (xb, 1, cols, channels)
    first = start // xb
    at = lambda which: pl.BlockSpec(block, lambda s, i, r: (i + first, r[which, s], 0, 0))
    fixed = lambda shape: pl.BlockSpec(shape, lambda s, i, r: (0,) * len(shape))
    if halo is None:
        after, after_spec = features, at(2)
    else:
        after, after_spec = halo, pl.BlockSpec((xb, cols, channels), lambda s, i, r: (i, 0, 0))
    piece_specs = [
        pl.BlockSpec((p.shape[0], 1, cols, channels), lambda s, i, r: (0, r[1, s], 0, 0))
        for p in pieces
    ]
    tokens = xb * cols
    sub = min(512, tokens)
    in_specs = [
        at(0),
        at(1),
        after_spec,
        pl.BlockSpec((tokens, waves_cols), lambda s, i, r: (i + first, 0)),
        pl.BlockSpec((1, 3, channels), lambda s, i, r: (s, 0, 0)),
        fixed((channels, hidden)),
        fixed((1, hidden)),
        fixed((hidden, channels)),
        fixed((1, channels)),
        *piece_specs,
    ]
    args = [rows, features, features, after, inv, taps, w_in, bias_in, w_out, bias_out, *pieces]
    aliases = {}
    if out is not None:
        aliases = {len(args): 0}
        in_specs.append(pl.BlockSpec(memory_space=pl.ANY))
        args.append(out)
    work = slots * count * cols
    return pl.pallas_call(
        functools.partial(row_kernel, len(pieces), sub),
        grid_spec=pltpu.PrefetchScalarGridSpec(
            num_scalar_prefetch=1,
            grid=(slots, count // xb),
            in_specs=in_specs,
            out_specs=at(1),
            scratch_shapes=[
                pltpu.VMEM((waves_cols, channels), BF16),
                pltpu.VMEM((tokens, channels), BF16),
                pltpu.VMEM((tokens, hidden), BF16),
            ],
        ),
        out_shape=jax.ShapeDtypeStruct(features.shape, BF16),
        input_output_aliases=aliases,
        compiler_params=pltpu.CompilerParams(vmem_limit_bytes=VMEM_BYTES),
        cost_estimate=pl.CostEstimate(
            flops=2 * work * channels * (2 * hidden + waves_cols),
            bytes_accessed=work * channels * 10,
            transcendentals=work * hidden,
        ),
        name="rows" if halo is None else "halo_rows",
    )(*args)


def chunks_of(x_rows):
    unit = x_rows // 8
    return [(0, 3 * unit), (3 * unit, 3 * unit), (6 * unit, 2 * unit)]


def local(features, spectral_weight, conv_taps, w_in, bias_in, w_out, bias_out):
    x_rows, y_rows, cols, channels = features.shape
    modes = spectral_weight.shape[0]
    gx_size = lax.axis_size("gx")
    gy_size = lax.axis_size("gy")
    gx = lax.axis_index("gx")
    gy = lax.axis_index("gy")

    edges = [jnp.where(gy % 2 == p, y_rows - 1, 0) for p in range(2)]
    live = [gy_size > p + 1 for p in range(2)]
    halos = [[], []]
    for p in range(2):
        if live[p]:
            swaps = [(a, b) for i in range(p, gy_size - 1, 2) for a, b in ((i, i + 1), (i + 1, i))]
            for start, count in chunks_of(x_rows):
                edge = lax.dynamic_slice(
                    features, (start, edges[p], 0, 0), (count, 1, cols, channels)
                ).reshape(count, cols, channels)
                halos[p].append(lax.ppermute(edge, "gy", swaps))

    levels = gx_size.bit_length() - 1
    halving = max(min(levels - 1, modes.bit_length() - 1), 0)
    own = jnp.int32(0)
    for level in range(halving):
        own = own + (gx >> level & 1) * (modes >> level + 1)
    waves = jnp.arange(modes, dtype=jnp.int32) ^ own
    positions = gx * x_rows + jnp.arange(x_rows, dtype=jnp.int32)
    table, inverse = wave_tables(waves, positions, x_rows * gx_size)
    xb = x_rows // 8
    table = table.reshape(2 * modes, 8, xb).transpose(1, 0, 2)
    swap = lambda a, level: lax.ppermute(
        a, "gx", [(i, i ^ (1 << level)) for i in range(gx_size)]
    )
    send, keep, inv = forward_transform(features, table, inverse.T, xb, modes)
    for level in range(halving):
        got = swap(send, level)
        if level + 1 < halving:
            send, keep = halve(keep, got)
        else:
            send, keep = add(keep, got)
    for level in range(halving, levels):
        got = swap(send, level)
        if level + 1 < levels:
            send, keep = add(keep, got)
    owned = modes >> halving
    which = (own // owned).reshape(1)
    pieces = [mix(keep, got, spectral_weight, which)]
    for level in reversed(range(halving)):
        pieces = pieces + [swap(p, level) for p in pieces]

    def neighbours(row, outer_live):
        first = row == 0
        last = row == y_rows - 1
        before = jnp.where(first, row if not outer_live else row + 1, row - 1)
        return before

    none = jnp.zeros_like(conv_taps[0])
    rows, taps = [], []
    for row in range(1, y_rows - 1):
        rows.append(jnp.stack([jnp.int32(v) for v in (row - 1, row, row + 1)]))
        taps.append(conv_taps)
    edge_args = []
    for p in range(2):
        top = edges[p] == 0
        inner = jnp.where(top, 1, y_rows - 2)
        inner_tap = jnp.where(top, conv_taps[2], conv_taps[0])
        outer_tap = jnp.where(top, conv_taps[0], conv_taps[2])
        index = jnp.stack([inner, edges[p], edges[p]]).astype(jnp.int32)
        if live[p]:
            edge_args.append((p, index, jnp.stack([inner_tap, conv_taps[1], outer_tap])))
        else:
            rows.append(index)
            taps.append(jnp.stack([inner_tap, conv_taps[1], none]))
    dense = (w_in, bias_in[None], w_out, bias_out[None], pieces)
    out = None
    if rows:
        out = rows_of(
            None, features, inv, jnp.stack(taps), jnp.stack(rows, 1), *dense, x_rows // 2, 0, x_rows
        )
    for at, (start, count) in enumerate(chunks_of(x_rows)):
        for p, index, tap in edge_args:
            out = rows_of(
                out, features, inv, tap[None], index[:, None], *dense, xb, start, count, halos[p][at]
            )
    return out


def solution(mesh):
    return jax.shard_map(
        local,
        mesh=mesh,
        in_specs=(P("gx", "gy", None, None), P(), P(), P(), P(), P(), P()),
        out_specs=P("gx", "gy", None, None),
        check_vma=False,
    )
```

time: 179 us -> 85.2 us (0.48)
  matrix products: 53.8 us -> 0 us
  Pallas kernels: 0 us -> 49.6 us
  local copies, waits for them, and re-layouts: 53.1 us -> 6.98 us
  blocking collectives: 20.8 us -> 0 us
  between operations: 13.5 us -> 0.19 us
  waiting for transfers between devices: 18.3 us -> 8.6 us
  other arithmetic: 11.9 us -> 2.61 us
  starting transfers between devices: 7.54 us -> 16.7 us
    dot_general x7 -> x0, matrix products: 53.8 us -> none  [the longest x1 31.3 us: local(): jnp.dot(hidden, w_out, preferred_element_type=jnp.float32)]
    pallas_call x0 -> x9, Pallas kernels: none -> 49.6 us  [the longest x4 38.8 us: rows_of(): pl.pallas_call(functools.partial(row_kernel, len(pieces), sub), grid_spec...]
    convert_element_type x2 -> x6, local copies, waits for them, and re-layouts: 29.1 us -> 0.33 us  [the longest x3 0.18 us: wave_tables(): (jnp.stack([amplitude * cosines, -amplitude * sines], 1) * scale).astype(...]
    all_gather x1 -> x0, blocking collectives: 20.8 us -> none  [local(): mixed = lax.all_gather(mixed_own, 'gx', axis=1, tiled=True)]
    unnamed x14 -> x16, local copies, waits for them, and re-layouts: 20.2 us -> 1.86 us
    reduce_scatter x1 -> x0, waiting for transfers between devices: 18.3 us -> none  [local(): lax.psum_scatter(spectrum, 'gx', scatter_dimension=1, tiled=True)]
    unnamed x1 -> x0, other arithmetic: 10.9 us -> none
    ppermute x2 -> x14, starting transfers between devices: 7.54 us -> 16.7 us  [the longest x11 11.6 us: local(): lax.ppermute(a, 'gx', [(i, i ^ 1 << level) for i in range(gx_size)])]
  transfers between devices with their start and end apart: 3 -> 14, of which waited for: 1 -> 4; matrix products, arithmetic and copies ran while one was open for 20% -> 8% of each run, Pallas kernels for 0% -> 42%
where the time goes in v1:
time: 85.2 us; the launch traced here: 84.6 us
  Pallas kernels  49.6 us (58%)
  starting transfers between devices  16.7 us (20%)
  waiting for transfers between devices  8.6 us (10%)
  local copies, waits for them, and re-layouts  6.98 us (8%)
  other arithmetic  2.61 us (3%)
    pallas_call x4, Pallas kernels, rows_of(): pl.pallas_call(functools.partial(row_kernel, len(pieces), sub), grid_spec...  38.8 us
    ppermute x11, starting transfers between devices, local(): lax.ppermute(a, 'gx', [(i, i ^ 1 << level) for i in range(gx_size)])  11.6 us
    pallas_call x1, Pallas kernels, forward_transform(): pl.pallas_call(functools.partial(forward_kernel, half), grid=(steps,), in...  9.39 us
    ppermute x11, waiting for transfers between devices, local(): lax.ppermute(a, 'gx', [(i, i ^ 1 << level) for i in range(gx_size)])  8.59 us
    ppermute x3, starting transfers between devices, local(): halos[p].append(lax.ppermute(edge, 'gy', swaps))  5.01 us
    reshape x2, local copies, waits for them, and re-layouts, local(): edge = lax.dynamic_slice(features, (start, edges[p], 0, 0), (count, 1, co...  3.95 us
    unnamed x16, local copies, waits for them, and re-layouts  1.86 us
  transfers between devices with their start and end apart: 14, of which 4 were waited for; matrix products, arithmetic and copies ran while one was open for 8% of the time, Pallas kernels for 42%

profile of v1, /device:TPU:0, one launch (start us, length us, event | category | flops | bytes accessed | tf_op | source)
XLA Modules:
  0.0 84.6 jit_solution(4633417233551221629)
XLA Ops:
  0.0 0.2 broadcast_multiply_fusion.1
  0.3 0.1 copy.24
  0.5 0.1 convert_element_type.38
  0.7 9.4 %forward.1 = (bf16[16,4,8,256]{3,2,1,0:T(8,128)(2,1)}, f32[16,4,8,256]{3,2,1,0:T(8,128)S(1)}, bf16[4096,256]{1,0:T(8,128)(2,1)S(1)}) custom-call(bf16[8,32,64]{2,1,0:T(8,128)(2,1)S(1)} %bitcast.28, bf16[512,32]{1,0:T(8,128)(2,1)S(1)} %bitcast.27, bf16[512,4,8,256]{3,2,1,0:T(8,128)(2,1)} %here_ref.7), custom_call_target="tpu_custom_call" | custom-call | flops 2147483648 | bytes 8388608 | tf_op jit(solution)/shard_map/forward/pallas_call | solution.py:81
  10.1 0.8 copy-done.3
  10.9 0.5 collective-permute-start.1
  11.3 2.9 %dynamic-slice_bitcast_fusion = (bf16[192,8,256]{2,1,0:T(8,128)(2,1)}, bf16[192,8,256]{2,1,0:T(8,128)(2,1)}) fusion(bf16[512,4,8,256]{3,2,1,0:T(8,128)(2,1)} %here_ref.7, s32[]{:T(128)} %select_n.88), kind=kLoop, calls=%fused_computation | loop fusion | bytes 3145732 | tf_op jit(solution)/shard_map/reshape | solution.py:331
  14.2 3.0 %collective-permute-start.13 = (bf16[192,8,256]{2,1,0:T(8,128)(2,1)}, bf16[192,8,256]{2,1,0:T(8,128)(2,1)}, u32[]{:S(2)}, u32[]{:S(2)}) collective-permute-start(bf16[192,8,256]{2,1,0:T(8,128)(2,1)} %get-tuple-element.23), channel_id=1, source_target_pairs={{0,1},{1,0},{2,3},{3,2},{4,5},{5,4},{6,7},{7,6},{8,9},{9,8},{10,11... | collective-permute-start | bytes 2359304 | tf_op jit(solution)/shard_map/ppermute | solution.py:332
  17.3 1.0 %copy-done.4 = f32[16,4,8,256]{3,2,1,0:T(8,128)S(1)} copy-done((f32[16,4,8,256]{3,2,1,0:T(8,128)S(1)}, f32[16,4,8,256]{3,2,1,0:T(8,128)}, u32[]{:S(2)}) %copy-start.4) | copy-done | bytes 524312
  18.4 1.6 %collective-permute-start.2 = (bf16[8,4,8,256]{3,2,1,0:T(8,128)(2,1)S(1)}, bf16[8,4,8,256]{3,2,1,0:T(8,128)(2,1)S(1)}, u32[]{:S(2)}, u32[]{:S(2)}) collective-permute-start(bf16[8,4,8,256]{3,2,1,0:T(8,128)(2,1)S(1)} %get-tuple-element.18), channel_id=1, source_target_pairs={{0,4},{2,6},{4,0},{6,2},{8,12},{10,14},{12,8},{14,10},{16,20},{18,... | collective-permute-start | bytes 393224 | tf_op jit(solution)/shard_map/ppermute | solution.py:344
  20.0 0.7 fusion.11
  20.6 2.8 %collective-permute-done.2.got_ref = bf16[8,4,8,256]{3,2,1,0:T(8,128)(2,1)S(1)} collective-permute-done((bf16[8,4,8,256]{3,2,1,0:T(8,128)(2,1)S(1)}, bf16[8,4,8,256]{3,2,1,0:T(8,128)(2,1)S(1)}, u32[]{:S(2)}, u32[]{:S(2)}) %collective-permute-start.2) | collective-permute-done | bytes 131104 | tf_op jit(solution)/shard_map/ppermute | solution.py:344
  23.5 1.6 %collective-permute-start.3 = (bf16[4,4,8,256]{3,2,1,0:T(8,128)(2,1)S(1)}, bf16[4,4,8,256]{3,2,1,0:T(8,128)(2,1)S(1)}, u32[]{:S(2)}, u32[]{:S(2)}) collective-permute-start(bf16[4,4,8,256]{3,2,1,0:T(8,128)(2,1)S(1)} %get-tuple-element.20), channel_id=1, source_target_pairs={{0,8},{2,10},{4,12},{6,14},{8,0},{10,2},{12,4},{14,6},{16,24},{18,... | collective-permute-start | bytes 196616 | tf_op jit(solution)/shard_map/ppermute | solution.py:344
  25.2 0.7 copy.25
  25.8 1.9 %collective-permute-done.3.got_ref = bf16[4,4,8,256]{3,2,1,0:T(8,128)(2,1)S(1)} collective-permute-done((bf16[4,4,8,256]{3,2,1,0:T(8,128)(2,1)S(1)}, bf16[4,4,8,256]{3,2,1,0:T(8,128)(2,1)S(1)}, u32[]{:S(2)}, u32[]{:S(2)}) %collective-permute-start.3) | collective-permute-done | bytes 65568 | tf_op jit(solution)/shard_map/ppermute | solution.py:344
  27.8 2.7 %collective-permute-start.4 = (bf16[4,4,8,256]{3,2,1,0:T(8,128)(2,1)S(1)}, bf16[4,4,8,256]{3,2,1,0:T(8,128)(2,1)S(1)}, u32[]{:S(2)}, u32[]{:S(2)}) collective-permute-start(bf16[4,4,8,256]{3,2,1,0:T(8,128)(2,1)S(1)} %get-tuple-element.22), channel_id=1, source_target_pairs={{0,16},{2,18},{4,20},{6,22},{8,24},{10,26},{12,28},{14,30},{16,0},... | collective-permute-start | bytes 196616 | tf_op jit(solution)/shard_map/ppermute | solution.py:344
  30.6 2.4 %collective-permute-done.4.got_ref = bf16[4,4,8,256]{3,2,1,0:T(8,128)(2,1)S(1)} collective-permute-done((bf16[4,4,8,256]{3,2,1,0:T(8,128)(2,1)S(1)}, bf16[4,4,8,256]{3,2,1,0:T(8,128)(2,1)S(1)}, u32[]{:S(2)}, u32[]{:S(2)}) %collective-permute-start.4) | collective-permute-done | bytes 65568 | tf_op jit(solution)/shard_map/ppermute | solution.py:344
  33.0 1.3 %mix.1.rest_0_ = bf16[4,4,8,256]{3,2,1,0:T(8,128)(2,1)S(1)} custom-call(s32[1]{0:T(128)} %bitcast.9.which_ref, f32[4,4,8,256]{3,2,1,0:T(8,128)S(1)} %get-tuple-element.21.keep_ref, bf16[4,4,8,256]{3,2,1,0:T(8,128)(2,1)S(1)} %collective-permute-done.4.got_ref, bf16[16,2,256,256]{3,2,1,0:T(8,128)(2,1)} %weight_ref.1), custom_call_target="tpu_custom_call" | custom-call | tf_op jit(solution)/shard_map/mix/pallas_call | solution.py:168
  34.3 1.6 %collective-permute-start.5 = (bf16[4,4,8,256]{3,2,1,0:T(8,128)(2,1)S(1)}, bf16[4,4,8,256]{3,2,1,0:T(8,128)(2,1)S(1)}, u32[]{:S(2)}, u32[]{:S(2)}) collective-permute-start(bf16[4,4,8,256]{3,2,1,0:T(8,128)(2,1)S(1)} %mix.1.rest_0_), channel_id=1, source_target_pairs={{0,8},{2,10},{4,12},{6,14},{8,0},{10,2},{12,4},{14,6},{16,24},{18,... | collective-permute-start | bytes 196616 | tf_op jit(solution)/shard_map/ppermute | solution.py:344
  36.0 1.1 %dynamic-slice_bitcast_fusion.2 = bf16[128,8,256]{2,1,0:T(8,128)(2,1)S(1)} fusion(bf16[512,4,8,256]{3,2,1,0:T(8,128)(2,1)} %here_ref.7, s32[]{:T(128)} %select_n.88), kind=kLoop, calls=%fused_computation.2 | loop fusion | bytes 1048580 | tf_op jit(solution)/shard_map/reshape | solution.py:331
  37.1 1.6 %collective-permute-start.6 = (bf16[4,4,8,256]{3,2,1,0:T(8,128)(2,1)S(1)}, bf16[4,4,8,256]{3,2,1,0:T(8,128)(2,1)S(1)}, u32[]{:S(2)}, u32[]{:S(2)}) collective-permute-start(bf16[4,4,8,256]{3,2,1,0:T(8,128)(2,1)S(1)} %mix.1.rest_0_), channel_id=1, source_target_pairs={{0,4},{2,6},{4,0},{6,2},{8,12},{10,14},{12,8},{14,10},{16,20},{18,... | collective-permute-start | bytes 196616 | tf_op jit(solution)/shard_map/ppermute | solution.py:344
  38.7 1.5 %collective-permute-start.7 = (bf16[4,4,8,256]{3,2,1,0:T(8,128)(2,1)S(1)}, bf16[4,4,8,256]{3,2,1,0:T(8,128)(2,1)S(1)}, u32[]{:S(2)}, u32[]{:S(2)}) collective-permute-start(bf16[4,4,8,256]{3,2,1,0:T(8,128)(2,1)S(1)} %collective-permute-done.5.rest_1_), channel_id=1, source_target_pairs={{0,4},{2,6},{4,0},{6,2},{8,12},{10,14},{12,8},{14,10},{16,20},{18,... | collective-permute-start | bytes 196616 | tf_op jit(solution)/shard_map/ppermute | solution.py:344
  40.2 0.8 pad_maximum_fusion.taps_ref
  41.0 0.5 collective-permute-start.9
  41.5 1.4 %collective-permute-done.7.rest_3_ = bf16[4,4,8,256]{3,2,1,0:T(8,128)(2,1)S(1)} collective-permute-done((bf16[4,4,8,256]{3,2,1,0:T(8,128)(2,1)S(1)}, bf16[4,4,8,256]{3,2,1,0:T(8,128)(2,1)S(1)}, u32[]{:S(2)}, u32[]{:S(2)}) %collective-permute-start.7) | collective-permute-done | bytes 65568 | tf_op jit(solution)/shard_map/ppermute | solution.py:344
  42.9 0.8 pad_add_fusion.rows_ref
  43.7 0.5 collective-permute-start.12
  44.2 1.5 %collective-permute-start = (bf16[128,8,256]{2,1,0:T(8,128)(2,1)S(1)}, bf16[128,8,256]{2,1,0:T(8,128)(2,1)S(1)}, u32[]{:S(2)}, u32[]{:S(2)}) collective-permute-start(bf16[128,8,256]{2,1,0:T(8,128)(2,1)S(1)} %dynamic-slice_bitcast_fusion.2), channel_id=1, source_target_pairs={{0,1},{1,0},{2,3},{3,2},{4,5},{5,4},{6,7},{7,6},{8,9},{9,8},{10,11... | collective-permute-start | bytes 1572872 | tf_op jit(solution)/shard_map/ppermute | solution.py:332
  45.8 22.8 %rows.1.rest_8_ = bf16[512,4,8,256]{3,2,1,0:T(8,128)(2,1)} custom-call(s32[3,3]{1,0:T(4,128)S(1)} %pad_add_fusion.rows_ref, bf16[512,4,8,256]{3,2,1,0:T(8,128)(2,1)} %here_ref.7, bf16[512,4,8,256]{3,2,1,0:T(8,128)(2,1)} %here_ref.7, bf16[512,4,8,256]{3,2,1,0:T(8,128)(2,1)} %here_ref.7, bf16[4096,256]{1,0:T(8,128)(2,1)S(1)} %get-tuple-element.14.inv_ref, ...), custom_call_target="tpu_custom_call" | custom-call | flops 14495514624 | bytes 31457280 | tf_op jit(solution)/shard_map/rows/pallas_call | solution.py:284
  68.6 5.8 %halo_rows.3.rest_8_ = bf16[512,4,8,256]{3,2,1,0:T(8,128)(2,1)} custom-call(s32[3,1]{1,0:T(4,128)S(1)} %copy.28.rows_ref, bf16[512,4,8,256]{3,2,1,0:T(8,128)(2,1)} %here_ref.7, bf16[512,4,8,256]{3,2,1,0:T(8,128)(2,1)} %here_ref.7, bf16[192,8,256]{2,1,0:T(8,128)(2,1)} %collective-permute-done.13.after_ref, ...), custom_call_target="tpu_custom_call", output_to_operand_aliasing={{}: (18, {})} | custom-call | flops 1811939328 | bytes 3932160 | tf_op jit(solution)/shard_map/halo_rows/pallas_call | solution.py:284
  74.4 5.6 %halo_rows.4.rest_8_ = bf16[512,4,8,256]{3,2,1,0:T(8,128)(2,1)} custom-call(s32[3,1]{1,0:T(4,128)S(1)} %copy.28.rows_ref, bf16[512,4,8,256]{3,2,1,0:T(8,128)(2,1)} %here_ref.7, bf16[512,4,8,256]{3,2,1,0:T(8,128)(2,1)} %here_ref.7, bf16[192,8,256]{2,1,0:T(8,128)(2,1)S(1)} %collective-permute-done.12.after_ref, ...), custom_call_target="tpu_custom_call", output_to_operand_aliasing={{}: (18, {})} | custom-call | flops 1811939328 | bytes 3932160 | tf_op jit(solution)/shard_map/halo_rows/pallas_call | solution.py:284
  80.1 4.5 %halo_rows.5 = bf16[512,4,8,256]{3,2,1,0:T(8,128)(2,1)} custom-call(s32[3,1]{1,0:T(4,128)S(1)} %copy.28.rows_ref, bf16[512,4,8,256]{3,2,1,0:T(8,128)(2,1)} %here_ref.7, bf16[512,4,8,256]{3,2,1,0:T(8,128)(2,1)} %here_ref.7, bf16[128,8,256]{2,1,0:T(8,128)(2,1)S(1)} %collective-permute-done.after_ref, ...), custom_call_target="tpu_custom_call", output_to_operand_aliasing={{}: (18, {})} | custom-call | flops 1207959552 | bytes 2621440 | tf_op jit(solution)/shard_map/halo_rows/pallas_call | solution.py:284
  (44 shorter events, 0.7 us)
Async XLA Ops:
  0.0 17.3 %copy-start.7 = (f32[3,256]{1,0:T(4,128)S(1)}, f32[3,256]{1,0:T(4,128)}, u32[]{:S(2)}) copy-start(f32[3,256]{1,0:T(4,128)} %param.9) | copy-start | bytes 9220
  0.7 45.1 %copy-start.1 = (bf16[256,1024]{1,0:T(8,128)(2,1)S(1)}, bf16[256,1024]{1,0:T(8,128)(2,1)}, u32[]{:S(2)}) copy-start(bf16[256,1024]{1,0:T(8,128)(2,1)} %w_in_ref.7) | copy-start | bytes 1572868
  0.7 45.1 %copy-start.2 = (bf16[1024,256]{1,0:T(8,128)(2,1)S(1)}, bf16[1024,256]{1,0:T(8,128)(2,1)}, u32[]{:S(2)}) copy-start(bf16[1024,256]{1,0:T(8,128)(2,1)} %w_out_ref.7) | copy-start | bytes 1572868
  0.7 45.1 %copy-start.5 = (f32[1024]{0:T(1024)S(1)}, f32[1024]{0:T(1024)}, u32[]{:S(2)}) copy-start(f32[1024]{0:T(1024)} %param.11) | copy-start | bytes 12292
  0.7 45.1 %copy-start.6 = (f32[256]{0:T(256)S(1)}, f32[256]{0:T(256)}, u32[]{:S(2)}) copy-start(f32[256]{0:T(256)} %param.13) | copy-start | bytes 3076
  10.1 0.8 copy-start.3
  10.9 57.7 %copy-start = (bf16[4096,256]{1,0:T(8,128)(2,1)}, bf16[4096,256]{1,0:T(8,128)(2,1)S(1)}, u32[]{:S(2)}) copy-start(bf16[4096,256]{1,0:T(8,128)(2,1)S(1)} %get-tuple-element.14.inv_ref) | copy-start | bytes 6291460
  10.9 6.4 %collective-permute-start.1 = (bf16[16,4,8,256]{3,2,1,0:T(8,128)(2,1)}, bf16[16,4,8,256]{3,2,1,0:T(8,128)(2,1)S(1)}, u32[]{:S(2)}, u32[]{:S(2)}) collective-permute-start(bf16[16,4,8,256]{3,2,1,0:T(8,128)(2,1)} %get-tuple-element.16), channel_id=1, source_target_pairs={{0,2},{2,0},{4,6},{6,4},{8,10},{10,8},{12,14},{14,12},{16,18},{18,... | collective-permute-start | bytes 786440 | tf_op jit(solution)/shard_map/ppermute | solution.py:344
  14.2 54.4 %collective-permute-start.13 = (bf16[192,8,256]{2,1,0:T(8,128)(2,1)}, bf16[192,8,256]{2,1,0:T(8,128)(2,1)}, u32[]{:S(2)}, u32[]{:S(2)}) collective-permute-start(bf16[192,8,256]{2,1,0:T(8,128)(2,1)} %get-tuple-element.23), channel_id=1, source_target_pairs={{0,1},{1,0},{2,3},{3,2},{4,5},{5,4},{6,7},{7,6},{8,9},{9,8},{10,11... | collective-permute-start | bytes 2359304 | tf_op jit(solution)/shard_map/ppermute | solution.py:332
  17.3 1.0 %copy-start.4 = (f32[16,4,8,256]{3,2,1,0:T(8,128)S(1)}, f32[16,4,8,256]{3,2,1,0:T(8,128)}, u32[]{:S(2)}) copy-start(f32[16,4,8,256]{3,2,1,0:T(8,128)} %copy-done.3) | copy-start | bytes 1572868
  18.4 5.0 %collective-permute-start.2 = (bf16[8,4,8,256]{3,2,1,0:T(8,128)(2,1)S(1)}, bf16[8,4,8,256]{3,2,1,0:T(8,128)(2,1)S(1)}, u32[]{:S(2)}, u32[]{:S(2)}) collective-permute-start(bf16[8,4,8,256]{3,2,1,0:T(8,128)(2,1)S(1)} %get-tuple-element.18), channel_id=1, source_target_pairs={{0,4},{2,6},{4,0},{6,2},{8,12},{10,14},{12,8},{14,10},{16,20},{18,... | collective-permute-start | bytes 393224 | tf_op jit(solution)/shard_map/ppermute | solution.py:344
  23.5 4.3 %collective-permute-start.3 = (bf16[4,4,8,256]{3,2,1,0:T(8,128)(2,1)S(1)}, bf16[4,4,8,256]{3,2,1,0:T(8,128)(2,1)S(1)}, u32[]{:S(2)}, u32[]{:S(2)}) collective-permute-start(bf16[4,4,8,256]{3,2,1,0:T(8,128)(2,1)S(1)} %get-tuple-element.20), channel_id=1, source_target_pairs={{0,8},{2,10},{4,12},{6,14},{8,0},{10,2},{12,4},{14,6},{16,24},{18,... | collective-permute-start | bytes 196616 | tf_op jit(solution)/shard_map/ppermute | solution.py:344
  27.8 5.2 %collective-permute-start.4 = (bf16[4,4,8,256]{3,2,1,0:T(8,128)(2,1)S(1)}, bf16[4,4,8,256]{3,2,1,0:T(8,128)(2,1)S(1)}, u32[]{:S(2)}, u32[]{:S(2)}) collective-permute-start(bf16[4,4,8,256]{3,2,1,0:T(8,128)(2,1)S(1)} %get-tuple-element.22), channel_id=1, source_target_pairs={{0,16},{2,18},{4,20},{6,22},{8,24},{10,26},{12,28},{14,30},{16,0},... | collective-permute-start | bytes 196616 | tf_op jit(solution)/shard_map/ppermute | solution.py:344
  34.3 4.3 %collective-permute-start.5 = (bf16[4,4,8,256]{3,2,1,0:T(8,128)(2,1)S(1)}, bf16[4,4,8,256]{3,2,1,0:T(8,128)(2,1)S(1)}, u32[]{:S(2)}, u32[]{:S(2)}) collective-permute-start(bf16[4,4,8,256]{3,2,1,0:T(8,128)(2,1)S(1)} %mix.1.rest_0_), channel_id=1, source_target_pairs={{0,8},{2,10},{4,12},{6,14},{8,0},{10,2},{12,4},{14,6},{16,24},{18,... | collective-permute-start | bytes 196616 | tf_op jit(solution)/shard_map/ppermute | solution.py:344
  37.1 4.4 %collective-permute-start.6 = (bf16[4,4,8,256]{3,2,1,0:T(8,128)(2,1)S(1)}, bf16[4,4,8,256]{3,2,1,0:T(8,128)(2,1)S(1)}, u32[]{:S(2)}, u32[]{:S(2)}) collective-permute-start(bf16[4,4,8,256]{3,2,1,0:T(8,128)(2,1)S(1)} %mix.1.rest_0_), channel_id=1, source_target_pairs={{0,4},{2,6},{4,0},{6,2},{8,12},{10,14},{12,8},{14,10},{16,20},{18,... | collective-permute-start | bytes 196616 | tf_op jit(solution)/shard_map/ppermute | solution.py:344
  38.7 4.3 %collective-permute-start.7 = (bf16[4,4,8,256]{3,2,1,0:T(8,128)(2,1)S(1)}, bf16[4,4,8,256]{3,2,1,0:T(8,128)(2,1)S(1)}, u32[]{:S(2)}, u32[]{:S(2)}) collective-permute-start(bf16[4,4,8,256]{3,2,1,0:T(8,128)(2,1)S(1)} %collective-permute-done.5.rest_1_), channel_id=1, source_target_pairs={{0,4},{2,6},{4,0},{6,2},{8,12},{10,14},{12,8},{14,10},{16,20},{18,... | collective-permute-start | bytes 196616 | tf_op jit(solution)/shard_map/ppermute | solution.py:344
  41.0 2.8 %collective-permute-start.8 = (bf16[4,4,8,256]{3,2,1,0:T(8,128)(2,1)S(1)}, bf16[4,4,8,256]{3,2,1,0:T(8,128)(2,1)S(1)}, u32[]{:S(2)}, u32[]{:S(2)}) collective-permute-start(bf16[4,4,8,256]{3,2,1,0:T(8,128)(2,1)S(1)} %mix.1.rest_0_), channel_id=1, source_target_pairs={{0,2},{2,0},{4,6},{6,4},{8,10},{10,8},{12,14},{14,12},{16,18},{18,... | collective-permute-start | bytes 196616 | tf_op jit(solution)/shard_map/ppermute | solution.py:344
  41.0 4.8 %collective-permute-start.9 = (bf16[4,4,8,256]{3,2,1,0:T(8,128)(2,1)S(1)}, bf16[4,4,8,256]{3,2,1,0:T(8,128)(2,1)S(1)}, u32[]{:S(2)}, u32[]{:S(2)}) collective-permute-start(bf16[4,4,8,256]{3,2,1,0:T(8,128)(2,1)S(1)} %collective-permute-done.5.rest_1_), channel_id=1, source_target_pairs={{0,2},{2,0},{4,6},{6,4},{8,10},{10,8},{12,14},{14,12},{16,18},{18,... | collective-permute-start | bytes 196616 | tf_op jit(solution)/shard_map/ppermute | solution.py:344
  41.5 2.8 %collective-permute-start.10 = (bf16[4,4,8,256]{3,2,1,0:T(8,128)(2,1)S(1)}, bf16[4,4,8,256]{3,2,1,0:T(8,128)(2,1)S(1)}, u32[]{:S(2)}, u32[]{:S(2)}) collective-permute-start(bf16[4,4,8,256]{3,2,1,0:T(8,128)(2,1)S(1)} %collective-permute-done.6.rest_2_), channel_id=1, source_target_pairs={{0,2},{2,0},{4,6},{6,4},{8,10},{10,8},{12,14},{14,12},{16,18},{18,... | collective-permute-start | bytes 196616 | tf_op jit(solution)/shard_map/ppermute | solution.py:344
  42.9 2.8 %collective-permute-start.11 = (bf16[4,4,8,256]{3,2,1,0:T(8,128)(2,1)S(1)}, bf16[4,4,8,256]{3,2,1,0:T(8,128)(2,1)S(1)}, u32[]{:S(2)}, u32[]{:S(2)}) collective-permute-start(bf16[4,4,8,256]{3,2,1,0:T(8,128)(2,1)S(1)} %collective-permute-done.7.rest_3_), channel_id=1, source_target_pairs={{0,2},{2,0},{4,6},{6,4},{8,10},{10,8},{12,14},{14,12},{16,18},{18,... | collective-permute-start | bytes 196616 | tf_op jit(solution)/shard_map/ppermute | solution.py:344
  43.7 30.7 %collective-permute-start.12 = (bf16[192,8,256]{2,1,0:T(8,128)(2,1)}, bf16[192,8,256]{2,1,0:T(8,128)(2,1)S(1)}, u32[]{:S(2)}, u32[]{:S(2)}) collective-permute-start(bf16[192,8,256]{2,1,0:T(8,128)(2,1)} %get-tuple-element.24), channel_id=1, source_target_pairs={{0,1},{1,0},{2,3},{3,2},{4,5},{5,4},{6,7},{7,6},{8,9},{9,8},{10,11... | collective-permute-start | bytes 2359304 | tf_op jit(solution)/shard_map/ppermute | solution.py:332
  44.2 35.8 %collective-permute-start = (bf16[128,8,256]{2,1,0:T(8,128)(2,1)S(1)}, bf16[128,8,256]{2,1,0:T(8,128)(2,1)S(1)}, u32[]{:S(2)}, u32[]{:S(2)}) collective-permute-start(bf16[128,8,256]{2,1,0:T(8,128)(2,1)S(1)} %dynamic-slice_bitcast_fusion.2), channel_id=1, source_target_pairs={{0,1},{1,0},{2,3},{3,2},{4,5},{5,4},{6,7},{7,6},{8,9},{9,8},{10,11... | collective-permute-start | bytes 1572872 | tf_op jit(solution)/shard_map/ppermute | solution.py:332

commit v2 on v0

v2 whole, which is shorter than its diff:
```python
import functools
import math

import jax
import jax.numpy as jnp
from jax import lax
from jax.experimental import pallas as pl
from jax.experimental.pallas import tpu as pltpu
from jax.sharding import PartitionSpec as P

F32 = jnp.float32
BF16 = jnp.bfloat16
GELU_A = math.sqrt(2.0 / math.pi)
GELU_B = GELU_A * 0.044715
SMALL_BYTES = 16 * 2**20
ROWS_BYTES = 36 * 2**20


def wave_tables(own, start, modes, x_rows, total):
    shape = (2 * modes, x_rows)
    row = lax.broadcasted_iota(jnp.int32, shape, 0)
    waves = row // 2 ^ own
    product = waves * (start + lax.broadcasted_iota(jnp.int32, shape, 1)) % total
    angles = 2.0 * math.pi / total * product.astype(F32)
    scale = 1.0 / math.sqrt(total)
    parts = jnp.where(row % 2 == 0, jnp.cos(angles), -jnp.sin(angles))
    amplitude = jnp.where(waves == 0, 1.0, 2.0).astype(F32)
    return (parts * scale).astype(BF16), (amplitude * parts * scale).astype(BF16)


def spread(table, cols):
    waves, xb = table.shape
    columns = waves * cols
    place = (
        lax.broadcasted_iota(jnp.int32, (waves, columns), 1) // cols
        == lax.broadcasted_iota(jnp.int32, (waves, columns), 0)
    )
    tall = lax.dot_general(
        table, place.astype(F32).astype(BF16), (((0,), (0,)), ((), ())), preferred_element_type=F32
    )
    same = lax.broadcasted_iota(jnp.int32, (1, cols, columns), 2) % cols == lax.broadcasted_iota(
        jnp.int32, (1, cols, columns), 1
    )
    return jnp.where(same, tall[:, None, :], 0.0).reshape(xb * cols, columns).astype(BF16)


def spread_wide(table, cols):
    waves, xb = table.shape
    width = xb * cols
    place = (
        lax.broadcasted_iota(jnp.int32, (xb, width), 1) // cols
        == lax.broadcasted_iota(jnp.int32, (xb, width), 0)
    )
    wide = jnp.dot(table, place.astype(F32).astype(BF16), preferred_element_type=F32)
    same = lax.broadcasted_iota(jnp.int32, (1, cols, width), 2) % cols == lax.broadcasted_iota(
        jnp.int32, (1, cols, width), 1
    )
    return jnp.where(same, wide[:, None, :], 0.0).reshape(waves * cols, width).astype(BF16)


def cut_kernel(p, start, rows_ref, variant_ref, field_ref, ahead_ref, cut_ref):
    row = rows_ref[variant_ref[0], p]
    cut_ref[...] = field_ref[start : start + cut_ref.shape[0], row]


def cut_edge(field, rows, variant, p, part, parts, ahead):
    x_rows, _, cols, channels = field.shape
    count = x_rows // parts
    return pl.pallas_call(
        functools.partial(cut_kernel, p, part * count),
        in_specs=[
            pl.BlockSpec(memory_space=pltpu.SMEM),
            pl.BlockSpec(memory_space=pltpu.SMEM),
            pl.BlockSpec(memory_space=pltpu.VMEM),
            pl.BlockSpec(memory_space=pl.ANY),
        ],
        out_specs=pl.BlockSpec(memory_space=pltpu.VMEM),
        out_shape=jax.ShapeDtypeStruct((count, cols, channels), BF16),
        compiler_params=pltpu.CompilerParams(vmem_limit_bytes=SMALL_BYTES),
        name="cut",
    )(rows, variant, field, ahead)


def widen_kernel(table_ref, wide_ref):
    x_rows = table_ref.shape[1]
    cols = wide_ref.shape[1] // x_rows
    xb = min(x_rows, 128)
    width = xb * cols
    for part in range(x_rows // xb):
        wide_ref[:, part * width : (part + 1) * width] = spread_wide(
            table_ref[:, part * xb : (part + 1) * xb], cols
        )


def widen(table, cols):
    waves, x_rows = table.shape
    return pl.pallas_call(
        widen_kernel,
        out_shape=jax.ShapeDtypeStruct((waves * cols, x_rows * cols), BF16),
        compiler_params=pltpu.CompilerParams(vmem_limit_bytes=SMALL_BYTES),
        cost_estimate=pl.CostEstimate(
            flops=10**9, bytes_accessed=4 * waves * cols * x_rows * cols, transcendentals=0
        ),
        name="widen",
    )(table)


def forward_kernel(rows_ref, variant_ref, wide_ref, field_ref, send_ref, keep_ref):
    x_rows, y_rows, cols, channels = field_ref.shape
    sent = send_ref.shape[1]
    waves = send_ref.shape[0]
    for place in range(y_rows):
        row = rows_ref[variant_ref[0], place]
        part = jnp.dot(
            wide_ref[...],
            field_ref[:, row].reshape(x_rows * cols, channels),
            preferred_element_type=F32,
        ).reshape(waves, cols, channels)
        if place < sent:
            send_ref[:, place] = part.astype(BF16)
        else:
            keep_ref[:, place - sent] = part


def forward_transform(features, wide, rows, variant):
    x_rows, y_rows, cols, channels = features.shape
    shape = (wide.shape[0] // cols, y_rows // 2, cols, channels)
    vmem = pl.BlockSpec(memory_space=pltpu.VMEM)
    smem = pl.BlockSpec(memory_space=pltpu.SMEM)
    return pl.pallas_call(
        forward_kernel,
        in_specs=[smem, smem, vmem, vmem],
        out_specs=[vmem, vmem],
        out_shape=[jax.ShapeDtypeStruct(shape, BF16), jax.ShapeDtypeStruct(shape, F32)],
        compiler_params=pltpu.CompilerParams(vmem_limit_bytes=SMALL_BYTES),
        name="forward",
    )(rows, variant, wide, features)


def prepare_kernel(which_ref, table_ref, weight_ref, inv_ref, own_ref, sem):
    owned = own_ref.shape[0]
    move = pltpu.make_async_copy(weight_ref.at[pl.ds(which_ref[0], owned)], own_ref, sem)
    move.start()
    waves, x_rows = table_ref.shape
    cols = inv_ref.shape[0] // x_rows
    xb = min(x_rows, 128)
    for part in range(x_rows // xb):
        inv_ref[part * xb * cols : (part + 1) * xb * cols] = spread(
            table_ref[:, part * xb : (part + 1) * xb], cols
        )
    move.wait()


def prepare(table, cols, weight, which, owned):
    waves, x_rows = table.shape
    vmem = pl.BlockSpec(memory_space=pltpu.VMEM)
    return pl.pallas_call(
        prepare_kernel,
        in_specs=[
            pl.BlockSpec(memory_space=pltpu.SMEM),
            vmem,
            pl.BlockSpec(memory_space=pltpu.HBM),
        ],
        out_specs=[vmem, vmem],
        out_shape=[
            jax.ShapeDtypeStruct((x_rows * cols, waves * cols), BF16),
            jax.ShapeDtypeStruct((owned,) + weight.shape[1:], BF16),
        ],
        scratch_shapes=[pltpu.SemaphoreType.DMA],
        compiler_params=pltpu.CompilerParams(vmem_limit_bytes=SMALL_BYTES),
        name="prepare",
    )(which, table, weight)


def halve_kernel(half, keep_ref, got_ref, *refs):
    send_ref, next_ref = refs[-2:]
    next_ref[...] = keep_ref[:half] + got_ref[:half].astype(F32)
    send_ref[...] = (keep_ref[half:] + got_ref[half:].astype(F32)).astype(BF16)


def add_kernel(keep_ref, got_ref, *refs):
    send_ref, next_ref = refs[-2:]
    total = keep_ref[...] + got_ref[...].astype(F32)
    next_ref[...] = total
    send_ref[...] = total.astype(BF16)


def combine(keep, got, halve, ahead):
    half = keep.shape[0] // 2 if halve else keep.shape[0]
    shape = (half,) + keep.shape[1:]
    vmem = pl.BlockSpec(memory_space=pltpu.VMEM)
    return pl.pallas_call(
        functools.partial(halve_kernel, half) if halve else add_kernel,
        in_specs=[vmem, vmem] + [pl.BlockSpec(memory_space=pl.ANY)] * len(ahead),
        out_specs=[vmem, vmem],
        out_shape=[jax.ShapeDtypeStruct(shape, BF16), jax.ShapeDtypeStruct(shape, F32)],
        compiler_params=pltpu.CompilerParams(vmem_limit_bytes=SMALL_BYTES),
        name="halve" if halve else "add",
    )(keep, got, *ahead)


def join_kernel(mine_ref, got_ref, out_ref):
    half = mine_ref.shape[0]
    out_ref[:half] = mine_ref[...]
    out_ref[half:] = got_ref[...]


def join(mine, got):
    return pl.pallas_call(
        join_kernel,
        out_shape=jax.ShapeDtypeStruct((2 * mine.shape[0],) + mine.shape[1:], BF16),
        compiler_params=pltpu.CompilerParams(vmem_limit_bytes=SMALL_BYTES),
        name="join",
    )(mine, got)


def stack_kernel(*refs):
    out_ref = refs[-1]
    rows, _, channels = out_ref.shape
    at = 0
    for ref in refs[:-1]:
        count = ref.shape[0] * ref.shape[2]
        for row in range(rows):
            out_ref[row, at : at + count] = ref[:, row].reshape(count, channels)
        at += count


def stack_modes(pieces):
    waves = sum(p.shape[0] for p in pieces)
    _, rows, cols, channels = pieces[0].shape
    return pl.pallas_call(
        stack_kernel,
        out_shape=jax.ShapeDtypeStruct((rows, waves * cols, channels), BF16),
        compiler_params=pltpu.CompilerParams(vmem_limit_bytes=SMALL_BYTES),
        name="stack",
    )(*pieces)


def mix_kernel(keep_ref, got_ref, weight_ref, out_ref):
    modes = weight_ref.shape[0]
    _, rows, cols, channels = keep_ref.shape
    count = rows * cols
    dot = functools.partial(jnp.dot, preferred_element_type=F32)
    for mode in range(modes):
        both = slice(2 * mode, 2 * mode + 2)
        parts = keep_ref[both] + got_ref[both].astype(F32)
        parts = parts.reshape(2 * count, channels).astype(BF16)
        by_real = dot(parts, weight_ref[mode, 0])
        by_imag = dot(parts, weight_ref[mode, 1])
        mixed_real = by_real[:count] - by_imag[count:]
        mixed_imag = by_imag[:count] + by_real[count:]
        out_ref[2 * mode] = mixed_real.reshape(rows, cols, channels).astype(BF16)
        out_ref[2 * mode + 1] = mixed_imag.reshape(rows, cols, channels).astype(BF16)


def mix(keep, got, weight):
    return pl.pallas_call(
        mix_kernel,
        out_shape=jax.ShapeDtypeStruct(keep.shape, BF16),
        compiler_params=pltpu.CompilerParams(vmem_limit_bytes=SMALL_BYTES),
        name="mix",
    )(keep, got, weight)


BEFORE, HERE, AFTER, BLOCK, PLACE, GROUP, HALO, FLIP, DROP = range(9)


def row_kernel(
    halos, sub, items_ref, variant_ref, field_ref, inv_ref, taps_ref,
    w_in_ref, bias_in_ref, w_out_ref, bias_out_ref, mine_ref, other_ref, *rest
):
    halo_refs = rest[:halos]
    out_ref, mixed_ref, joined_ref, hidden_ref = rest[-4:]
    xb = out_ref.shape[0]
    cols, channels = out_ref.shape[-2:]
    tokens = xb * cols
    field = lambda which: items_ref[variant_ref[0], which, pl.program_id(0)]

    @pl.when(field(GROUP) == 0)
    def _():
        mixed_ref[...] = mine_ref[field(PLACE)]

    @pl.when(field(GROUP) == 1)
    def _():
        mixed_ref[...] = other_ref[field(PLACE)]

    start = field(BLOCK) * xb
    before, here, after = field(BEFORE), field(HERE), field(AFTER)
    taps = taps_ref[...]
    flip = field(FLIP) == 1
    tap_before = jnp.where(flip, taps[2:3], taps[0:1]).astype(BF16)
    tap_here = taps[1:2].astype(BF16)
    tap_after = jnp.where(flip, taps[0:1], taps[2:3])
    tap_after = jnp.where(field(DROP) == 1, 0.0, tap_after).astype(BF16)
    source = field(HALO)

    def load(row, s):
        return field_ref[pl.ds(start + s * sub // cols, sub // cols), row].reshape(sub, channels)

    def load_after(s):
        part = load(after, s)
        for at, ref in enumerate(halo_refs):
            halo = ref[s * sub // cols : (s + 1) * sub // cols].reshape(sub, channels)
            part = jnp.where(source == at + 1, halo, part)
        return part

    def join(s):
        rows = slice(s * sub, (s + 1) * sub)
        lines = pl.ds(pl.multiple_of(start * cols, xb * cols) + s * sub, sub)
        spectral = jnp.dot(inv_ref[lines], mixed_ref[...], preferred_element_type=F32)
        conv = (
            tap_before * load(before, s) + tap_here * load(here, s) + tap_after * load_after(s)
        )
        joined_ref[rows] = (spectral + conv.astype(F32)).astype(BF16)

    def expand(s):
        rows = slice(s * sub, (s + 1) * sub)
        x = jnp.dot(joined_ref[rows], w_in_ref[...], preferred_element_type=F32)
        x = (x + bias_in_ref[...]).astype(BF16)
        u = x * (BF16(GELU_A) + BF16(GELU_B) * (x * x))
        hidden_ref[rows] = x + x * jnp.tanh(u)

    def project(s):
        rows = slice(s * sub, (s + 1) * sub)
        y = jnp.dot(hidden_ref[rows], w_out_ref[...], preferred_element_type=F32)
        y = load(here, s).astype(F32) + (0.5 * y + bias_out_ref[...])
        out_ref[s * sub // cols : (s + 1) * sub // cols] = y.reshape(
            (sub // cols,) + out_ref.shape[1:]
        ).astype(BF16)

    parts = tokens // sub
    for s in range(parts + 2):
        if s < parts:
            join(s)
        if 0 <= s - 1 < parts:
            expand(s - 1)
        if s >= 2:
            project(s - 2)


def rows_of(out, field, inv, items, variant, taps, dense, mixed, halos, xb, sub):
    x_rows, y_rows, cols, channels = field.shape
    w_in, bias_in, w_out, bias_out = dense
    hidden = w_in.shape[1]
    waves_cols = inv.shape[1]
    count = items.shape[2]
    tokens = xb * cols
    args = [
        items, variant, field, inv, taps, w_in, bias_in, w_out, bias_out, *mixed, *halos,
    ]
    in_specs = [pl.BlockSpec(memory_space=pltpu.VMEM)] * (len(args) - 2)
    aliases = {}
    if out is not None:
        aliases = {len(args): 0}
        in_specs.append(pl.BlockSpec(memory_space=pl.ANY))
        args.append(out)
    return pl.pallas_call(
        functools.partial(row_kernel, len(halos), min(sub, tokens)),
        grid_spec=pltpu.PrefetchScalarGridSpec(
            num_scalar_prefetch=2,
            grid=(count,),
            in_specs=in_specs,
            out_specs=pl.BlockSpec(
                (xb, 1, cols, channels), lambda i, r, v: (r[v[0], BLOCK, i], r[v[0], HERE, i], 0, 0)
            ),
            scratch_shapes=[
                pltpu.VMEM((waves_cols, channels), BF16),
                pltpu.VMEM((tokens, channels), BF16),
                pltpu.VMEM((tokens, hidden), BF16),
            ],
        ),
        out_shape=jax.ShapeDtypeStruct(field.shape, BF16),
        input_output_aliases=aliases,
        compiler_params=pltpu.CompilerParams(vmem_limit_bytes=ROWS_BYTES),
        name="rows",
    )(*args)


def local(features, spectral_weight, conv_taps, w_in, bias_in, w_out, bias_out):
    x_rows, y_rows, cols, channels = features.shape
    modes = spectral_weight.shape[0]
    gx_size = lax.axis_size("gx")
    gy_size = lax.axis_size("gy")
    gx = lax.axis_index("gx")
    gy = lax.axis_index("gy")

    half_rows = y_rows // 2
    side = gx & 1
    variant = (gy % 2 * 2 + side).reshape(1)
    variants = [(odd, core) for odd in range(2) for core in range(2)]
    edges_of = lambda odd: [0 if odd else y_rows - 1, y_rows - 1 if odd else 0]
    live = [p for p in range(2) if gy_size > p + 1]
    side_rows = lambda core: [core * half_rows + i for i in range(half_rows)]
    order = jnp.array([side_rows(1 - core) + side_rows(core) for _, core in variants], jnp.int32)
    edge_rows = jnp.array([edges_of(odd) for odd, _ in variants], jnp.int32)

    levels = gx_size.bit_length() - 1
    halving = max(min(levels - 1, modes.bit_length()), 1)
    own = jnp.int32(0)
    for level in range(1, halving):
        own = own + (gx >> level & 1) * (modes >> level)
    table, inverse = wave_tables(own, gx * x_rows, modes, x_rows, x_rows * gx_size)
    swap = lambda a, level: lax.ppermute(
        a, "gx", [(i, i ^ (1 << level)) for i in range(gx_size)]
    )
    parts = half_rows
    xb = x_rows // parts
    halos = [[] for _ in range(parts)]
    send, keep = forward_transform(features, widen(table, cols), order, variant)
    owned = modes >> halving - 1
    inv, weight = prepare(inverse, cols, spectral_weight, own.reshape(1), owned)
    for level in range(levels):
        got = swap(send, level)
        cut = []
        if level < parts:
            for p in live:
                pairs = [(i, i + 1) for i in range(p, gy_size - 1, 2)]
                cut.append(cut_edge(features, edge_rows, variant, p, level, parts, send))
                halos[level].append(
                    lax.ppermute(cut[-1], "gy", pairs + [(b, a) for a, b in pairs])
                )
        if level + 1 < levels:
            ahead = cut + ([weight] if level == levels - 2 else [])
            send, keep = combine(keep, got, level + 1 < halving, ahead)
    mixed = mix(keep, got, weight)
    for level in reversed(range(2, halving)):
        mixed = join(mixed, swap(mixed, level))
    mixed = [stack_modes([mixed, swap(mixed, 1)] if halving > 1 else [mixed])]
    mixed.append(swap(mixed[0], 0))

    def block_of(core, before, here, after, part, halo=0, flip=0, drop=0):
        group = 0 if here // half_rows == core else 1
        return before, here, after, part, here % half_rows, group, halo, flip, drop

    def calls_of(odd, core):
        calls = [[] for _ in range(parts)]
        for row in range(1, y_rows - 1):
            for part in range(parts):
                calls[0].append(block_of(core, row - 1, row, row + 1, part))
        for p, edge in reversed(list(enumerate(edges_of(odd)))):
            inner, flip = (1, 1) if edge == 0 else (y_rows - 2, 0)
            for part in range(parts):
                halo = live.index(p) + 1 if p in live else 0
                calls[part if halo else 0].append(
                    block_of(core, inner, edge, edge, part, halo, flip, 0 if halo else 1)
                )
        return calls

    every = [calls_of(odd, core) for odd, core in variants]
    dense = (w_in, bias_in[None], w_out, bias_out[None])
    out = None
    for part in range(parts):
        items = jnp.array([list(zip(*calls[part])) for calls in every], jnp.int32)
        out = rows_of(
            out, features, inv, items, variant, conv_taps, dense, mixed, halos[part], xb, 512 if part == 0 else 256
        )
    return out


def solution(mesh):
    return jax.shard_map(
        local,
        mesh=mesh,
        in_specs=(P("gx", "gy", None, None), P(), P(), P(), P(), P(), P()),
        out_specs=P("gx", "gy", None, None),
        check_vma=False,
    )
```

time: 179 us -> 69.2 us (0.39)
  matrix products: 53.8 us -> 0 us
  local copies, waits for them, and re-layouts: 53.1 us -> 4.12 us
  Pallas kernels: 0 us -> 35.3 us
  blocking collectives: 20.8 us -> 0 us
  between operations: 13.5 us -> 0.27 us
  other arithmetic: 11.9 us -> 0.38 us
  starting transfers between devices: 7.54 us -> 13.1 us
  waiting for transfers between devices: 18.3 us -> 15.8 us
    dot_general x7 -> x0, matrix products: 53.8 us -> none  [the longest x1 31.3 us: local(): jnp.dot(hidden, w_out, preferred_element_type=jnp.float32)]
    pallas_call x0 -> x13, Pallas kernels: none -> 35.3 us  [the longest x2 29.1 us: rows_of(): pl.pallas_call(functools.partial(row_kernel, len(halos), min(sub, tokens)...]
    convert_element_type x2 -> x0, local copies, waits for them, and re-layouts: 29.1 us -> none  [the longest x1 17.7 us: local(): features.reshape(x_rows * row_count, channels).astype(jnp.float32)]
    all_gather x1 -> x0, blocking collectives: 20.8 us -> none  [local(): mixed = lax.all_gather(mixed_own, 'gx', axis=1, tiled=True)]
    reduce_scatter x1 -> x0, waiting for transfers between devices: 18.3 us -> none  [local(): lax.psum_scatter(spectrum, 'gx', scatter_dimension=1, tiled=True)]
    unnamed x14 -> x24, local copies, waits for them, and re-layouts: 20.2 us -> 4.12 us
    ppermute x2 -> x9, waiting for transfers between devices: 0.01 us -> 15.8 us  [the longest x7 15.8 us: local(): lax.ppermute(a, 'gx', [(i, i ^ 1 << level) for i in range(gx_size)])]
    unnamed x1 -> x0, other arithmetic: 10.9 us -> none
  transfers between devices with their start and end apart: 3 -> 9, of which waited for: 1 -> 6; matrix products, arithmetic and copies ran while one was open for 20% -> 0% of each run, Pallas kernels for 0% -> 38%
where the time goes in v2:
time: 69.2 us; the launch traced here: 69 us
  Pallas kernels  35.3 us (51%)
  waiting for transfers between devices  15.8 us (23%)
  starting transfers between devices  13.1 us (19%)
  local copies, waits for them, and re-layouts  4.12 us (6%)
    pallas_call x2, Pallas kernels, rows_of(): pl.pallas_call(functools.partial(row_kernel, len(halos), min(sub, tokens)...  29.1 us
    ppermute x7, waiting for transfers between devices, local(): lax.ppermute(a, 'gx', [(i, i ^ 1 << level) for i in range(gx_size)])  15.8 us
    ppermute x7, starting transfers between devices, local(): lax.ppermute(a, 'gx', [(i, i ^ 1 << level) for i in range(gx_size)])  9.78 us
    unnamed x24, local copies, waits for them, and re-layouts  4.12 us
    ppermute x2, starting transfers between devices, local(): lax.ppermute(cut[-1], 'gy', pairs + [(b, a) for a, b in pairs])  3.36 us
    pallas_call x1, Pallas kernels, forward_transform(): pl.pallas_call(forward_kernel, in_specs=[smem, smem, vmem, vmem], out_spe...  2.96 us
    pallas_call x2, Pallas kernels, cut_edge(): pl.pallas_call(functools.partial(cut_kernel, p, part * count), in_specs=[...  1.42 us
  transfers between devices with their start and end apart: 9, of which 6 were waited for; matrix products, arithmetic and copies ran while one was open for 0% of the time, Pallas kernels for 38%

profile of v2, /device:TPU:0, one launch (start us, length us, event | category | flops | bytes accessed | tf_op | source)
XLA Modules:
  0.0 69.0 jit_solution(14986781455978695479)
XLA Ops:
  0.1 0.4 multiply_convert_fusion
  0.4 0.7 widen.1.wide_ref
  1.1 0.0 copy-start
  1.1 3.4 %copy-done = bf16[512,4,8,256]{3,2,1,0:T(8,128)(2,1)S(1)} copy-done((bf16[512,4,8,256]{3,2,1,0:T(8,128)(2,1)S(1)}, bf16[512,4,8,256]{3,2,1,0:T(8,128)(2,1)}, u32[]{:S(2)}) %copy-start) | copy-done | bytes 8388632
  4.5 0.7 copy-done.11
  5.2 3.0 %forward.1 = (bf16[32,2,8,256]{3,2,1,0:T(8,128)(2,1)S(1)}, f32[32,2,8,256]{3,2,1,0:T(8,128)S(1)}) custom-call(s32[4,4]{1,0:T(4,128)S(1)} %copy-done.11, s32[1]{0:T(128)} %bitcast.variant_ref, bf16[256,4096]{1,0:T(8,128)(2,1)S(1)} %widen.1.wide_ref, bf16[512,4,8,256]{3,2,1,0:T(8,128)(2,1)S(1)} %copy-done), custom_call_target="tpu_custom_call" | custom-call | tf_op jit(solution)/shard_map/forward/pallas_call | solution.py:130
  8.1 0.5 collective-permute-start
  8.7 0.7 %cut.2.refs_0_ = bf16[256,8,256]{2,1,0:T(8,128)(2,1)S(1)} custom-call(s32[4,2]{1,0:T(4,128)S(1)} %copy-done.9, s32[1]{0:T(128)} %bitcast.variant_ref, bf16[512,4,8,256]{3,2,1,0:T(8,128)(2,1)S(1)} %copy-done.1, bf16[32,2,8,256]{3,2,1,0:T(8,128)(2,1)S(1)} %get-tuple-element.17.ahead_ref), custom_call_target="tpu_custom_call" | custom-call | tf_op jit(solution)/shard_map/cut/pallas_call | solution.py:69
  9.4 2.9 %collective-permute-start.8 = (bf16[256,8,256]{2,1,0:T(8,128)(2,1)S(1)}, bf16[256,8,256]{2,1,0:T(8,128)(2,1)S(1)}, u32[]{:S(2)}, u32[]{:S(2)}) collective-permute-start(bf16[256,8,256]{2,1,0:T(8,128)(2,1)S(1)} %cut.2.refs_0_), channel_id=1, source_target_pairs={{0,1},{1,0},{2,3},{3,2},{4,5},{5,4},{6,7},{7,6},{8,9},{9,8},{10,11... | collective-permute-start | bytes 3145736 | tf_op jit(solution)/shard_map/ppermute | solution.py:420
  12.3 0.1 halve.2
  12.4 0.0 copy-start.3
  12.4 0.0 copy-start.6
  12.4 0.0 copy-start.7
  12.4 0.7 %cut.3.refs_0_ = bf16[256,8,256]{2,1,0:T(8,128)(2,1)S(1)} custom-call(s32[4,2]{1,0:T(4,128)S(1)} %copy-done.9, s32[1]{0:T(128)} %bitcast.variant_ref, bf16[512,4,8,256]{3,2,1,0:T(8,128)(2,1)S(1)} %copy-done.1, bf16[16,2,8,256]{3,2,1,0:T(8,128)(2,1)S(1)} %get-tuple-element.19.ahead_ref), custom_call_target="tpu_custom_call" | custom-call | tf_op jit(solution)/shard_map/cut/pallas_call | solution.py:69
  13.1 0.5 collective-permute-start.7
  13.6 1.7 %collective-permute-start.1 = (bf16[16,2,8,256]{3,2,1,0:T(8,128)(2,1)S(1)}, bf16[16,2,8,256]{3,2,1,0:T(8,128)(2,1)S(1)}, u32[]{:S(2)}, u32[]{:S(2)}) collective-permute-start(bf16[16,2,8,256]{3,2,1,0:T(8,128)(2,1)S(1)} %get-tuple-element.19.ahead_ref), channel_id=1, source_target_pairs={{0,4},{2,6},{4,0},{6,2},{8,12},{10,14},{12,8},{14,10},{16,20},{18,... | collective-permute-start | bytes 393224 | tf_op jit(solution)/shard_map/ppermute | solution.py:403
  15.3 3.6 %collective-permute-done.1.got_ref = bf16[16,2,8,256]{3,2,1,0:T(8,128)(2,1)S(1)} collective-permute-done((bf16[16,2,8,256]{3,2,1,0:T(8,128)(2,1)S(1)}, bf16[16,2,8,256]{3,2,1,0:T(8,128)(2,1)S(1)}, u32[]{:S(2)}, u32[]{:S(2)}) %collective-permute-start.1) | collective-permute-done | bytes 131104 | tf_op jit(solution)/shard_map/ppermute | solution.py:403
  18.9 1.6 %collective-permute-start.2 = (bf16[8,2,8,256]{3,2,1,0:T(8,128)(2,1)S(1)}, bf16[8,2,8,256]{3,2,1,0:T(8,128)(2,1)S(1)}, u32[]{:S(2)}, u32[]{:S(2)}) collective-permute-start(bf16[8,2,8,256]{3,2,1,0:T(8,128)(2,1)S(1)} %get-tuple-element.21), channel_id=1, source_target_pairs={{0,8},{2,10},{4,12},{6,14},{8,0},{10,2},{12,4},{14,6},{16,24},{18,... | collective-permute-start | bytes 196616 | tf_op jit(solution)/shard_map/ppermute | solution.py:403
  20.5 0.7 %prepare.1 = (bf16[4096,256]{1,0:T(8,128)(2,1)S(1)}, bf16[4,2,256,256]{3,2,1,0:T(8,128)(2,1)S(1)}) custom-call(s32[1]{0:T(128)} %bitcast.1.which_ref, bf16[32,512]{1,0:T(8,128)(2,1)S(1)} %get-tuple-element.26.table_ref, bf16[16,2,256,256]{3,2,1,0:T(8,128)(2,1)S(1)} %copy-done.2), custom_call_target="tpu_custom_call" | custom-call | tf_op jit(solution)/shard_map/prepare/pallas_call | solution.py:157
  21.3 2.0 %collective-permute-done.2.got_ref = bf16[8,2,8,256]{3,2,1,0:T(8,128)(2,1)S(1)} collective-permute-done((bf16[8,2,8,256]{3,2,1,0:T(8,128)(2,1)S(1)}, bf16[8,2,8,256]{3,2,1,0:T(8,128)(2,1)S(1)}, u32[]{:S(2)}, u32[]{:S(2)}) %collective-permute-start.2) | collective-permute-done | bytes 65568 | tf_op jit(solution)/shard_map/ppermute | solution.py:403
  23.2 2.7 %collective-permute-start.3 = (bf16[8,2,8,256]{3,2,1,0:T(8,128)(2,1)S(1)}, bf16[8,2,8,256]{3,2,1,0:T(8,128)(2,1)S(1)}, u32[]{:S(2)}, u32[]{:S(2)}) collective-permute-start(bf16[8,2,8,256]{3,2,1,0:T(8,128)(2,1)S(1)} %get-tuple-element.24), channel_id=1, source_target_pairs={{0,16},{2,18},{4,20},{6,22},{8,24},{10,26},{12,28},{14,30},{16,0},... | collective-permute-start | bytes 196616 | tf_op jit(solution)/shard_map/ppermute | solution.py:403
  25.9 2.6 %collective-permute-done.3.got_ref = bf16[8,2,8,256]{3,2,1,0:T(8,128)(2,1)S(1)} collective-permute-done((bf16[8,2,8,256]{3,2,1,0:T(8,128)(2,1)S(1)}, bf16[8,2,8,256]{3,2,1,0:T(8,128)(2,1)S(1)}, u32[]{:S(2)}, u32[]{:S(2)}) %collective-permute-start.3) | collective-permute-done | bytes 65568 | tf_op jit(solution)/shard_map/ppermute | solution.py:403
  28.5 0.3 mix.1.mine_ref
  28.8 1.6 %collective-permute-start.4 = (bf16[8,2,8,256]{3,2,1,0:T(8,128)(2,1)S(1)}, bf16[8,2,8,256]{3,2,1,0:T(8,128)(2,1)S(1)}, u32[]{:S(2)}, u32[]{:S(2)}) collective-permute-start(bf16[8,2,8,256]{3,2,1,0:T(8,128)(2,1)S(1)} %mix.1.mine_ref), channel_id=1, source_target_pairs={{0,8},{2,10},{4,12},{6,14},{8,0},{10,2},{12,4},{14,6},{16,24},{18,... | collective-permute-start | bytes 196616 | tf_op jit(solution)/shard_map/ppermute | solution.py:403
  30.4 2.7 %collective-permute-done.4.got_ref = bf16[8,2,8,256]{3,2,1,0:T(8,128)(2,1)S(1)} collective-permute-done((bf16[8,2,8,256]{3,2,1,0:T(8,128)(2,1)S(1)}, bf16[8,2,8,256]{3,2,1,0:T(8,128)(2,1)S(1)}, u32[]{:S(2)}, u32[]{:S(2)}) %collective-permute-start.4) | collective-permute-done | bytes 65568 | tf_op jit(solution)/shard_map/ppermute | solution.py:403
  33.1 1.6 %collective-permute-start.5 = (bf16[16,2,8,256]{3,2,1,0:T(8,128)(2,1)S(1)}, bf16[16,2,8,256]{3,2,1,0:T(8,128)(2,1)S(1)}, u32[]{:S(2)}, u32[]{:S(2)}) collective-permute-start(bf16[16,2,8,256]{3,2,1,0:T(8,128)(2,1)S(1)} %join.1.refs_0_), channel_id=1, source_target_pairs={{0,4},{2,6},{4,0},{6,2},{8,12},{10,14},{12,8},{14,10},{16,20},{18,... | collective-permute-start | bytes 393224 | tf_op jit(solution)/shard_map/ppermute | solution.py:403
  34.7 3.4 %collective-permute-done.5.refs_1_ = bf16[16,2,8,256]{3,2,1,0:T(8,128)(2,1)S(1)} collective-permute-done((bf16[16,2,8,256]{3,2,1,0:T(8,128)(2,1)S(1)}, bf16[16,2,8,256]{3,2,1,0:T(8,128)(2,1)S(1)}, u32[]{:S(2)}, u32[]{:S(2)}) %collective-permute-start.5) | collective-permute-done | bytes 131104 | tf_op jit(solution)/shard_map/ppermute | solution.py:403
  38.2 0.1 collective-permute-start.6
  38.3 1.5 %collective-permute-done.6.other_ref = bf16[2,256,256]{2,1,0:T(8,128)(2,1)S(1)} collective-permute-done((bf16[2,256,256]{2,1,0:T(8,128)(2,1)S(1)}, bf16[2,256,256]{2,1,0:T(8,128)(2,1)S(1)}, u32[]{:S(2)}, u32[]{:S(2)}) %collective-permute-start.6) | collective-permute-done | bytes 262176 | tf_op jit(solution)/shard_map/ppermute | solution.py:403
  39.8 0.0 copy-start.5
  39.8 23.7 %rows.2.rest_1_ = bf16[512,4,8,256]{3,2,1,0:T(8,128)(2,1)} custom-call(s32[4,9,7]{2,1,0:T(8,128)S(1)} %copy-done.6, s32[1]{0:T(128)} %bitcast.variant_ref, bf16[512,4,8,256]{3,2,1,0:T(8,128)(2,1)S(1)} %copy-done.1, bf16[4096,256]{1,0:T(8,128)(2,1)S(1)} %get-tuple-element.15.inv_ref, f32[3,256]{1,0:T(4,128)S(1)} %copy-done.7, ...), custom_call_target="tpu_custom_call" | custom-call | tf_op jit(solution)/shard_map/rows/pallas_call | solution.py:357
  63.5 5.5 %rows.3 = bf16[512,4,8,256]{3,2,1,0:T(8,128)(2,1)} custom-call(s32[4,9,1]{2,1,0:T(8,128)S(1)} %copy-done.5, s32[1]{0:T(128)} %bitcast.variant_ref, bf16[512,4,8,256]{3,2,1,0:T(8,128)(2,1)S(1)} %copy-done.1, bf16[4096,256]{1,0:T(8,128)(2,1)S(1)} %get-tuple-element.15.inv_ref, f32[3,256]{1,0:T(4,128)S(1)} %copy-done.7, ...), custom_call_target="tpu_custom_call", output_to_operand_aliasing={{}: (12, {})} | custom-call | tf_op jit(solution)/shard_map/rows/pallas_call | solution.py:357
  (28 shorter events, 0.1 us)
Async XLA Ops:
  0.0 8.7 %copy-start.9 = (s32[4,2]{1,0:T(4,128)S(1)}, s32[4,2]{1,0:T(4,128)}, u32[]{:S(2)}) copy-start(s32[4,2]{1,0:T(4,128)} %constant.81.clone.rows_ref) | copy-start | bytes 100
  1.1 3.4 %copy-start = (bf16[512,4,8,256]{3,2,1,0:T(8,128)(2,1)S(1)}, bf16[512,4,8,256]{3,2,1,0:T(8,128)(2,1)}, u32[]{:S(2)}) copy-start(bf16[512,4,8,256]{3,2,1,0:T(8,128)(2,1)} %field_ref.9) | copy-start | bytes 25165828
  4.5 0.7 copy-start.11
  5.2 3.5 %copy-start.1 = (bf16[512,4,8,256]{3,2,1,0:T(8,128)(2,1)S(1)}, bf16[512,4,8,256]{3,2,1,0:T(8,128)(2,1)}, u32[]{:S(2)}) copy-start(bf16[512,4,8,256]{3,2,1,0:T(8,128)(2,1)} %field_ref.9) | copy-start | bytes 25165828
  8.1 4.1 %collective-permute-start = (bf16[32,2,8,256]{3,2,1,0:T(8,128)(2,1)S(1)}, bf16[32,2,8,256]{3,2,1,0:T(8,128)(2,1)S(1)}, u32[]{:S(2)}, u32[]{:S(2)}) collective-permute-start(bf16[32,2,8,256]{3,2,1,0:T(8,128)(2,1)S(1)} %get-tuple-element.17.ahead_ref), channel_id=1, source_target_pairs={{0,2},{2,0},{4,6},{6,4},{8,10},{10,8},{12,14},{14,12},{16,18},{18,... | collective-permute-start | bytes 786440 | tf_op jit(solution)/shard_map/ppermute | solution.py:403
  9.4 11.2 %copy-start.2 = (bf16[16,2,256,256]{3,2,1,0:T(8,128)(2,1)S(1)}, bf16[16,2,256,256]{3,2,1,0:T(8,128)(2,1)}, u32[]{:S(2)}) copy-start(bf16[16,2,256,256]{3,2,1,0:T(8,128)(2,1)} %weight_ref.1) | copy-start | bytes 12582916
  9.4 30.4 %collective-permute-start.8 = (bf16[256,8,256]{2,1,0:T(8,128)(2,1)S(1)}, bf16[256,8,256]{2,1,0:T(8,128)(2,1)S(1)}, u32[]{:S(2)}, u32[]{:S(2)}) collective-permute-start(bf16[256,8,256]{2,1,0:T(8,128)(2,1)S(1)} %cut.2.refs_0_), channel_id=1, source_target_pairs={{0,1},{1,0},{2,3},{3,2},{4,5},{5,4},{6,7},{7,6},{8,9},{9,8},{10,11... | collective-permute-start | bytes 3145736 | tf_op jit(solution)/shard_map/ppermute | solution.py:420
  12.4 27.4 %copy-start.3 = (bf16[256,1024]{1,0:T(8,128)(2,1)S(1)}, bf16[256,1024]{1,0:T(8,128)(2,1)}, u32[]{:S(2)}) copy-start(bf16[256,1024]{1,0:T(8,128)(2,1)} %w_in_ref.3) | copy-start | bytes 1572868
  12.4 27.4 %copy-start.4 = (bf16[1024,256]{1,0:T(8,128)(2,1)S(1)}, bf16[1024,256]{1,0:T(8,128)(2,1)}, u32[]{:S(2)}) copy-start(bf16[1024,256]{1,0:T(8,128)(2,1)} %w_out_ref.3) | copy-start | bytes 1572868
  12.4 27.4 %copy-start.6 = (s32[4,9,7]{2,1,0:T(8,128)S(1)}, s32[4,9,7]{2,1,0:T(8,128)}, u32[]{:S(2)}) copy-start(s32[4,9,7]{2,1,0:T(8,128)} %constant.82.clone.items_ref) | copy-start | bytes 3028
  12.4 27.4 %copy-start.7 = (f32[3,256]{1,0:T(4,128)S(1)}, f32[3,256]{1,0:T(4,128)}, u32[]{:S(2)}) copy-start(f32[3,256]{1,0:T(4,128)} %taps_ref.3) | copy-start | bytes 9220
  12.4 27.4 %copy-start.8 = (f32[1024]{0:T(1024)S(1)}, f32[1024]{0:T(1024)}, u32[]{:S(2)}) copy-start(f32[1024]{0:T(1024)} %param.15) | copy-start | bytes 12292
  12.4 27.4 %copy-start.10 = (f32[256]{0:T(256)S(1)}, f32[256]{0:T(256)}, u32[]{:S(2)}) copy-start(f32[256]{0:T(256)} %param.17) | copy-start | bytes 3076
  13.1 50.4 %collective-permute-start.7 = (bf16[256,8,256]{2,1,0:T(8,128)(2,1)S(1)}, bf16[256,8,256]{2,1,0:T(8,128)(2,1)S(1)}, u32[]{:S(2)}, u32[]{:S(2)}) collective-permute-start(bf16[256,8,256]{2,1,0:T(8,128)(2,1)S(1)} %cut.3.refs_0_), channel_id=1, source_target_pairs={{0,1},{1,0},{2,3},{3,2},{4,5},{5,4},{6,7},{7,6},{8,9},{9,8},{10,11... | collective-permute-start | bytes 3145736 | tf_op jit(solution)/shard_map/ppermute | solution.py:420
  13.6 5.3 %collective-permute-start.1 = (bf16[16,2,8,256]{3,2,1,0:T(8,128)(2,1)S(1)}, bf16[16,2,8,256]{3,2,1,0:T(8,128)(2,1)S(1)}, u32[]{:S(2)}, u32[]{:S(2)}) collective-permute-start(bf16[16,2,8,256]{3,2,1,0:T(8,128)(2,1)S(1)} %get-tuple-element.19.ahead_ref), channel_id=1, source_target_pairs={{0,4},{2,6},{4,0},{6,2},{8,12},{10,14},{12,8},{14,10},{16,20},{18,... | collective-permute-start | bytes 393224 | tf_op jit(solution)/shard_map/ppermute | solution.py:403
  18.9 4.3 %collective-permute-start.2 = (bf16[8,2,8,256]{3,2,1,0:T(8,128)(2,1)S(1)}, bf16[8,2,8,256]{3,2,1,0:T(8,128)(2,1)S(1)}, u32[]{:S(2)}, u32[]{:S(2)}) collective-permute-start(bf16[8,2,8,256]{3,2,1,0:T(8,128)(2,1)S(1)} %get-tuple-element.21), channel_id=1, source_target_pairs={{0,8},{2,10},{4,12},{6,14},{8,0},{10,2},{12,4},{14,6},{16,24},{18,... | collective-permute-start | bytes 196616 | tf_op jit(solution)/shard_map/ppermute | solution.py:403
  23.2 5.2 %collective-permute-start.3 = (bf16[8,2,8,256]{3,2,1,0:T(8,128)(2,1)S(1)}, bf16[8,2,8,256]{3,2,1,0:T(8,128)(2,1)S(1)}, u32[]{:S(2)}, u32[]{:S(2)}) collective-permute-start(bf16[8,2,8,256]{3,2,1,0:T(8,128)(2,1)S(1)} %get-tuple-element.24), channel_id=1, source_target_pairs={{0,16},{2,18},{4,20},{6,22},{8,24},{10,26},{12,28},{14,30},{16,0},... | collective-permute-start | bytes 196616 | tf_op jit(solution)/shard_map/ppermute | solution.py:403
  28.8 4.3 %collective-permute-start.4 = (bf16[8,2,8,256]{3,2,1,0:T(8,128)(2,1)S(1)}, bf16[8,2,8,256]{3,2,1,0:T(8,128)(2,1)S(1)}, u32[]{:S(2)}, u32[]{:S(2)}) collective-permute-start(bf16[8,2,8,256]{3,2,1,0:T(8,128)(2,1)S(1)} %mix.1.mine_ref), channel_id=1, source_target_pairs={{0,8},{2,10},{4,12},{6,14},{8,0},{10,2},{12,4},{14,6},{16,24},{18,... | collective-permute-start | bytes 196616 | tf_op jit(solution)/shard_map/ppermute | solution.py:403
  33.1 5.0 %collective-permute-start.5 = (bf16[16,2,8,256]{3,2,1,0:T(8,128)(2,1)S(1)}, bf16[16,2,8,256]{3,2,1,0:T(8,128)(2,1)S(1)}, u32[]{:S(2)}, u32[]{:S(2)}) collective-permute-start(bf16[16,2,8,256]{3,2,1,0:T(8,128)(2,1)S(1)} %join.1.refs_0_), channel_id=1, source_target_pairs={{0,4},{2,6},{4,0},{6,2},{8,12},{10,14},{12,8},{14,10},{16,20},{18,... | collective-permute-start | bytes 393224 | tf_op jit(solution)/shard_map/ppermute | solution.py:403
  38.2 1.6 %collective-permute-start.6 = (bf16[2,256,256]{2,1,0:T(8,128)(2,1)S(1)}, bf16[2,256,256]{2,1,0:T(8,128)(2,1)S(1)}, u32[]{:S(2)}, u32[]{:S(2)}) collective-permute-start(bf16[2,256,256]{2,1,0:T(8,128)(2,1)S(1)} %stack.1.mine_ref), channel_id=1, source_target_pairs={{0,2},{2,0},{4,6},{6,4},{8,10},{10,8},{12,14},{14,12},{16,18},{18,... | collective-permute-start | bytes 786440 | tf_op jit(solution)/shard_map/ppermute | solution.py:403
  39.8 23.7 %copy-start.5 = (s32[4,9,1]{2,1,0:T(8,128)S(1)}, s32[4,9,1]{2,1,0:T(8,128)}, u32[]{:S(2)}) copy-start(s32[4,9,1]{2,1,0:T(8,128)} %constant.83.clone.items_ref) | copy-start | bytes 436

commit v3 on v2

--- a/solution.py
+++ b/solution.py
@@ -58,29 +58,6 @@
     return jnp.where(same, wide[:, None, :], 0.0).reshape(waves * cols, width).astype(BF16)
 
 
-def cut_kernel(p, start, rows_ref, variant_ref, field_ref, ahead_ref, cut_ref):
-    row = rows_ref[variant_ref[0], p]
-    cut_ref[...] = field_ref[start : start + cut_ref.shape[0], row]
-
-
-def cut_edge(field, rows, variant, p, part, parts, ahead):
-    x_rows, _, cols, channels = field.shape
-    count = x_rows // parts
-    return pl.pallas_call(
-        functools.partial(cut_kernel, p, part * count),
-        in_specs=[
-            pl.BlockSpec(memory_space=pltpu.SMEM),
-            pl.BlockSpec(memory_space=pltpu.SMEM),
-            pl.BlockSpec(memory_space=pltpu.VMEM),
-            pl.BlockSpec(memory_space=pl.ANY),
-        ],
-        out_specs=pl.BlockSpec(memory_space=pltpu.VMEM),
-        out_shape=jax.ShapeDtypeStruct((count, cols, channels), BF16),
-        compiler_params=pltpu.CompilerParams(vmem_limit_bytes=SMALL_BYTES),
-        name="cut",
-    )(rows, variant, field, ahead)
-
-
 def widen_kernel(table_ref, wide_ref):
     x_rows = table_ref.shape[1]
     cols = wide_ref.shape[1] // x_rows
@@ -99,18 +76,18 @@
         out_shape=jax.ShapeDtypeStruct((waves * cols, x_rows * cols), BF16),
         compiler_params=pltpu.CompilerParams(vmem_limit_bytes=SMALL_BYTES),
         cost_estimate=pl.CostEstimate(
-            flops=10**9, bytes_accessed=4 * waves * cols * x_rows * cols, transcendentals=0
+            flops=5 * 10**9, bytes_accessed=4 * waves * cols * x_rows * cols, transcendentals=0
         ),
         name="widen",
     )(table)
 
 
-def forward_kernel(rows_ref, variant_ref, wide_ref, field_ref, send_ref, keep_ref):
+def forward_kernel(live, place_ref, wide_ref, field_ref, send_ref, keep_ref, *edge_refs):
     x_rows, y_rows, cols, channels = field_ref.shape
     sent = send_ref.shape[1]
     waves = send_ref.shape[0]
     for place in range(y_rows):
-        row = rows_ref[variant_ref[0], place]
+        row = jnp.where(place_ref[0] >> 1 & 1 == 0, (place + sent) % y_rows, place)
         part = jnp.dot(
             wide_ref[...],
             field_ref[:, row].reshape(x_rows * cols, channels),
@@ -120,26 +97,55 @@
             send_ref[:, place] = part.astype(BF16)
         else:
             keep_ref[:, place - sent] = part
-
-
-def forward_transform(features, wide, rows, variant):
+    odd = place_ref[0] & 1
+    for p, ref in zip(live, edge_refs):
+        ref[...] = field_ref[:, (odd if p else 1 - odd) * (y_rows - 1)]
+
+
+def forward_transform(features, wide, place, live):
     x_rows, y_rows, cols, channels = features.shape
     shape = (wide.shape[0] // cols, y_rows // 2, cols, channels)
     vmem = pl.BlockSpec(memory_space=pltpu.VMEM)
     smem = pl.BlockSpec(memory_space=pltpu.SMEM)
     return pl.pallas_call(
-        forward_kernel,
-        in_specs=[smem, smem, vmem, vmem],
-        out_specs=[vmem, vmem],
-        out_shape=[jax.ShapeDtypeStruct(shape, BF16), jax.ShapeDtypeStruct(shape, F32)],
+        functools.partial(forward_kernel, live),
+        in_specs=[smem, vmem, vmem],
+        out_specs=[vmem] * (2 + len(live)),
+        out_shape=[
+            jax.ShapeDtypeStruct(shape, BF16),
+            jax.ShapeDtypeStruct(shape, F32),
+            *[jax.ShapeDtypeStruct((x_rows, cols, channels), BF16) for _ in live],
+        ],
         compiler_params=pltpu.CompilerParams(vmem_limit_bytes=SMALL_BYTES),
         name="forward",
-    )(rows, variant, wide, features)
-
-
-def prepare_kernel(which_ref, table_ref, weight_ref, inv_ref, own_ref, sem):
+    )(place, wide, features)
+
+
+def cut_kernel(start, edge_ref, ahead_ref, cut_ref):
+    cut_ref[...] = edge_ref[start : start + cut_ref.shape[0]]
+
+
+def cut_edge(edge, part, parts, ahead):
+    count = edge.shape[0] // parts
+    vmem = pl.BlockSpec(memory_space=pltpu.VMEM)
+    return pl.pallas_call(
+        functools.partial(cut_kernel, part * count),
+        in_specs=[vmem, pl.BlockSpec(memory_space=pl.ANY)],
+        out_specs=vmem,
+        out_shape=jax.ShapeDtypeStruct((count,) + edge.shape[1:], BF16),
+        compiler_params=pltpu.CompilerParams(vmem_limit_bytes=SMALL_BYTES),
+        name="cut",
+    )(edge, ahead)
+
+
+def first_mode(gx, halving, modes):
+    return sum((gx >> level & 1) * (modes >> level) for level in range(1, halving))
+
+
+def prepare_kernel(halving, place_ref, table_ref, weight_ref, inv_ref, own_ref, sem):
     owned = own_ref.shape[0]
-    move = pltpu.make_async_copy(weight_ref.at[pl.ds(which_ref[0], owned)], own_ref, sem)
+    first = first_mode(place_ref[0] >> 1, halving, weight_ref.shape[0])
+    move = pltpu.make_async_copy(weight_ref.at[pl.ds(first, owned)], own_ref, sem)
     move.start()
     waves, x_rows = table_ref.shape
     cols = inv_ref.shape[0] // x_rows
@@ -151,11 +157,12 @@
     move.wait()
 
 
-def prepare(table, cols, weight, which, owned):
+def prepare(table, cols, weight, place, halving):
     waves, x_rows = table.shape
+    owned = weight.shape[0] >> halving - 1
     vmem = pl.BlockSpec(memory_space=pltpu.VMEM)
     return pl.pallas_call(
-        prepare_kernel,
+        functools.partial(prepare_kernel, halving),
         in_specs=[
             pl.BlockSpec(memory_space=pltpu.SMEM),
             vmem,
@@ -169,7 +176,7 @@
         scratch_shapes=[pltpu.SemaphoreType.DMA],
         compiler_params=pltpu.CompilerParams(vmem_limit_bytes=SMALL_BYTES),
         name="prepare",
-    )(which, table, weight)
+    )(place, table, weight)
 
 
 def halve_kernel(half, keep_ref, got_ref, *refs):
@@ -266,7 +273,7 @@
 
 
 def row_kernel(
-    halos, sub, items_ref, variant_ref, field_ref, inv_ref, taps_ref,
+    halos, sub, items_ref, place_ref, field_ref, inv_ref, taps_ref,
     w_in_ref, bias_in_ref, w_out_ref, bias_out_ref, mine_ref, other_ref, *rest
 ):
     halo_refs = rest[:halos]
@@ -274,7 +281,7 @@
     xb = out_ref.shape[0]
     cols, channels = out_ref.shape[-2:]
     tokens = xb * cols
-    field = lambda which: items_ref[variant_ref[0], which, pl.program_id(0)]
+    field = lambda which: items_ref[place_ref[0] & 3, which, pl.program_id(0)]
 
     @pl.when(field(GROUP) == 0)
     def _():
@@ -338,7 +345,7 @@
             project(s - 2)
 
 
-def rows_of(out, field, inv, items, variant, taps, dense, mixed, halos, xb, sub):
+def rows_of(out, field, inv, items, place, taps, dense, mixed, halos, xb, sub):
     x_rows, y_rows, cols, channels = field.shape
     w_in, bias_in, w_out, bias_out = dense
     hidden = w_in.shape[1]
@@ -346,7 +353,7 @@
     count = items.shape[2]
     tokens = xb * cols
     args = [
-        items, variant, field, inv, taps, w_in, bias_in, w_out, bias_out, *mixed, *halos,
+        items, place, field, inv, taps, w_in, bias_in, w_out, bias_out, *mixed, *halos,
     ]
     in_specs = [pl.BlockSpec(memory_space=pltpu.VMEM)] * (len(args) - 2)
     aliases = {}
@@ -361,7 +368,7 @@
             grid=(count,),
             in_specs=in_specs,
             out_specs=pl.BlockSpec(
-                (xb, 1, cols, channels), lambda i, r, v: (r[v[0], BLOCK, i], r[v[0], HERE, i], 0, 0)
+                (xb, 1, cols, channels), lambda i, r, v: (r[v[0] & 3, BLOCK, i], r[v[0] & 3, HERE, i], 0, 0)
             ),
             scratch_shapes=[
                 pltpu.VMEM((waves_cols, channels), BF16),
@@ -385,20 +392,14 @@
     gy = lax.axis_index("gy")
 
     half_rows = y_rows // 2
-    side = gx & 1
-    variant = (gy % 2 * 2 + side).reshape(1)
-    variants = [(odd, core) for odd in range(2) for core in range(2)]
+    place = (gx * 2 + gy % 2).reshape(1)
+    variants = [(odd, core) for core in range(2) for odd in range(2)]
     edges_of = lambda odd: [0 if odd else y_rows - 1, y_rows - 1 if odd else 0]
     live = [p for p in range(2) if gy_size > p + 1]
-    side_rows = lambda core: [core * half_rows + i for i in range(half_rows)]
-    order = jnp.array([side_rows(1 - core) + side_rows(core) for _, core in variants], jnp.int32)
-    edge_rows = jnp.array([edges_of(odd) for odd, _ in variants], jnp.int32)
 
     levels = gx_size.bit_length() - 1
     halving = max(min(levels - 1, modes.bit_length()), 1)
-    own = jnp.int32(0)
-    for level in range(1, halving):
-        own = own + (gx >> level & 1) * (modes >> level)
+    own = first_mode(gx, halving, modes)
     table, inverse = wave_tables(own, gx * x_rows, modes, x_rows, x_rows * gx_size)
     swap = lambda a, level: lax.ppermute(
         a, "gx", [(i, i ^ (1 << level)) for i in range(gx_size)]
@@ -406,16 +407,15 @@
     parts = half_rows
     xb = x_rows // parts
     halos = [[] for _ in range(parts)]
-    send, keep = forward_transform(features, widen(table, cols), order, variant)
-    owned = modes >> halving - 1
-    inv, weight = prepare(inverse, cols, spectral_weight, own.reshape(1), owned)
+    send, keep, *edge = forward_transform(features, widen(table, cols), place, live)
+    inv, weight = prepare(inverse, cols, spectral_weight, place, halving)
     for level in range(levels):
         got = swap(send, level)
         cut = []
         if level < parts:
             for p in live:
                 pairs = [(i, i + 1) for i in range(p, gy_size - 1, 2)]
-                cut.append(cut_edge(features, edge_rows, variant, p, level, parts, send))
+                cut.append(cut_edge(edge[live.index(p)], level, parts, send))
                 halos[level].append(
                     lax.ppermute(cut[-1], "gy", pairs + [(b, a) for a, b in pairs])
                 )
@@ -452,7 +452,7 @@
     for part in range(parts):
         items = jnp.array([list(zip(*calls[part])) for calls in every], jnp.int32)
         out = rows_of(
-            out, features, inv, items, variant, conv_taps, dense, mixed, halos[part], xb, 512 if part == 0 else 256
+            out, features, inv, items, place, conv_taps, dense, mixed, halos[part], xb, 512
         )
     return out
 

time: 69.2 us -> 67.2 us (0.971)
  Pallas kernels: 35.3 us -> 33.5 us
  local copies, waits for them, and re-layouts: 4.12 us -> 3.42 us
    pallas_call x4, Pallas kernels: 5.1 us -> 3.54 us  [the longest x1 2.67 us: forward_transform(): pl.pallas_call(functools.partial(forward_kernel, live), in_specs=[smem, v...]
    unnamed x24 -> x22, local copies, waits for them, and re-layouts: 4.12 us -> 3.42 us
  transfers between devices with their start and end apart: 9 -> 9, of which waited for: 6 -> 6; matrix products, arithmetic and copies ran while one was open for 0% -> 0% of each run, Pallas kernels for 38% -> 37%
where the time goes in v3:
time: 67.2 us; the launch traced here: 67.1 us
  Pallas kernels  33.5 us (50%)
  waiting for transfers between devices  15.9 us (24%)
  starting transfers between devices  13.6 us (20%)
  local copies, waits for them, and re-layouts  3.42 us (5%)
    pallas_call x2, Pallas kernels, rows_of(): pl.pallas_call(functools.partial(row_kernel, len(halos), min(sub, tokens)...  28.9 us
    ppermute x7, waiting for transfers between devices, local(): lax.ppermute(a, 'gx', [(i, i ^ 1 << level) for i in range(gx_size)])  15.9 us
    ppermute x7, starting transfers between devices, local(): lax.ppermute(a, 'gx', [(i, i ^ 1 << level) for i in range(gx_size)])  9.64 us
    ppermute x2, starting transfers between devices, local(): lax.ppermute(cut[-1], 'gy', pairs + [(b, a) for a, b in pairs])  4 us
    unnamed x22, local copies, waits for them, and re-layouts  3.42 us
    pallas_call x1, Pallas kernels, forward_transform(): pl.pallas_call(functools.partial(forward_kernel, live), in_specs=[smem, v...  2.67 us
  transfers between devices with their start and end apart: 9, of which 6 were waited for; matrix products, arithmetic and copies ran while one was open for 0% of the time, Pallas kernels for 37%

profile of v3, /device:TPU:0, one launch (start us, length us, event | category | flops | bytes accessed | tf_op | source)
XLA Modules:
  0.0 67.1 jit_solution(6555762824827548341)
XLA Ops:
  0.0 0.4 multiply_convert_fusion
  0.4 0.7 widen.1.wide_ref
  1.1 0.0 copy-start
  1.1 3.4 %copy-done = bf16[512,4,8,256]{3,2,1,0:T(8,128)(2,1)S(1)} copy-done((bf16[512,4,8,256]{3,2,1,0:T(8,128)(2,1)S(1)}, bf16[512,4,8,256]{3,2,1,0:T(8,128)(2,1)}, u32[]{:S(2)}) %copy-start) | copy-done | bytes 8388632
  4.5 2.7 %forward.1 = (bf16[32,2,8,256]{3,2,1,0:T(8,128)(2,1)S(1)}, f32[32,2,8,256]{3,2,1,0:T(8,128)S(1)}, bf16[512,8,256]{2,1,0:T(8,128)(2,1)S(1)}) custom-call(s32[1]{0:T(128)} %bitcast.place_ref, bf16[256,4096]{1,0:T(8,128)(2,1)S(1)} %widen.1.wide_ref, bf16[512,4,8,256]{3,2,1,0:T(8,128)(2,1)S(1)} %copy-done), custom_call_target="tpu_custom_call" | custom-call | tf_op jit(solution)/shard_map/forward/pallas_call | solution.py:110
  7.2 0.5 collective-permute-start
  7.7 0.1 cut.2.refs_0_
  7.8 2.6 %collective-permute-start.8 = (bf16[256,8,256]{2,1,0:T(8,128)(2,1)S(1)}, bf16[256,8,256]{2,1,0:T(8,128)(2,1)S(1)}, u32[]{:S(2)}, u32[]{:S(2)}) collective-permute-start(bf16[256,8,256]{2,1,0:T(8,128)(2,1)S(1)} %cut.2.refs_0_), channel_id=1, source_target_pairs={{0,1},{1,0},{2,3},{3,2},{4,5},{5,4},{6,7},{7,6},{8,9},{9,8},{10,11... | collective-permute-start | bytes 3145736 | tf_op jit(solution)/shard_map/ppermute | solution.py:420
  10.3 0.0 collective-permute-done.got_ref
  10.4 0.1 cut.3.refs_0_
  10.5 1.4 %collective-permute-start.7 = (bf16[256,8,256]{2,1,0:T(8,128)(2,1)S(1)}, bf16[256,8,256]{2,1,0:T(8,128)(2,1)S(1)}, u32[]{:S(2)}, u32[]{:S(2)}) collective-permute-start(bf16[256,8,256]{2,1,0:T(8,128)(2,1)S(1)} %cut.3.refs_0_), channel_id=1, source_target_pairs={{0,1},{1,0},{2,3},{3,2},{4,5},{5,4},{6,7},{7,6},{8,9},{9,8},{10,11... | collective-permute-start | bytes 3145736 | tf_op jit(solution)/shard_map/ppermute | solution.py:420
  11.9 1.5 %collective-permute-start.1 = (bf16[16,2,8,256]{3,2,1,0:T(8,128)(2,1)S(1)}, bf16[16,2,8,256]{3,2,1,0:T(8,128)(2,1)S(1)}, u32[]{:S(2)}, u32[]{:S(2)}) collective-permute-start(bf16[16,2,8,256]{3,2,1,0:T(8,128)(2,1)S(1)} %get-tuple-element.21.ahead_ref), channel_id=1, source_target_pairs={{0,4},{2,6},{4,0},{6,2},{8,12},{10,14},{12,8},{14,10},{16,20},{18,... | collective-permute-start | bytes 393224 | tf_op jit(solution)/shard_map/ppermute | solution.py:404
  13.4 3.7 %collective-permute-done.1.got_ref = bf16[16,2,8,256]{3,2,1,0:T(8,128)(2,1)S(1)} collective-permute-done((bf16[16,2,8,256]{3,2,1,0:T(8,128)(2,1)S(1)}, bf16[16,2,8,256]{3,2,1,0:T(8,128)(2,1)S(1)}, u32[]{:S(2)}, u32[]{:S(2)}) %collective-permute-start.1) | collective-permute-done | bytes 131104 | tf_op jit(solution)/shard_map/ppermute | solution.py:404
  17.2 0.0 copy-start.6
  17.2 0.0 copy-start.7
  17.2 0.0 copy-start.8
  17.2 1.6 %collective-permute-start.2 = (bf16[8,2,8,256]{3,2,1,0:T(8,128)(2,1)S(1)}, bf16[8,2,8,256]{3,2,1,0:T(8,128)(2,1)S(1)}, u32[]{:S(2)}, u32[]{:S(2)}) collective-permute-start(bf16[8,2,8,256]{3,2,1,0:T(8,128)(2,1)S(1)} %get-tuple-element.23), channel_id=1, source_target_pairs={{0,8},{2,10},{4,12},{6,14},{8,0},{10,2},{12,4},{14,6},{16,24},{18,... | collective-permute-start | bytes 196616 | tf_op jit(solution)/shard_map/ppermute | solution.py:404
  18.9 0.7 %prepare.1 = (bf16[4096,256]{1,0:T(8,128)(2,1)S(1)}, bf16[4,2,256,256]{3,2,1,0:T(8,128)(2,1)S(1)}) custom-call(s32[1]{0:T(128)} %bitcast.place_ref, bf16[32,512]{1,0:T(8,128)(2,1)S(1)} %get-tuple-element.28.table_ref, bf16[16,2,256,256]{3,2,1,0:T(8,128)(2,1)S(1)} %copy-done.1), custom_call_target="tpu_custom_call" | custom-call | tf_op jit(solution)/shard_map/prepare/pallas_call | solution.py:164
  19.6 1.9 %collective-permute-done.2.got_ref = bf16[8,2,8,256]{3,2,1,0:T(8,128)(2,1)S(1)} collective-permute-done((bf16[8,2,8,256]{3,2,1,0:T(8,128)(2,1)S(1)}, bf16[8,2,8,256]{3,2,1,0:T(8,128)(2,1)S(1)}, u32[]{:S(2)}, u32[]{:S(2)}) %collective-permute-start.2) | collective-permute-done | bytes 65568 | tf_op jit(solution)/shard_map/ppermute | solution.py:404
  21.6 2.7 %collective-permute-start.3 = (bf16[8,2,8,256]{3,2,1,0:T(8,128)(2,1)S(1)}, bf16[8,2,8,256]{3,2,1,0:T(8,128)(2,1)S(1)}, u32[]{:S(2)}, u32[]{:S(2)}) collective-permute-start(bf16[8,2,8,256]{3,2,1,0:T(8,128)(2,1)S(1)} %get-tuple-element.26), channel_id=1, source_target_pairs={{0,16},{2,18},{4,20},{6,22},{8,24},{10,26},{12,28},{14,30},{16,0},... | collective-permute-start | bytes 196616 | tf_op jit(solution)/shard_map/ppermute | solution.py:404
  24.3 2.6 %collective-permute-done.3.got_ref = bf16[8,2,8,256]{3,2,1,0:T(8,128)(2,1)S(1)} collective-permute-done((bf16[8,2,8,256]{3,2,1,0:T(8,128)(2,1)S(1)}, bf16[8,2,8,256]{3,2,1,0:T(8,128)(2,1)S(1)}, u32[]{:S(2)}, u32[]{:S(2)}) %collective-permute-start.3) | collective-permute-done | bytes 65568 | tf_op jit(solution)/shard_map/ppermute | solution.py:404
  26.8 0.3 mix.1.mine_ref
  27.1 1.6 %collective-permute-start.4 = (bf16[8,2,8,256]{3,2,1,0:T(8,128)(2,1)S(1)}, bf16[8,2,8,256]{3,2,1,0:T(8,128)(2,1)S(1)}, u32[]{:S(2)}, u32[]{:S(2)}) collective-permute-start(bf16[8,2,8,256]{3,2,1,0:T(8,128)(2,1)S(1)} %mix.1.mine_ref), channel_id=1, source_target_pairs={{0,8},{2,10},{4,12},{6,14},{8,0},{10,2},{12,4},{14,6},{16,24},{18,... | collective-permute-start | bytes 196616 | tf_op jit(solution)/shard_map/ppermute | solution.py:404
  28.8 2.7 %collective-permute-done.4.got_ref = bf16[8,2,8,256]{3,2,1,0:T(8,128)(2,1)S(1)} collective-permute-done((bf16[8,2,8,256]{3,2,1,0:T(8,128)(2,1)S(1)}, bf16[8,2,8,256]{3,2,1,0:T(8,128)(2,1)S(1)}, u32[]{:S(2)}, u32[]{:S(2)}) %collective-permute-start.4) | collective-permute-done | bytes 65568 | tf_op jit(solution)/shard_map/ppermute | solution.py:404
  31.5 1.6 %collective-permute-start.5 = (bf16[16,2,8,256]{3,2,1,0:T(8,128)(2,1)S(1)}, bf16[16,2,8,256]{3,2,1,0:T(8,128)(2,1)S(1)}, u32[]{:S(2)}, u32[]{:S(2)}) collective-permute-start(bf16[16,2,8,256]{3,2,1,0:T(8,128)(2,1)S(1)} %join.1.refs_0_), channel_id=1, source_target_pairs={{0,4},{2,6},{4,0},{6,2},{8,12},{10,14},{12,8},{14,10},{16,20},{18,... | collective-permute-start | bytes 393224 | tf_op jit(solution)/shard_map/ppermute | solution.py:404
  33.1 3.4 %collective-permute-done.5.refs_1_ = bf16[16,2,8,256]{3,2,1,0:T(8,128)(2,1)S(1)} collective-permute-done((bf16[16,2,8,256]{3,2,1,0:T(8,128)(2,1)S(1)}, bf16[16,2,8,256]{3,2,1,0:T(8,128)(2,1)S(1)}, u32[]{:S(2)}, u32[]{:S(2)}) %collective-permute-start.5) | collective-permute-done | bytes 131104 | tf_op jit(solution)/shard_map/ppermute | solution.py:404
  36.5 0.1 collective-permute-start.6
  36.6 1.5 %collective-permute-done.6.other_ref = bf16[2,256,256]{2,1,0:T(8,128)(2,1)S(1)} collective-permute-done((bf16[2,256,256]{2,1,0:T(8,128)(2,1)S(1)}, bf16[2,256,256]{2,1,0:T(8,128)(2,1)S(1)}, u32[]{:S(2)}, u32[]{:S(2)}) %collective-permute-start.6) | collective-permute-done | bytes 262176 | tf_op jit(solution)/shard_map/ppermute | solution.py:404
  38.1 0.0 collective-permute-done.8.rest_0_
  38.2 0.0 copy-start.4
  38.2 23.7 %rows.2.rest_1_ = bf16[512,4,8,256]{3,2,1,0:T(8,128)(2,1)} custom-call(s32[4,9,7]{2,1,0:T(8,128)S(1)} %copy-done.5, s32[1]{0:T(128)} %bitcast.place_ref, bf16[512,4,8,256]{3,2,1,0:T(8,128)(2,1)S(1)} %bitcast.4, bf16[4096,256]{1,0:T(8,128)(2,1)S(1)} %get-tuple-element.16.inv_ref, f32[3,256]{1,0:T(4,128)S(1)} %copy-done.6, bf16[256,1024]{1,0:T(8,128)(2,1)S(1)} %copy-done.2, ...), custom_call_target="tpu_custom_call" | custom-call | tf_op jit(solution)/shard_map/rows/pallas_call | solution.py:364
  62.0 5.1 %rows.3 = bf16[512,4,8,256]{3,2,1,0:T(8,128)(2,1)} custom-call(s32[4,9,1]{2,1,0:T(8,128)S(1)} %copy-done.4, s32[1]{0:T(128)} %bitcast.place_ref, bf16[512,4,8,256]{3,2,1,0:T(8,128)(2,1)S(1)} %bitcast.4, bf16[4096,256]{1,0:T(8,128)(2,1)S(1)} %get-tuple-element.16.inv_ref, f32[3,256]{1,0:T(4,128)S(1)} %copy-done.6, ...), custom_call_target="tpu_custom_call", output_to_operand_aliasing={{}: (12, {})} | custom-call | tf_op jit(solution)/shard_map/rows/pallas_call | solution.py:364
  (27 shorter events, 0.2 us)
Async XLA Ops:
  1.1 3.4 %copy-start = (bf16[512,4,8,256]{3,2,1,0:T(8,128)(2,1)S(1)}, bf16[512,4,8,256]{3,2,1,0:T(8,128)(2,1)}, u32[]{:S(2)}) copy-start(bf16[512,4,8,256]{3,2,1,0:T(8,128)(2,1)} %field_ref.5) | copy-start | bytes 25165828
  7.2 3.2 %collective-permute-start = (bf16[32,2,8,256]{3,2,1,0:T(8,128)(2,1)S(1)}, bf16[32,2,8,256]{3,2,1,0:T(8,128)(2,1)S(1)}, u32[]{:S(2)}, u32[]{:S(2)}) collective-permute-start(bf16[32,2,8,256]{3,2,1,0:T(8,128)(2,1)S(1)} %get-tuple-element.18.ahead_ref), channel_id=1, source_target_pairs={{0,2},{2,0},{4,6},{6,4},{8,10},{10,8},{12,14},{14,12},{16,18},{18,... | collective-permute-start | bytes 786440 | tf_op jit(solution)/shard_map/ppermute | solution.py:404
  7.7 11.2 %copy-start.1 = (bf16[16,2,256,256]{3,2,1,0:T(8,128)(2,1)S(1)}, bf16[16,2,256,256]{3,2,1,0:T(8,128)(2,1)}, u32[]{:S(2)}) copy-start(bf16[16,2,256,256]{3,2,1,0:T(8,128)(2,1)} %weight_ref.1) | copy-start | bytes 12582916
  7.7 30.4 %slice-start = ((s8[8388608]{0:T(1024)(128)(4,1)}), s8[4194304]{0:T(1024)(128)(4,1)S(1)}, s32[]{:S(2)}) async-start(s8[8388608]{0:T(1024)(128)(4,1)} %bitcast.3), calls=%async_computation | async-start | bytes 8388608
  7.8 30.4 %collective-permute-start.8 = (bf16[256,8,256]{2,1,0:T(8,128)(2,1)S(1)}, bf16[256,8,256]{2,1,0:T(8,128)(2,1)S(1)}, u32[]{:S(2)}, u32[]{:S(2)}) collective-permute-start(bf16[256,8,256]{2,1,0:T(8,128)(2,1)S(1)} %cut.2.refs_0_), channel_id=1, source_target_pairs={{0,1},{1,0},{2,3},{3,2},{4,5},{5,4},{6,7},{7,6},{8,9},{9,8},{10,11... | collective-permute-start | bytes 3145736 | tf_op jit(solution)/shard_map/ppermute | solution.py:420
  10.5 51.5 %collective-permute-start.7 = (bf16[256,8,256]{2,1,0:T(8,128)(2,1)S(1)}, bf16[256,8,256]{2,1,0:T(8,128)(2,1)S(1)}, u32[]{:S(2)}, u32[]{:S(2)}) collective-permute-start(bf16[256,8,256]{2,1,0:T(8,128)(2,1)S(1)} %cut.3.refs_0_), channel_id=1, source_target_pairs={{0,1},{1,0},{2,3},{3,2},{4,5},{5,4},{6,7},{7,6},{8,9},{9,8},{10,11... | collective-permute-start | bytes 3145736 | tf_op jit(solution)/shard_map/ppermute | solution.py:420
  11.9 5.3 %collective-permute-start.1 = (bf16[16,2,8,256]{3,2,1,0:T(8,128)(2,1)S(1)}, bf16[16,2,8,256]{3,2,1,0:T(8,128)(2,1)S(1)}, u32[]{:S(2)}, u32[]{:S(2)}) collective-permute-start(bf16[16,2,8,256]{3,2,1,0:T(8,128)(2,1)S(1)} %get-tuple-element.21.ahead_ref), channel_id=1, source_target_pairs={{0,4},{2,6},{4,0},{6,2},{8,12},{10,14},{12,8},{14,10},{16,20},{18,... | collective-permute-start | bytes 393224 | tf_op jit(solution)/shard_map/ppermute | solution.py:404
  17.2 21.0 %slice-start.1 = ((s8[8388608]{0:T(1024)(128)(4,1)}), s8[4194304]{0:T(1024)(128)(4,1)S(1)}, s32[]{:S(2)}) async-start(s8[8388608]{0:T(1024)(128)(4,1)} %bitcast.3), calls=%async_computation.1 | async-start | bytes 8388608
  17.2 21.0 %copy-start.2 = (bf16[256,1024]{1,0:T(8,128)(2,1)S(1)}, bf16[256,1024]{1,0:T(8,128)(2,1)}, u32[]{:S(2)}) copy-start(bf16[256,1024]{1,0:T(8,128)(2,1)} %w_in_ref.3) | copy-start | bytes 1572868
  17.2 21.0 %copy-start.3 = (bf16[1024,256]{1,0:T(8,128)(2,1)S(1)}, bf16[1024,256]{1,0:T(8,128)(2,1)}, u32[]{:S(2)}) copy-start(bf16[1024,256]{1,0:T(8,128)(2,1)} %w_out_ref.3) | copy-start | bytes 1572868
  17.2 21.0 %copy-start.5 = (s32[4,9,7]{2,1,0:T(8,128)S(1)}, s32[4,9,7]{2,1,0:T(8,128)}, u32[]{:S(2)}) copy-start(s32[4,9,7]{2,1,0:T(8,128)} %constant.76.clone.items_ref) | copy-start | bytes 3028
  17.2 21.0 %copy-start.6 = (f32[3,256]{1,0:T(4,128)S(1)}, f32[3,256]{1,0:T(4,128)}, u32[]{:S(2)}) copy-start(f32[3,256]{1,0:T(4,128)} %taps_ref.3) | copy-start | bytes 9220
  17.2 21.0 %copy-start.7 = (f32[1024]{0:T(1024)S(1)}, f32[1024]{0:T(1024)}, u32[]{:S(2)}) copy-start(f32[1024]{0:T(1024)} %param.13) | copy-start | bytes 12292
  17.2 21.0 %copy-start.8 = (f32[256]{0:T(256)S(1)}, f32[256]{0:T(256)}, u32[]{:S(2)}) copy-start(f32[256]{0:T(256)} %param.15) | copy-start | bytes 3076
  17.2 4.3 %collective-permute-start.2 = (bf16[8,2,8,256]{3,2,1,0:T(8,128)(2,1)S(1)}, bf16[8,2,8,256]{3,2,1,0:T(8,128)(2,1)S(1)}, u32[]{:S(2)}, u32[]{:S(2)}) collective-permute-start(bf16[8,2,8,256]{3,2,1,0:T(8,128)(2,1)S(1)} %get-tuple-element.23), channel_id=1, source_target_pairs={{0,8},{2,10},{4,12},{6,14},{8,0},{10,2},{12,4},{14,6},{16,24},{18,... | collective-permute-start | bytes 196616 | tf_op jit(solution)/shard_map/ppermute | solution.py:404
  21.6 5.2 %collective-permute-start.3 = (bf16[8,2,8,256]{3,2,1,0:T(8,128)(2,1)S(1)}, bf16[8,2,8,256]{3,2,1,0:T(8,128)(2,1)S(1)}, u32[]{:S(2)}, u32[]{:S(2)}) collective-permute-start(bf16[8,2,8,256]{3,2,1,0:T(8,128)(2,1)S(1)} %get-tuple-element.26), channel_id=1, source_target_pairs={{0,16},{2,18},{4,20},{6,22},{8,24},{10,26},{12,28},{14,30},{16,0},... | collective-permute-start | bytes 196616 | tf_op jit(solution)/shard_map/ppermute | solution.py:404
  27.1 4.3 %collective-permute-start.4 = (bf16[8,2,8,256]{3,2,1,0:T(8,128)(2,1)S(1)}, bf16[8,2,8,256]{3,2,1,0:T(8,128)(2,1)S(1)}, u32[]{:S(2)}, u32[]{:S(2)}) collective-permute-start(bf16[8,2,8,256]{3,2,1,0:T(8,128)(2,1)S(1)} %mix.1.mine_ref), channel_id=1, source_target_pairs={{0,8},{2,10},{4,12},{6,14},{8,0},{10,2},{12,4},{14,6},{16,24},{18,... | collective-permute-start | bytes 196616 | tf_op jit(solution)/shard_map/ppermute | solution.py:404
  31.5 5.0 %collective-permute-start.5 = (bf16[16,2,8,256]{3,2,1,0:T(8,128)(2,1)S(1)}, bf16[16,2,8,256]{3,2,1,0:T(8,128)(2,1)S(1)}, u32[]{:S(2)}, u32[]{:S(2)}) collective-permute-start(bf16[16,2,8,256]{3,2,1,0:T(8,128)(2,1)S(1)} %join.1.refs_0_), channel_id=1, source_target_pairs={{0,4},{2,6},{4,0},{6,2},{8,12},{10,14},{12,8},{14,10},{16,20},{18,... | collective-permute-start | bytes 393224 | tf_op jit(solution)/shard_map/ppermute | solution.py:404
  36.5 1.6 %collective-permute-start.6 = (bf16[2,256,256]{2,1,0:T(8,128)(2,1)S(1)}, bf16[2,256,256]{2,1,0:T(8,128)(2,1)S(1)}, u32[]{:S(2)}, u32[]{:S(2)}) collective-permute-start(bf16[2,256,256]{2,1,0:T(8,128)(2,1)S(1)} %stack.1.mine_ref), channel_id=1, source_target_pairs={{0,2},{2,0},{4,6},{6,4},{8,10},{10,8},{12,14},{14,12},{16,18},{18,... | collective-permute-start | bytes 786440 | tf_op jit(solution)/shard_map/ppermute | solution.py:404
  38.2 23.8 %copy-start.4 = (s32[4,9,1]{2,1,0:T(8,128)S(1)}, s32[4,9,1]{2,1,0:T(8,128)}, u32[]{:S(2)}) copy-start(s32[4,9,1]{2,1,0:T(8,128)} %constant.77.clone.items_ref) | copy-start | bytes 436

commit v4 on v3

--- a/solution.py
+++ b/solution.py
@@ -121,20 +121,19 @@
     )(place, wide, features)
 
 
-def cut_kernel(start, edge_ref, ahead_ref, cut_ref):
-    cut_ref[...] = edge_ref[start : start + cut_ref.shape[0]]
-
-
-def cut_edge(edge, part, parts, ahead):
-    count = edge.shape[0] // parts
+def hold_kernel(edge_ref, ahead_ref, out_ref):
+    out_ref[...] = edge_ref[...]
+
+
+def hold(edge, ahead):
     vmem = pl.BlockSpec(memory_space=pltpu.VMEM)
     return pl.pallas_call(
-        functools.partial(cut_kernel, part * count),
+        hold_kernel,
         in_specs=[vmem, pl.BlockSpec(memory_space=pl.ANY)],
         out_specs=vmem,
-        out_shape=jax.ShapeDtypeStruct((count,) + edge.shape[1:], BF16),
-        compiler_params=pltpu.CompilerParams(vmem_limit_bytes=SMALL_BYTES),
-        name="cut",
+        out_shape=jax.ShapeDtypeStruct(edge.shape, BF16),
+        compiler_params=pltpu.CompilerParams(vmem_limit_bytes=SMALL_BYTES),
+        name="hold",
     )(edge, ahead)
 
 
@@ -307,7 +306,7 @@
     def load_after(s):
         part = load(after, s)
         for at, ref in enumerate(halo_refs):
-            halo = ref[s * sub // cols : (s + 1) * sub // cols].reshape(sub, channels)
+            halo = ref[pl.ds(start + s * sub // cols, sub // cols)].reshape(sub, channels)
             part = jnp.where(source == at + 1, halo, part)
         return part
 
@@ -379,6 +378,11 @@
         out_shape=jax.ShapeDtypeStruct(field.shape, BF16),
         input_output_aliases=aliases,
         compiler_params=pltpu.CompilerParams(vmem_limit_bytes=ROWS_BYTES),
+        cost_estimate=pl.CostEstimate(
+            flops=2 * count * tokens * channels * (2 * hidden + waves_cols),
+            bytes_accessed=2 * count * tokens * channels,
+            transcendentals=count * tokens * hidden,
+        ),
         name="rows",
     )(*args)
 
@@ -406,21 +410,19 @@
     )
     parts = half_rows
     xb = x_rows // parts
-    halos = [[] for _ in range(parts)]
+    halos = []
     send, keep, *edge = forward_transform(features, widen(table, cols), place, live)
     inv, weight = prepare(inverse, cols, spectral_weight, place, halving)
     for level in range(levels):
         got = swap(send, level)
-        cut = []
-        if level < parts:
-            for p in live:
+        ahead = []
+        if level == 0:
+            for p, row in zip(live, edge):
                 pairs = [(i, i + 1) for i in range(p, gy_size - 1, 2)]
-                cut.append(cut_edge(edge[live.index(p)], level, parts, send))
-                halos[level].append(
-                    lax.ppermute(cut[-1], "gy", pairs + [(b, a) for a, b in pairs])
-                )
+                ahead.append(hold(row, send))
+                halos.append(lax.ppermute(ahead[-1], "gy", pairs + [(b, a) for a, b in pairs]))
         if level + 1 < levels:
-            ahead = cut + ([weight] if level == levels - 2 else [])
+            ahead += [weight] if level == levels - 2 else []
             send, keep = combine(keep, got, level + 1 < halving, ahead)
     mixed = mix(keep, got, weight)
     for level in reversed(range(2, halving)):
@@ -433,7 +435,7 @@
         return before, here, after, part, here % half_rows, group, halo, flip, drop
 
     def calls_of(odd, core):
-        calls = [[] for _ in range(parts)]
+        calls = [[], []]
         for row in range(1, y_rows - 1):
             for part in range(parts):
                 calls[0].append(block_of(core, row - 1, row, row + 1, part))
@@ -441,7 +443,7 @@
             inner, flip = (1, 1) if edge == 0 else (y_rows - 2, 0)
             for part in range(parts):
                 halo = live.index(p) + 1 if p in live else 0
-                calls[part if halo else 0].append(
+                calls[1 if halo else 0].append(
                     block_of(core, inner, edge, edge, part, halo, flip, 0 if halo else 1)
                 )
         return calls
@@ -449,10 +451,10 @@
     every = [calls_of(odd, core) for odd, core in variants]
     dense = (w_in, bias_in[None], w_out, bias_out[None])
     out = None
-    for part in range(parts):
-        items = jnp.array([list(zip(*calls[part])) for calls in every], jnp.int32)
+    for call in range(2 if live else 1):
+        items = jnp.array([list(zip(*calls[call])) for calls in every], jnp.int32)
         out = rows_of(
-            out, features, inv, items, place, conv_taps, dense, mixed, halos[part], xb, 512
+            out, features, inv, items, place, conv_taps, dense, mixed, halos if call else [], xb, 512
         )
     return out
 

time: 67.2 us -> 66 us (0.982)
  starting transfers between devices: 13.6 us -> 12.3 us
    ppermute x2 -> x1, starting transfers between devices: 4 us -> 2.59 us  [local(): lax.ppermute(ahead[-1], 'gy', pairs + [(b, a) for a, b in pairs])]
  transfers between devices with their start and end apart: 9 -> 8, of which waited for: 6 -> 6; matrix products, arithmetic and copies ran while one was open for 0% -> 0% of each run, Pallas kernels for 37% -> 33%
where the time goes in v4:
time: 66 us; the launch traced here: 65.8 us
  Pallas kernels  33.3 us (50%)
  waiting for transfers between devices  16.2 us (25%)
  starting transfers between devices  12.3 us (19%)
  local copies, waits for them, and re-layouts  3.43 us (5%)
    pallas_call x2, Pallas kernels, rows_of(): pl.pallas_call(functools.partial(row_kernel, len(halos), min(sub, tokens)...  28.7 us
    ppermute x7, waiting for transfers between devices, local(): lax.ppermute(a, 'gx', [(i, i ^ 1 << level) for i in range(gx_size)])  16.2 us
    ppermute x7, starting transfers between devices, local(): lax.ppermute(a, 'gx', [(i, i ^ 1 << level) for i in range(gx_size)])  9.71 us
    unnamed x22, local copies, waits for them, and re-layouts  3.43 us
    pallas_call x1, Pallas kernels, forward_transform(): pl.pallas_call(functools.partial(forward_kernel, live), in_specs=[smem, v...  2.67 us
    ppermute x1, starting transfers between devices, local(): lax.ppermute(ahead[-1], 'gy', pairs + [(b, a) for a, b in pairs])  2.59 us
  transfers between devices with their start and end apart: 8, of which 6 were waited for; matrix products, arithmetic and copies ran while one was open for 0% of the time, Pallas kernels for 33%

profile of v4, /device:TPU:0, one launch (start us, length us, event | category | flops | bytes accessed | tf_op | source)
XLA Modules:
  0.0 65.8 jit_solution(3372598707382437600)
XLA Ops:
  0.0 0.4 multiply_convert_fusion
  0.4 0.7 %widen.1.wide_ref = bf16[256,4096]{1,0:T(8,128)(2,1)S(1)} custom-call(bf16[32,512]{1,0:T(8,128)(2,1)S(1)} %get-tuple-element.27.table_ref), custom_call_target="tpu_custom_call" | custom-call | flops 5000000000 | bytes 4194304 | tf_op jit(solution)/shard_map/widen/pallas_call | solution.py:74
  1.1 0.0 copy-start
  1.1 3.4 %copy-done = bf16[512,4,8,256]{3,2,1,0:T(8,128)(2,1)S(1)} copy-done((bf16[512,4,8,256]{3,2,1,0:T(8,128)(2,1)S(1)}, bf16[512,4,8,256]{3,2,1,0:T(8,128)(2,1)}, u32[]{:S(2)}) %copy-start) | copy-done | bytes 8388632
  4.5 2.7 %forward.1 = (bf16[32,2,8,256]{3,2,1,0:T(8,128)(2,1)S(1)}, f32[32,2,8,256]{3,2,1,0:T(8,128)S(1)}, bf16[512,8,256]{2,1,0:T(8,128)(2,1)S(1)}) custom-call(s32[1]{0:T(128)} %bitcast.place_ref, bf16[256,4096]{1,0:T(8,128)(2,1)S(1)} %widen.1.wide_ref, bf16[512,4,8,256]{3,2,1,0:T(8,128)(2,1)S(1)} %copy-done), custom_call_target="tpu_custom_call" | custom-call | tf_op jit(solution)/shard_map/forward/pallas_call | solution.py:110
  7.2 0.5 collective-permute-start
  7.7 0.1 hold.1.refs_0_
  7.8 2.6 %collective-permute-start.7 = (bf16[512,8,256]{2,1,0:T(8,128)(2,1)S(1)}, bf16[512,8,256]{2,1,0:T(8,128)(2,1)S(1)}, u32[]{:S(2)}, u32[]{:S(2)}) collective-permute-start(bf16[512,8,256]{2,1,0:T(8,128)(2,1)S(1)} %hold.1.refs_0_), channel_id=1, source_target_pairs={{0,1},{1,0},{2,3},{3,2},{4,5},{5,4},{6,7},{7,6},{8,9},{9,8},{10,11... | collective-permute-start | bytes 6291464 | tf_op jit(solution)/shard_map/ppermute | solution.py:423
  10.4 0.0 collective-permute-done.got_ref
  10.5 1.6 %collective-permute-start.1 = (bf16[16,2,8,256]{3,2,1,0:T(8,128)(2,1)S(1)}, bf16[16,2,8,256]{3,2,1,0:T(8,128)(2,1)S(1)}, u32[]{:S(2)}, u32[]{:S(2)}) collective-permute-start(bf16[16,2,8,256]{3,2,1,0:T(8,128)(2,1)S(1)} %get-tuple-element.21), channel_id=1, source_target_pairs={{0,4},{2,6},{4,0},{6,2},{8,12},{10,14},{12,8},{14,10},{16,20},{18,... | collective-permute-start | bytes 393224 | tf_op jit(solution)/shard_map/ppermute | solution.py:408
  12.1 4.1 %collective-permute-done.1.got_ref = bf16[16,2,8,256]{3,2,1,0:T(8,128)(2,1)S(1)} collective-permute-done((bf16[16,2,8,256]{3,2,1,0:T(8,128)(2,1)S(1)}, bf16[16,2,8,256]{3,2,1,0:T(8,128)(2,1)S(1)}, u32[]{:S(2)}, u32[]{:S(2)}) %collective-permute-start.1) | collective-permute-done | bytes 131104 | tf_op jit(solution)/shard_map/ppermute | solution.py:408
  16.2 1.6 %collective-permute-start.2 = (bf16[8,2,8,256]{3,2,1,0:T(8,128)(2,1)S(1)}, bf16[8,2,8,256]{3,2,1,0:T(8,128)(2,1)S(1)}, u32[]{:S(2)}, u32[]{:S(2)}) collective-permute-start(bf16[8,2,8,256]{3,2,1,0:T(8,128)(2,1)S(1)} %get-tuple-element.23), channel_id=1, source_target_pairs={{0,8},{2,10},{4,12},{6,14},{8,0},{10,2},{12,4},{14,6},{16,24},{18,... | collective-permute-start | bytes 196616 | tf_op jit(solution)/shard_map/ppermute | solution.py:408
  17.8 0.7 %prepare.1 = (bf16[4096,256]{1,0:T(8,128)(2,1)S(1)}, bf16[4,2,256,256]{3,2,1,0:T(8,128)(2,1)S(1)}) custom-call(s32[1]{0:T(128)} %bitcast.place_ref, bf16[32,512]{1,0:T(8,128)(2,1)S(1)} %get-tuple-element.28.table_ref, bf16[16,2,256,256]{3,2,1,0:T(8,128)(2,1)S(1)} %copy-done.1), custom_call_target="tpu_custom_call" | custom-call | tf_op jit(solution)/shard_map/prepare/pallas_call | solution.py:163
  18.5 0.0 copy-start.2
  18.6 0.0 copy-start.3
  18.6 0.0 copy-start.5
  18.6 0.0 copy-start.6
  18.6 0.0 copy-start.7
  18.6 0.0 copy-start.8
  18.6 1.9 %collective-permute-done.2.got_ref = bf16[8,2,8,256]{3,2,1,0:T(8,128)(2,1)S(1)} collective-permute-done((bf16[8,2,8,256]{3,2,1,0:T(8,128)(2,1)S(1)}, bf16[8,2,8,256]{3,2,1,0:T(8,128)(2,1)S(1)}, u32[]{:S(2)}, u32[]{:S(2)}) %collective-permute-start.2) | collective-permute-done | bytes 65568 | tf_op jit(solution)/shard_map/ppermute | solution.py:408
  20.5 2.7 %collective-permute-start.3 = (bf16[8,2,8,256]{3,2,1,0:T(8,128)(2,1)S(1)}, bf16[8,2,8,256]{3,2,1,0:T(8,128)(2,1)S(1)}, u32[]{:S(2)}, u32[]{:S(2)}) collective-permute-start(bf16[8,2,8,256]{3,2,1,0:T(8,128)(2,1)S(1)} %get-tuple-element.26), channel_id=1, source_target_pairs={{0,16},{2,18},{4,20},{6,22},{8,24},{10,26},{12,28},{14,30},{16,0},... | collective-permute-start | bytes 196616 | tf_op jit(solution)/shard_map/ppermute | solution.py:408
  23.2 2.6 %collective-permute-done.3.got_ref = bf16[8,2,8,256]{3,2,1,0:T(8,128)(2,1)S(1)} collective-permute-done((bf16[8,2,8,256]{3,2,1,0:T(8,128)(2,1)S(1)}, bf16[8,2,8,256]{3,2,1,0:T(8,128)(2,1)S(1)}, u32[]{:S(2)}, u32[]{:S(2)}) %collective-permute-start.3) | collective-permute-done | bytes 65568 | tf_op jit(solution)/shard_map/ppermute | solution.py:408
  25.7 0.3 mix.1.mine_ref
  26.0 1.6 %collective-permute-start.4 = (bf16[8,2,8,256]{3,2,1,0:T(8,128)(2,1)S(1)}, bf16[8,2,8,256]{3,2,1,0:T(8,128)(2,1)S(1)}, u32[]{:S(2)}, u32[]{:S(2)}) collective-permute-start(bf16[8,2,8,256]{3,2,1,0:T(8,128)(2,1)S(1)} %mix.1.mine_ref), channel_id=1, source_target_pairs={{0,8},{2,10},{4,12},{6,14},{8,0},{10,2},{12,4},{14,6},{16,24},{18,... | collective-permute-start | bytes 196616 | tf_op jit(solution)/shard_map/ppermute | solution.py:408
  27.7 2.7 %collective-permute-done.4.got_ref = bf16[8,2,8,256]{3,2,1,0:T(8,128)(2,1)S(1)} collective-permute-done((bf16[8,2,8,256]{3,2,1,0:T(8,128)(2,1)S(1)}, bf16[8,2,8,256]{3,2,1,0:T(8,128)(2,1)S(1)}, u32[]{:S(2)}, u32[]{:S(2)}) %collective-permute-start.4) | collective-permute-done | bytes 65568 | tf_op jit(solution)/shard_map/ppermute | solution.py:408
  30.4 1.6 %collective-permute-start.5 = (bf16[16,2,8,256]{3,2,1,0:T(8,128)(2,1)S(1)}, bf16[16,2,8,256]{3,2,1,0:T(8,128)(2,1)S(1)}, u32[]{:S(2)}, u32[]{:S(2)}) collective-permute-start(bf16[16,2,8,256]{3,2,1,0:T(8,128)(2,1)S(1)} %join.1.refs_0_), channel_id=1, source_target_pairs={{0,4},{2,6},{4,0},{6,2},{8,12},{10,14},{12,8},{14,10},{16,20},{18,... | collective-permute-start | bytes 393224 | tf_op jit(solution)/shard_map/ppermute | solution.py:408
  32.0 3.4 %collective-permute-done.5.refs_1_ = bf16[16,2,8,256]{3,2,1,0:T(8,128)(2,1)S(1)} collective-permute-done((bf16[16,2,8,256]{3,2,1,0:T(8,128)(2,1)S(1)}, bf16[16,2,8,256]{3,2,1,0:T(8,128)(2,1)S(1)}, u32[]{:S(2)}, u32[]{:S(2)}) %collective-permute-start.5) | collective-permute-done | bytes 131104 | tf_op jit(solution)/shard_map/ppermute | solution.py:408
  35.4 0.1 collective-permute-start.6
  35.5 1.5 %collective-permute-done.6.other_ref = bf16[2,256,256]{2,1,0:T(8,128)(2,1)S(1)} collective-permute-done((bf16[2,256,256]{2,1,0:T(8,128)(2,1)S(1)}, bf16[2,256,256]{2,1,0:T(8,128)(2,1)S(1)}, u32[]{:S(2)}, u32[]{:S(2)}) %collective-permute-start.6) | collective-permute-done | bytes 262176 | tf_op jit(solution)/shard_map/ppermute | solution.py:408
  37.1 0.0 copy-start.4
  37.1 20.4 %rows.2.rest_1_ = bf16[512,4,8,256]{3,2,1,0:T(8,128)(2,1)} custom-call(s32[4,9,6]{2,1,0:T(8,128)S(1)} %copy-done.8, s32[1]{0:T(128)} %bitcast.place_ref, bf16[512,4,8,256]{3,2,1,0:T(8,128)(2,1)S(1)} %bitcast.4, bf16[4096,256]{1,0:T(8,128)(2,1)S(1)} %get-tuple-element.16.inv_ref, f32[3,256]{1,0:T(4,128)S(1)} %copy-done.5, bf16[256,1024]{1,0:T(8,128)(2,1)S(1)} %copy-done.2, ...), custom_call_target="tpu_custom_call" | custom-call | flops 14495514624 | bytes 6291456 | tf_op jit(solution)/shard_map/rows/pallas_call | solution.py:363
  57.5 8.3 %rows.3 = bf16[512,4,8,256]{3,2,1,0:T(8,128)(2,1)} custom-call(s32[4,9,2]{2,1,0:T(8,128)S(1)} %copy-done.4, s32[1]{0:T(128)} %bitcast.place_ref, bf16[512,4,8,256]{3,2,1,0:T(8,128)(2,1)S(1)} %bitcast.4, bf16[4096,256]{1,0:T(8,128)(2,1)S(1)} %get-tuple-element.16.inv_ref, f32[3,256]{1,0:T(4,128)S(1)} %copy-done.5, ...), custom_call_target="tpu_custom_call", output_to_operand_aliasing={{}: (12, {})} | custom-call | flops 4831838208 | bytes 2097152 | tf_op jit(solution)/shard_map/rows/pallas_call | solution.py:363
  (24 shorter events, 0.2 us)
Async XLA Ops:
  1.1 3.4 %copy-start = (bf16[512,4,8,256]{3,2,1,0:T(8,128)(2,1)S(1)}, bf16[512,4,8,256]{3,2,1,0:T(8,128)(2,1)}, u32[]{:S(2)}) copy-start(bf16[512,4,8,256]{3,2,1,0:T(8,128)(2,1)} %field_ref.5) | copy-start | bytes 25165828
  7.2 3.3 %collective-permute-start = (bf16[32,2,8,256]{3,2,1,0:T(8,128)(2,1)S(1)}, bf16[32,2,8,256]{3,2,1,0:T(8,128)(2,1)S(1)}, u32[]{:S(2)}, u32[]{:S(2)}) collective-permute-start(bf16[32,2,8,256]{3,2,1,0:T(8,128)(2,1)S(1)} %get-tuple-element.18.ahead_ref), channel_id=1, source_target_pairs={{0,2},{2,0},{4,6},{6,4},{8,10},{10,8},{12,14},{14,12},{16,18},{18,... | collective-permute-start | bytes 786440 | tf_op jit(solution)/shard_map/ppermute | solution.py:408
  7.7 10.1 %copy-start.1 = (bf16[16,2,256,256]{3,2,1,0:T(8,128)(2,1)S(1)}, bf16[16,2,256,256]{3,2,1,0:T(8,128)(2,1)}, u32[]{:S(2)}) copy-start(bf16[16,2,256,256]{3,2,1,0:T(8,128)(2,1)} %weight_ref.1) | copy-start | bytes 12582916
  7.7 29.3 %slice-start = ((s8[8388608]{0:T(1024)(128)(4,1)}), s8[4194304]{0:T(1024)(128)(4,1)S(1)}, s32[]{:S(2)}) async-start(s8[8388608]{0:T(1024)(128)(4,1)} %bitcast.3), calls=%async_computation | async-start | bytes 8388608
  7.8 49.7 %collective-permute-start.7 = (bf16[512,8,256]{2,1,0:T(8,128)(2,1)S(1)}, bf16[512,8,256]{2,1,0:T(8,128)(2,1)S(1)}, u32[]{:S(2)}, u32[]{:S(2)}) collective-permute-start(bf16[512,8,256]{2,1,0:T(8,128)(2,1)S(1)} %hold.1.refs_0_), channel_id=1, source_target_pairs={{0,1},{1,0},{2,3},{3,2},{4,5},{5,4},{6,7},{7,6},{8,9},{9,8},{10,11... | collective-permute-start | bytes 6291464 | tf_op jit(solution)/shard_map/ppermute | solution.py:423
  10.5 5.7 %collective-permute-start.1 = (bf16[16,2,8,256]{3,2,1,0:T(8,128)(2,1)S(1)}, bf16[16,2,8,256]{3,2,1,0:T(8,128)(2,1)S(1)}, u32[]{:S(2)}, u32[]{:S(2)}) collective-permute-start(bf16[16,2,8,256]{3,2,1,0:T(8,128)(2,1)S(1)} %get-tuple-element.21), channel_id=1, source_target_pairs={{0,4},{2,6},{4,0},{6,2},{8,12},{10,14},{12,8},{14,10},{16,20},{18,... | collective-permute-start | bytes 393224 | tf_op jit(solution)/shard_map/ppermute | solution.py:408
  16.1 20.9 %slice-start.1 = ((s8[8388608]{0:T(1024)(128)(4,1)}), s8[4194304]{0:T(1024)(128)(4,1)S(1)}, s32[]{:S(2)}) async-start(s8[8388608]{0:T(1024)(128)(4,1)} %bitcast.3), calls=%async_computation.1 | async-start | bytes 8388608
  16.2 4.3 %collective-permute-start.2 = (bf16[8,2,8,256]{3,2,1,0:T(8,128)(2,1)S(1)}, bf16[8,2,8,256]{3,2,1,0:T(8,128)(2,1)S(1)}, u32[]{:S(2)}, u32[]{:S(2)}) collective-permute-start(bf16[8,2,8,256]{3,2,1,0:T(8,128)(2,1)S(1)} %get-tuple-element.23), channel_id=1, source_target_pairs={{0,8},{2,10},{4,12},{6,14},{8,0},{10,2},{12,4},{14,6},{16,24},{18,... | collective-permute-start | bytes 196616 | tf_op jit(solution)/shard_map/ppermute | solution.py:408
  18.5 18.5 %copy-start.2 = (bf16[256,1024]{1,0:T(8,128)(2,1)S(1)}, bf16[256,1024]{1,0:T(8,128)(2,1)}, u32[]{:S(2)}) copy-start(bf16[256,1024]{1,0:T(8,128)(2,1)} %w_in_ref.3) | copy-start | bytes 1572868
  18.6 18.5 %copy-start.3 = (bf16[1024,256]{1,0:T(8,128)(2,1)S(1)}, bf16[1024,256]{1,0:T(8,128)(2,1)}, u32[]{:S(2)}) copy-start(bf16[1024,256]{1,0:T(8,128)(2,1)} %w_out_ref.3) | copy-start | bytes 1572868
  18.6 18.5 %copy-start.5 = (f32[3,256]{1,0:T(4,128)S(1)}, f32[3,256]{1,0:T(4,128)}, u32[]{:S(2)}) copy-start(f32[3,256]{1,0:T(4,128)} %taps_ref.3) | copy-start | bytes 9220
  18.6 18.5 %copy-start.6 = (f32[1024]{0:T(1024)S(1)}, f32[1024]{0:T(1024)}, u32[]{:S(2)}) copy-start(f32[1024]{0:T(1024)} %param.13) | copy-start | bytes 12292
  18.6 18.5 %copy-start.7 = (f32[256]{0:T(256)S(1)}, f32[256]{0:T(256)}, u32[]{:S(2)}) copy-start(f32[256]{0:T(256)} %param.15) | copy-start | bytes 3076
  18.6 18.5 %copy-start.8 = (s32[4,9,6]{2,1,0:T(8,128)S(1)}, s32[4,9,6]{2,1,0:T(8,128)}, u32[]{:S(2)}) copy-start(s32[4,9,6]{2,1,0:T(8,128)} %constant.76.clone.items_ref) | copy-start | bytes 2596
  20.5 5.2 %collective-permute-start.3 = (bf16[8,2,8,256]{3,2,1,0:T(8,128)(2,1)S(1)}, bf16[8,2,8,256]{3,2,1,0:T(8,128)(2,1)S(1)}, u32[]{:S(2)}, u32[]{:S(2)}) collective-permute-start(bf16[8,2,8,256]{3,2,1,0:T(8,128)(2,1)S(1)} %get-tuple-element.26), channel_id=1, source_target_pairs={{0,16},{2,18},{4,20},{6,22},{8,24},{10,26},{12,28},{14,30},{16,0},... | collective-permute-start | bytes 196616 | tf_op jit(solution)/shard_map/ppermute | solution.py:408
  26.0 4.3 %collective-permute-start.4 = (bf16[8,2,8,256]{3,2,1,0:T(8,128)(2,1)S(1)}, bf16[8,2,8,256]{3,2,1,0:T(8,128)(2,1)S(1)}, u32[]{:S(2)}, u32[]{:S(2)}) collective-permute-start(bf16[8,2,8,256]{3,2,1,0:T(8,128)(2,1)S(1)} %mix.1.mine_ref), channel_id=1, source_target_pairs={{0,8},{2,10},{4,12},{6,14},{8,0},{10,2},{12,4},{14,6},{16,24},{18,... | collective-permute-start | bytes 196616 | tf_op jit(solution)/shard_map/ppermute | solution.py:408
  30.4 5.0 %collective-permute-start.5 = (bf16[16,2,8,256]{3,2,1,0:T(8,128)(2,1)S(1)}, bf16[16,2,8,256]{3,2,1,0:T(8,128)(2,1)S(1)}, u32[]{:S(2)}, u32[]{:S(2)}) collective-permute-start(bf16[16,2,8,256]{3,2,1,0:T(8,128)(2,1)S(1)} %join.1.refs_0_), channel_id=1, source_target_pairs={{0,4},{2,6},{4,0},{6,2},{8,12},{10,14},{12,8},{14,10},{16,20},{18,... | collective-permute-start | bytes 393224 | tf_op jit(solution)/shard_map/ppermute | solution.py:408
  35.4 1.6 %collective-permute-start.6 = (bf16[2,256,256]{2,1,0:T(8,128)(2,1)S(1)}, bf16[2,256,256]{2,1,0:T(8,128)(2,1)S(1)}, u32[]{:S(2)}, u32[]{:S(2)}) collective-permute-start(bf16[2,256,256]{2,1,0:T(8,128)(2,1)S(1)} %stack.1.mine_ref), channel_id=1, source_target_pairs={{0,2},{2,0},{4,6},{6,4},{8,10},{10,8},{12,14},{14,12},{16,18},{18,... | collective-permute-start | bytes 786440 | tf_op jit(solution)/shard_map/ppermute | solution.py:408
  37.1 20.4 %copy-start.4 = (s32[4,9,2]{2,1,0:T(8,128)S(1)}, s32[4,9,2]{2,1,0:T(8,128)}, u32[]{:S(2)}) copy-start(s32[4,9,2]{2,1,0:T(8,128)} %constant.77.clone.items_ref) | copy-start | bytes 868

commit v5 on v4

--- a/solution.py
+++ b/solution.py
@@ -16,16 +16,16 @@
 ROWS_BYTES = 36 * 2**20
 
 
-def wave_tables(own, start, modes, x_rows, total):
+def wave_table(gx, halving, modes, x_rows, total, inverse):
     shape = (2 * modes, x_rows)
     row = lax.broadcasted_iota(jnp.int32, shape, 0)
-    waves = row // 2 ^ own
-    product = waves * (start + lax.broadcasted_iota(jnp.int32, shape, 1)) % total
+    waves = row // 2 ^ first_mode(gx, halving, modes)
+    product = waves * (gx * x_rows + lax.broadcasted_iota(jnp.int32, shape, 1)) % total
     angles = 2.0 * math.pi / total * product.astype(F32)
-    scale = 1.0 / math.sqrt(total)
     parts = jnp.where(row % 2 == 0, jnp.cos(angles), -jnp.sin(angles))
-    amplitude = jnp.where(waves == 0, 1.0, 2.0).astype(F32)
-    return (parts * scale).astype(BF16), (amplitude * parts * scale).astype(BF16)
+    if inverse:
+        parts = jnp.where(waves == 0, 1.0, 2.0) * parts
+    return (parts * (1.0 / math.sqrt(total))).astype(BF16)
 
 
 def spread(table, cols):
@@ -58,28 +58,30 @@
     return jnp.where(same, wide[:, None, :], 0.0).reshape(waves * cols, width).astype(BF16)
 
 
-def widen_kernel(table_ref, wide_ref):
-    x_rows = table_ref.shape[1]
-    cols = wide_ref.shape[1] // x_rows
+def widen_kernel(halving, modes, total, place_ref, wide_ref):
+    cols = wide_ref.shape[0] // (2 * modes)
+    x_rows = wide_ref.shape[1] // cols
+    table = wave_table(place_ref[0] >> 1, halving, modes, x_rows, total, False)
     xb = min(x_rows, 128)
     width = xb * cols
     for part in range(x_rows // xb):
         wide_ref[:, part * width : (part + 1) * width] = spread_wide(
-            table_ref[:, part * xb : (part + 1) * xb], cols
+            table[:, part * xb : (part + 1) * xb], cols
         )
 
 
-def widen(table, cols):
-    waves, x_rows = table.shape
-    return pl.pallas_call(
-        widen_kernel,
-        out_shape=jax.ShapeDtypeStruct((waves * cols, x_rows * cols), BF16),
+def widen(place, halving, modes, cols, x_rows, total):
+    rows = 2 * modes
+    return pl.pallas_call(
+        functools.partial(widen_kernel, halving, modes, total),
+        in_specs=[pl.BlockSpec(memory_space=pltpu.SMEM)],
+        out_shape=jax.ShapeDtypeStruct((rows * cols, x_rows * cols), BF16),
         compiler_params=pltpu.CompilerParams(vmem_limit_bytes=SMALL_BYTES),
         cost_estimate=pl.CostEstimate(
-            flops=5 * 10**9, bytes_accessed=4 * waves * cols * x_rows * cols, transcendentals=0
+            flops=5 * 10**9, bytes_accessed=4 * rows * cols * x_rows * cols, transcendentals=0
         ),
         name="widen",
-    )(table)
+    )(place)
 
 
 def forward_kernel(live, place_ref, wide_ref, field_ref, send_ref, keep_ref, *edge_refs):
@@ -141,41 +143,41 @@
     return sum((gx >> level & 1) * (modes >> level) for level in range(1, halving))
 
 
-def prepare_kernel(halving, place_ref, table_ref, weight_ref, inv_ref, own_ref, sem):
+def prepare_kernel(halving, total, place_ref, weight_ref, inv_ref, own_ref, sem):
     owned = own_ref.shape[0]
     first = first_mode(place_ref[0] >> 1, halving, weight_ref.shape[0])
     move = pltpu.make_async_copy(weight_ref.at[pl.ds(first, owned)], own_ref, sem)
     move.start()
-    waves, x_rows = table_ref.shape
-    cols = inv_ref.shape[0] // x_rows
+    modes = weight_ref.shape[0]
+    cols = inv_ref.shape[1] // (2 * modes)
+    x_rows = inv_ref.shape[0] // cols
+    table = wave_table(place_ref[0] >> 1, halving, modes, x_rows, total, True)
     xb = min(x_rows, 128)
     for part in range(x_rows // xb):
         inv_ref[part * xb * cols : (part + 1) * xb * cols] = spread(
-            table_ref[:, part * xb : (part + 1) * xb], cols
+            table[:, part * xb : (part + 1) * xb], cols
         )
     move.wait()
 
 
-def prepare(table, cols, weight, place, halving):
-    waves, x_rows = table.shape
-    owned = weight.shape[0] >> halving - 1
+def prepare(x_rows, cols, weight, place, halving, total):
+    modes = weight.shape[0]
     vmem = pl.BlockSpec(memory_space=pltpu.VMEM)
     return pl.pallas_call(
-        functools.partial(prepare_kernel, halving),
+        functools.partial(prepare_kernel, halving, total),
         in_specs=[
             pl.BlockSpec(memory_space=pltpu.SMEM),
-            vmem,
             pl.BlockSpec(memory_space=pltpu.HBM),
         ],
         out_specs=[vmem, vmem],
         out_shape=[
-            jax.ShapeDtypeStruct((x_rows * cols, waves * cols), BF16),
-            jax.ShapeDtypeStruct((owned,) + weight.shape[1:], BF16),
+            jax.ShapeDtypeStruct((x_rows * cols, 2 * modes * cols), BF16),
+            jax.ShapeDtypeStruct((modes >> halving - 1,) + weight.shape[1:], BF16),
         ],
         scratch_shapes=[pltpu.SemaphoreType.DMA],
         compiler_params=pltpu.CompilerParams(vmem_limit_bytes=SMALL_BYTES),
         name="prepare",
-    )(place, table, weight)
+    )(place, weight)
 
 
 def halve_kernel(half, keep_ref, got_ref, *refs):
@@ -403,16 +405,17 @@
 
     levels = gx_size.bit_length() - 1
     halving = max(min(levels - 1, modes.bit_length()), 1)
-    own = first_mode(gx, halving, modes)
-    table, inverse = wave_tables(own, gx * x_rows, modes, x_rows, x_rows * gx_size)
+    total = x_rows * gx_size
     swap = lambda a, level: lax.ppermute(
         a, "gx", [(i, i ^ (1 << level)) for i in range(gx_size)]
     )
     parts = half_rows
     xb = x_rows // parts
     halos = []
-    send, keep, *edge = forward_transform(features, widen(table, cols), place, live)
-    inv, weight = prepare(inverse, cols, spectral_weight, place, halving)
+    send, keep, *edge = forward_transform(
+        features, widen(place, halving, modes, cols, x_rows, total), place, live
+    )
+    inv, weight = prepare(x_rows, cols, spectral_weight, place, halving, total)
     for level in range(levels):
         got = swap(send, level)
         ahead = []

time: 66 us -> 64.8 us (0.982)
  local copies, waits for them, and re-layouts: 3.43 us -> 2.59 us
    unnamed x22 -> x18, local copies, waits for them, and re-layouts: 3.43 us -> 2.59 us
  transfers between devices with their start and end apart: 8 -> 8, of which waited for: 6 -> 6; matrix products, arithmetic and copies ran while one was open for 0% -> 0% of each run, Pallas kernels for 33% -> 34%
where the time goes in v5:
time: 64.8 us; the launch traced here: 64.7 us
  Pallas kernels  33.7 us (52%)
  waiting for transfers between devices  16 us (25%)
  starting transfers between devices  12.3 us (19%)
  local copies, waits for them, and re-layouts  2.59 us (4%)
    pallas_call x2, Pallas kernels, rows_of(): pl.pallas_call(functools.partial(row_kernel, len(halos), min(sub, tokens)...  28.7 us
    ppermute x7, waiting for transfers between devices, local(): lax.ppermute(a, 'gx', [(i, i ^ 1 << level) for i in range(gx_size)])  16 us
    ppermute x7, starting transfers between devices, local(): lax.ppermute(a, 'gx', [(i, i ^ 1 << level) for i in range(gx_size)])  9.7 us
    pallas_call x1, Pallas kernels, forward_transform(): pl.pallas_call(functools.partial(forward_kernel, live), in_specs=[smem, v...  2.68 us
    unnamed x18, local copies, waits for them, and re-layouts  2.59 us
    ppermute x1, starting transfers between devices, local(): lax.ppermute(ahead[-1], 'gy', pairs + [(b, a) for a, b in pairs])  2.58 us
  transfers between devices with their start and end apart: 8, of which 6 were waited for; matrix products, arithmetic and copies ran while one was open for 0% of the time, Pallas kernels for 34%

profile of v5, /device:TPU:0, one launch (start us, length us, event | category | flops | bytes accessed | tf_op | source)
XLA Modules:
  0.0 64.7 jit_solution(605702233932685932)
XLA Ops:
  0.0 0.8 %widen.1.wide_ref = bf16[256,4096]{1,0:T(8,128)(2,1)S(1)} custom-call(s32[1]{0:T(128)} %bitcast.place_ref), custom_call_target="tpu_custom_call" | custom-call | flops 5000000000 | bytes 4194304 | tf_op jit(solution)/shard_map/widen/pallas_call | solution.py:75
  0.8 2.5 %copy-done = bf16[512,4,8,256]{3,2,1,0:T(8,128)(2,1)S(1)} copy-done((bf16[512,4,8,256]{3,2,1,0:T(8,128)(2,1)S(1)}, bf16[512,4,8,256]{3,2,1,0:T(8,128)(2,1)}, u32[]{:S(2)}) %copy-start) | copy-done | bytes 8388632
  3.4 2.7 %forward.1 = (bf16[32,2,8,256]{3,2,1,0:T(8,128)(2,1)S(1)}, f32[32,2,8,256]{3,2,1,0:T(8,128)S(1)}, bf16[512,8,256]{2,1,0:T(8,128)(2,1)S(1)}) custom-call(s32[1]{0:T(128)} %bitcast.place_ref, bf16[256,4096]{1,0:T(8,128)(2,1)S(1)} %widen.1.wide_ref, bf16[512,4,8,256]{3,2,1,0:T(8,128)(2,1)S(1)} %copy-done), custom_call_target="tpu_custom_call" | custom-call | tf_op jit(solution)/shard_map/forward/pallas_call | solution.py:112
  6.1 0.5 collective-permute-start
  6.6 0.1 hold.1.refs_0_
  6.7 2.6 %collective-permute-start.7 = (bf16[512,8,256]{2,1,0:T(8,128)(2,1)S(1)}, bf16[512,8,256]{2,1,0:T(8,128)(2,1)S(1)}, u32[]{:S(2)}, u32[]{:S(2)}) collective-permute-start(bf16[512,8,256]{2,1,0:T(8,128)(2,1)S(1)} %hold.1.refs_0_), channel_id=1, source_target_pairs={{0,1},{1,0},{2,3},{3,2},{4,5},{5,4},{6,7},{7,6},{8,9},{9,8},{10,11... | collective-permute-start | bytes 6291464 | tf_op jit(solution)/shard_map/ppermute | solution.py:426
  9.3 0.0 collective-permute-done.got_ref
  9.3 0.1 halve.2
  9.4 1.6 %collective-permute-start.1 = (bf16[16,2,8,256]{3,2,1,0:T(8,128)(2,1)S(1)}, bf16[16,2,8,256]{3,2,1,0:T(8,128)(2,1)S(1)}, u32[]{:S(2)}, u32[]{:S(2)}) collective-permute-start(bf16[16,2,8,256]{3,2,1,0:T(8,128)(2,1)S(1)} %get-tuple-element.21), channel_id=1, source_target_pairs={{0,4},{2,6},{4,0},{6,2},{8,12},{10,14},{12,8},{14,10},{16,20},{18,... | collective-permute-start | bytes 393224 | tf_op jit(solution)/shard_map/ppermute | solution.py:409
  11.0 4.1 %collective-permute-done.1.got_ref = bf16[16,2,8,256]{3,2,1,0:T(8,128)(2,1)S(1)} collective-permute-done((bf16[16,2,8,256]{3,2,1,0:T(8,128)(2,1)S(1)}, bf16[16,2,8,256]{3,2,1,0:T(8,128)(2,1)S(1)}, u32[]{:S(2)}, u32[]{:S(2)}) %collective-permute-start.1) | collective-permute-done | bytes 131104 | tf_op jit(solution)/shard_map/ppermute | solution.py:409
  15.1 1.6 %collective-permute-start.2 = (bf16[8,2,8,256]{3,2,1,0:T(8,128)(2,1)S(1)}, bf16[8,2,8,256]{3,2,1,0:T(8,128)(2,1)S(1)}, u32[]{:S(2)}, u32[]{:S(2)}) collective-permute-start(bf16[8,2,8,256]{3,2,1,0:T(8,128)(2,1)S(1)} %get-tuple-element.23), channel_id=1, source_target_pairs={{0,8},{2,10},{4,12},{6,14},{8,0},{10,2},{12,4},{14,6},{16,24},{18,... | collective-permute-start | bytes 196616 | tf_op jit(solution)/shard_map/ppermute | solution.py:409
  16.7 0.9 %prepare.1 = (bf16[4096,256]{1,0:T(8,128)(2,1)S(1)}, bf16[4,2,256,256]{3,2,1,0:T(8,128)(2,1)S(1)}) custom-call(s32[1]{0:T(128)} %bitcast.place_ref, bf16[16,2,256,256]{3,2,1,0:T(8,128)(2,1)S(1)} %copy-done.1), custom_call_target="tpu_custom_call" | custom-call | tf_op jit(solution)/shard_map/prepare/pallas_call | solution.py:166
  17.7 0.0 copy-start.2
  17.7 0.0 copy-start.3
  17.7 0.0 copy-start.5
  17.7 0.0 copy-start.6
  17.7 0.0 copy-start.7
  17.7 0.0 copy-start.8
  17.7 1.7 %collective-permute-done.2.got_ref = bf16[8,2,8,256]{3,2,1,0:T(8,128)(2,1)S(1)} collective-permute-done((bf16[8,2,8,256]{3,2,1,0:T(8,128)(2,1)S(1)}, bf16[8,2,8,256]{3,2,1,0:T(8,128)(2,1)S(1)}, u32[]{:S(2)}, u32[]{:S(2)}) %collective-permute-start.2) | collective-permute-done | bytes 65568 | tf_op jit(solution)/shard_map/ppermute | solution.py:409
  19.4 2.7 %collective-permute-start.3 = (bf16[8,2,8,256]{3,2,1,0:T(8,128)(2,1)S(1)}, bf16[8,2,8,256]{3,2,1,0:T(8,128)(2,1)S(1)}, u32[]{:S(2)}, u32[]{:S(2)}) collective-permute-start(bf16[8,2,8,256]{3,2,1,0:T(8,128)(2,1)S(1)} %get-tuple-element.26), channel_id=1, source_target_pairs={{0,16},{2,18},{4,20},{6,22},{8,24},{10,26},{12,28},{14,30},{16,0},... | collective-permute-start | bytes 196616 | tf_op jit(solution)/shard_map/ppermute | solution.py:409
  22.1 2.6 %collective-permute-done.3.got_ref = bf16[8,2,8,256]{3,2,1,0:T(8,128)(2,1)S(1)} collective-permute-done((bf16[8,2,8,256]{3,2,1,0:T(8,128)(2,1)S(1)}, bf16[8,2,8,256]{3,2,1,0:T(8,128)(2,1)S(1)}, u32[]{:S(2)}, u32[]{:S(2)}) %collective-permute-start.3) | collective-permute-done | bytes 65568 | tf_op jit(solution)/shard_map/ppermute | solution.py:409
  24.7 0.3 mix.1.mine_ref
  24.9 1.6 %collective-permute-start.4 = (bf16[8,2,8,256]{3,2,1,0:T(8,128)(2,1)S(1)}, bf16[8,2,8,256]{3,2,1,0:T(8,128)(2,1)S(1)}, u32[]{:S(2)}, u32[]{:S(2)}) collective-permute-start(bf16[8,2,8,256]{3,2,1,0:T(8,128)(2,1)S(1)} %mix.1.mine_ref), channel_id=1, source_target_pairs={{0,8},{2,10},{4,12},{6,14},{8,0},{10,2},{12,4},{14,6},{16,24},{18,... | collective-permute-start | bytes 196616 | tf_op jit(solution)/shard_map/ppermute | solution.py:409
  26.6 2.7 %collective-permute-done.4.got_ref = bf16[8,2,8,256]{3,2,1,0:T(8,128)(2,1)S(1)} collective-permute-done((bf16[8,2,8,256]{3,2,1,0:T(8,128)(2,1)S(1)}, bf16[8,2,8,256]{3,2,1,0:T(8,128)(2,1)S(1)}, u32[]{:S(2)}, u32[]{:S(2)}) %collective-permute-start.4) | collective-permute-done | bytes 65568 | tf_op jit(solution)/shard_map/ppermute | solution.py:409
  29.3 1.6 %collective-permute-start.5 = (bf16[16,2,8,256]{3,2,1,0:T(8,128)(2,1)S(1)}, bf16[16,2,8,256]{3,2,1,0:T(8,128)(2,1)S(1)}, u32[]{:S(2)}, u32[]{:S(2)}) collective-permute-start(bf16[16,2,8,256]{3,2,1,0:T(8,128)(2,1)S(1)} %join.1.refs_0_), channel_id=1, source_target_pairs={{0,4},{2,6},{4,0},{6,2},{8,12},{10,14},{12,8},{14,10},{16,20},{18,... | collective-permute-start | bytes 393224 | tf_op jit(solution)/shard_map/ppermute | solution.py:409
  30.9 3.4 %collective-permute-done.5.refs_1_ = bf16[16,2,8,256]{3,2,1,0:T(8,128)(2,1)S(1)} collective-permute-done((bf16[16,2,8,256]{3,2,1,0:T(8,128)(2,1)S(1)}, bf16[16,2,8,256]{3,2,1,0:T(8,128)(2,1)S(1)}, u32[]{:S(2)}, u32[]{:S(2)}) %collective-permute-start.5) | collective-permute-done | bytes 131104 | tf_op jit(solution)/shard_map/ppermute | solution.py:409
  34.3 0.1 collective-permute-start.6
  34.4 1.5 %collective-permute-done.6.other_ref = bf16[2,256,256]{2,1,0:T(8,128)(2,1)S(1)} collective-permute-done((bf16[2,256,256]{2,1,0:T(8,128)(2,1)S(1)}, bf16[2,256,256]{2,1,0:T(8,128)(2,1)S(1)}, u32[]{:S(2)}, u32[]{:S(2)}) %collective-permute-start.6) | collective-permute-done | bytes 262176 | tf_op jit(solution)/shard_map/ppermute | solution.py:409
  36.0 0.0 copy-start.4
  36.0 20.4 %rows.2.rest_1_ = bf16[512,4,8,256]{3,2,1,0:T(8,128)(2,1)} custom-call(s32[4,9,6]{2,1,0:T(8,128)S(1)} %copy-done.8, s32[1]{0:T(128)} %bitcast.place_ref, bf16[512,4,8,256]{3,2,1,0:T(8,128)(2,1)S(1)} %copy-done, bf16[4096,256]{1,0:T(8,128)(2,1)S(1)} %get-tuple-element.16.inv_ref, f32[3,256]{1,0:T(4,128)S(1)} %copy-done.5, bf16[256,1024]{1,0:T(8,128)(2,1)S(1)} %copy-done.2, ...), custom_call_target="tpu_custom_call" | custom-call | flops 14495514624 | bytes 6291456 | tf_op jit(solution)/shard_map/rows/pallas_call | solution.py:365
  56.4 0.0 collective-permute-done.7.rest_0_
  56.4 8.3 %rows.3 = bf16[512,4,8,256]{3,2,1,0:T(8,128)(2,1)} custom-call(s32[4,9,2]{2,1,0:T(8,128)S(1)} %copy-done.4, s32[1]{0:T(128)} %bitcast.place_ref, bf16[512,4,8,256]{3,2,1,0:T(8,128)(2,1)S(1)} %copy-done, bf16[4096,256]{1,0:T(8,128)(2,1)S(1)} %get-tuple-element.16.inv_ref, f32[3,256]{1,0:T(4,128)S(1)} %copy-done.5, ...), custom_call_target="tpu_custom_call", output_to_operand_aliasing={{}: (12, {})} | custom-call | flops 4831838208 | bytes 2097152 | tf_op jit(solution)/shard_map/rows/pallas_call | solution.py:365
  (14 shorter events, 0.1 us)
Async XLA Ops:
  0.0 3.4 %copy-start = (bf16[512,4,8,256]{3,2,1,0:T(8,128)(2,1)S(1)}, bf16[512,4,8,256]{3,2,1,0:T(8,128)(2,1)}, u32[]{:S(2)}) copy-start(bf16[512,4,8,256]{3,2,1,0:T(8,128)(2,1)} %field_ref.5) | copy-start | bytes 25165828
  6.1 3.2 %collective-permute-start = (bf16[32,2,8,256]{3,2,1,0:T(8,128)(2,1)S(1)}, bf16[32,2,8,256]{3,2,1,0:T(8,128)(2,1)S(1)}, u32[]{:S(2)}, u32[]{:S(2)}) collective-permute-start(bf16[32,2,8,256]{3,2,1,0:T(8,128)(2,1)S(1)} %get-tuple-element.18.ahead_ref), channel_id=1, source_target_pairs={{0,2},{2,0},{4,6},{6,4},{8,10},{10,8},{12,14},{14,12},{16,18},{18,... | collective-permute-start | bytes 786440 | tf_op jit(solution)/shard_map/ppermute | solution.py:409
  6.6 10.1 %copy-start.1 = (bf16[16,2,256,256]{3,2,1,0:T(8,128)(2,1)S(1)}, bf16[16,2,256,256]{3,2,1,0:T(8,128)(2,1)}, u32[]{:S(2)}) copy-start(bf16[16,2,256,256]{3,2,1,0:T(8,128)(2,1)} %weight_ref.1) | copy-start | bytes 12582916
  6.7 49.6 %collective-permute-start.7 = (bf16[512,8,256]{2,1,0:T(8,128)(2,1)S(1)}, bf16[512,8,256]{2,1,0:T(8,128)(2,1)S(1)}, u32[]{:S(2)}, u32[]{:S(2)}) collective-permute-start(bf16[512,8,256]{2,1,0:T(8,128)(2,1)S(1)} %hold.1.refs_0_), channel_id=1, source_target_pairs={{0,1},{1,0},{2,3},{3,2},{4,5},{5,4},{6,7},{7,6},{8,9},{9,8},{10,11... | collective-permute-start | bytes 6291464 | tf_op jit(solution)/shard_map/ppermute | solution.py:426
  9.4 5.7 %collective-permute-start.1 = (bf16[16,2,8,256]{3,2,1,0:T(8,128)(2,1)S(1)}, bf16[16,2,8,256]{3,2,1,0:T(8,128)(2,1)S(1)}, u32[]{:S(2)}, u32[]{:S(2)}) collective-permute-start(bf16[16,2,8,256]{3,2,1,0:T(8,128)(2,1)S(1)} %get-tuple-element.21), channel_id=1, source_target_pairs={{0,4},{2,6},{4,0},{6,2},{8,12},{10,14},{12,8},{14,10},{16,20},{18,... | collective-permute-start | bytes 393224 | tf_op jit(solution)/shard_map/ppermute | solution.py:409
  15.1 4.3 %collective-permute-start.2 = (bf16[8,2,8,256]{3,2,1,0:T(8,128)(2,1)S(1)}, bf16[8,2,8,256]{3,2,1,0:T(8,128)(2,1)S(1)}, u32[]{:S(2)}, u32[]{:S(2)}) collective-permute-start(bf16[8,2,8,256]{3,2,1,0:T(8,128)(2,1)S(1)} %get-tuple-element.23), channel_id=1, source_target_pairs={{0,8},{2,10},{4,12},{6,14},{8,0},{10,2},{12,4},{14,6},{16,24},{18,... | collective-permute-start | bytes 196616 | tf_op jit(solution)/shard_map/ppermute | solution.py:409
  17.7 18.3 %copy-start.2 = (bf16[256,1024]{1,0:T(8,128)(2,1)S(1)}, bf16[256,1024]{1,0:T(8,128)(2,1)}, u32[]{:S(2)}) copy-start(bf16[256,1024]{1,0:T(8,128)(2,1)} %w_in_ref.3) | copy-start | bytes 1572868
  17.7 18.3 %copy-start.3 = (bf16[1024,256]{1,0:T(8,128)(2,1)S(1)}, bf16[1024,256]{1,0:T(8,128)(2,1)}, u32[]{:S(2)}) copy-start(bf16[1024,256]{1,0:T(8,128)(2,1)} %w_out_ref.3) | copy-start | bytes 1572868
  17.7 18.3 %copy-start.5 = (f32[3,256]{1,0:T(4,128)S(1)}, f32[3,256]{1,0:T(4,128)}, u32[]{:S(2)}) copy-start(f32[3,256]{1,0:T(4,128)} %taps_ref.3) | copy-start | bytes 9220
  17.7 18.2 %copy-start.6 = (f32[1024]{0:T(1024)S(1)}, f32[1024]{0:T(1024)}, u32[]{:S(2)}) copy-start(f32[1024]{0:T(1024)} %param.13) | copy-start | bytes 12292
  17.7 18.2 %copy-start.7 = (f32[256]{0:T(256)S(1)}, f32[256]{0:T(256)}, u32[]{:S(2)}) copy-start(f32[256]{0:T(256)} %param.15) | copy-start | bytes 3076
  17.7 18.2 %copy-start.8 = (s32[4,9,6]{2,1,0:T(8,128)S(1)}, s32[4,9,6]{2,1,0:T(8,128)}, u32[]{:S(2)}) copy-start(s32[4,9,6]{2,1,0:T(8,128)} %constant.25.clone.items_ref) | copy-start | bytes 2596
  19.4 5.2 %collective-permute-start.3 = (bf16[8,2,8,256]{3,2,1,0:T(8,128)(2,1)S(1)}, bf16[8,2,8,256]{3,2,1,0:T(8,128)(2,1)S(1)}, u32[]{:S(2)}, u32[]{:S(2)}) collective-permute-start(bf16[8,2,8,256]{3,2,1,0:T(8,128)(2,1)S(1)} %get-tuple-element.26), channel_id=1, source_target_pairs={{0,16},{2,18},{4,20},{6,22},{8,24},{10,26},{12,28},{14,30},{16,0},... | collective-permute-start | bytes 196616 | tf_op jit(solution)/shard_map/ppermute | solution.py:409
  24.9 4.3 %collective-permute-start.4 = (bf16[8,2,8,256]{3,2,1,0:T(8,128)(2,1)S(1)}, bf16[8,2,8,256]{3,2,1,0:T(8,128)(2,1)S(1)}, u32[]{:S(2)}, u32[]{:S(2)}) collective-permute-start(bf16[8,2,8,256]{3,2,1,0:T(8,128)(2,1)S(1)} %mix.1.mine_ref), channel_id=1, source_target_pairs={{0,8},{2,10},{4,12},{6,14},{8,0},{10,2},{12,4},{14,6},{16,24},{18,... | collective-permute-start | bytes 196616 | tf_op jit(solution)/shard_map/ppermute | solution.py:409
  29.3 5.0 %collective-permute-start.5 = (bf16[16,2,8,256]{3,2,1,0:T(8,128)(2,1)S(1)}, bf16[16,2,8,256]{3,2,1,0:T(8,128)(2,1)S(1)}, u32[]{:S(2)}, u32[]{:S(2)}) collective-permute-start(bf16[16,2,8,256]{3,2,1,0:T(8,128)(2,1)S(1)} %join.1.refs_0_), channel_id=1, source_target_pairs={{0,4},{2,6},{4,0},{6,2},{8,12},{10,14},{12,8},{14,10},{16,20},{18,... | collective-permute-start | bytes 393224 | tf_op jit(solution)/shard_map/ppermute | solution.py:409
  34.3 1.6 %collective-permute-start.6 = (bf16[2,256,256]{2,1,0:T(8,128)(2,1)S(1)}, bf16[2,256,256]{2,1,0:T(8,128)(2,1)S(1)}, u32[]{:S(2)}, u32[]{:S(2)}) collective-permute-start(bf16[2,256,256]{2,1,0:T(8,128)(2,1)S(1)} %stack.1.mine_ref), channel_id=1, source_target_pairs={{0,2},{2,0},{4,6},{6,4},{8,10},{10,8},{12,14},{14,12},{16,18},{18,... | collective-permute-start | bytes 786440 | tf_op jit(solution)/shard_map/ppermute | solution.py:409
  36.0 20.4 %copy-start.4 = (s32[4,9,2]{2,1,0:T(8,128)S(1)}, s32[4,9,2]{2,1,0:T(8,128)}, u32[]{:S(2)}) copy-start(s32[4,9,2]{2,1,0:T(8,128)} %constant.26.clone.items_ref) | copy-start | bytes 868

commit v6 on v5

--- a/solution.py
+++ b/solution.py
@@ -306,10 +306,11 @@
         return field_ref[pl.ds(start + s * sub // cols, sub // cols), row].reshape(sub, channels)
 
     def load_after(s):
-        part = load(after, s)
-        for at, ref in enumerate(halo_refs):
-            halo = ref[pl.ds(start + s * sub // cols, sub // cols)].reshape(sub, channels)
-            part = jnp.where(source == at + 1, halo, part)
+        lines = pl.ds(start + s * sub // cols, sub // cols)
+        parts = [ref[lines].reshape(sub, channels) for ref in halo_refs] or [load(after, s)]
+        part = parts[0]
+        for at, other in enumerate(parts[1:]):
+            part = jnp.where(source == at + 2, other, part)
         return part
 
     def join(s):

time: 64.8 us -> 64.6 us (level)
  no operation moved by 1% of the time
where the time goes in v6:
time: 64.6 us; the launch traced here: 64.4 us
  Pallas kernels  33.4 us (52%)
  waiting for transfers between devices  16 us (25%)
  starting transfers between devices  12.3 us (19%)
  local copies, waits for them, and re-layouts  2.59 us (4%)
    pallas_call x2, Pallas kernels, rows_of(): pl.pallas_call(functools.partial(row_kernel, len(halos), min(sub, tokens)...  28.4 us
    ppermute x7, waiting for transfers between devices, local(): lax.ppermute(a, 'gx', [(i, i ^ 1 << level) for i in range(gx_size)])  16 us
    ppermute x7, starting transfers between devices, local(): lax.ppermute(a, 'gx', [(i, i ^ 1 << level) for i in range(gx_size)])  9.7 us
    pallas_call x1, Pallas kernels, forward_transform(): pl.pallas_call(functools.partial(forward_kernel, live), in_specs=[smem, v...  2.68 us
    unnamed x18, local copies, waits for them, and re-layouts  2.59 us
    ppermute x1, starting transfers between devices, local(): lax.ppermute(ahead[-1], 'gy', pairs + [(b, a) for a, b in pairs])  2.58 us
  transfers between devices with their start and end apart: 8, of which 6 were waited for; matrix products, arithmetic and copies ran while one was open for 0% of the time, Pallas kernels for 34%

profile of v6, /device:TPU:0, one launch (start us, length us, event | category | flops | bytes accessed | tf_op | source)
XLA Modules:
  0.0 64.4 jit_solution(16948809628732759415)
XLA Ops:
  0.0 0.8 %widen.1.wide_ref = bf16[256,4096]{1,0:T(8,128)(2,1)S(1)} custom-call(s32[1]{0:T(128)} %bitcast.place_ref), custom_call_target="tpu_custom_call" | custom-call | flops 5000000000 | bytes 4194304 | tf_op jit(solution)/shard_map/widen/pallas_call | solution.py:75
  0.8 2.5 %copy-done = bf16[512,4,8,256]{3,2,1,0:T(8,128)(2,1)S(1)} copy-done((bf16[512,4,8,256]{3,2,1,0:T(8,128)(2,1)S(1)}, bf16[512,4,8,256]{3,2,1,0:T(8,128)(2,1)}, u32[]{:S(2)}) %copy-start) | copy-done | bytes 8388632
  3.4 2.7 %forward.1 = (bf16[32,2,8,256]{3,2,1,0:T(8,128)(2,1)S(1)}, f32[32,2,8,256]{3,2,1,0:T(8,128)S(1)}, bf16[512,8,256]{2,1,0:T(8,128)(2,1)S(1)}) custom-call(s32[1]{0:T(128)} %bitcast.place_ref, bf16[256,4096]{1,0:T(8,128)(2,1)S(1)} %widen.1.wide_ref, bf16[512,4,8,256]{3,2,1,0:T(8,128)(2,1)S(1)} %copy-done), custom_call_target="tpu_custom_call" | custom-call | tf_op jit(solution)/shard_map/forward/pallas_call | solution.py:112
  6.1 0.5 collective-permute-start
  6.6 0.1 hold.1.refs_0_
  6.7 2.6 %collective-permute-start.7 = (bf16[512,8,256]{2,1,0:T(8,128)(2,1)S(1)}, bf16[512,8,256]{2,1,0:T(8,128)(2,1)S(1)}, u32[]{:S(2)}, u32[]{:S(2)}) collective-permute-start(bf16[512,8,256]{2,1,0:T(8,128)(2,1)S(1)} %hold.1.refs_0_), channel_id=1, source_target_pairs={{0,1},{1,0},{2,3},{3,2},{4,5},{5,4},{6,7},{7,6},{8,9},{9,8},{10,11... | collective-permute-start | bytes 6291464 | tf_op jit(solution)/shard_map/ppermute | solution.py:427
  9.3 0.0 collective-permute-done.got_ref
  9.3 0.1 halve.2
  9.4 1.6 %collective-permute-start.1 = (bf16[16,2,8,256]{3,2,1,0:T(8,128)(2,1)S(1)}, bf16[16,2,8,256]{3,2,1,0:T(8,128)(2,1)S(1)}, u32[]{:S(2)}, u32[]{:S(2)}) collective-permute-start(bf16[16,2,8,256]{3,2,1,0:T(8,128)(2,1)S(1)} %get-tuple-element.21), channel_id=1, source_target_pairs={{0,4},{2,6},{4,0},{6,2},{8,12},{10,14},{12,8},{14,10},{16,20},{18,... | collective-permute-start | bytes 393224 | tf_op jit(solution)/shard_map/ppermute | solution.py:410
  11.0 4.1 %collective-permute-done.1.got_ref = bf16[16,2,8,256]{3,2,1,0:T(8,128)(2,1)S(1)} collective-permute-done((bf16[16,2,8,256]{3,2,1,0:T(8,128)(2,1)S(1)}, bf16[16,2,8,256]{3,2,1,0:T(8,128)(2,1)S(1)}, u32[]{:S(2)}, u32[]{:S(2)}) %collective-permute-start.1) | collective-permute-done | bytes 131104 | tf_op jit(solution)/shard_map/ppermute | solution.py:410
  15.1 1.6 %collective-permute-start.2 = (bf16[8,2,8,256]{3,2,1,0:T(8,128)(2,1)S(1)}, bf16[8,2,8,256]{3,2,1,0:T(8,128)(2,1)S(1)}, u32[]{:S(2)}, u32[]{:S(2)}) collective-permute-start(bf16[8,2,8,256]{3,2,1,0:T(8,128)(2,1)S(1)} %get-tuple-element.23), channel_id=1, source_target_pairs={{0,8},{2,10},{4,12},{6,14},{8,0},{10,2},{12,4},{14,6},{16,24},{18,... | collective-permute-start | bytes 196616 | tf_op jit(solution)/shard_map/ppermute | solution.py:410
  16.7 0.9 %prepare.1 = (bf16[4096,256]{1,0:T(8,128)(2,1)S(1)}, bf16[4,2,256,256]{3,2,1,0:T(8,128)(2,1)S(1)}) custom-call(s32[1]{0:T(128)} %bitcast.place_ref, bf16[16,2,256,256]{3,2,1,0:T(8,128)(2,1)S(1)} %copy-done.1), custom_call_target="tpu_custom_call" | custom-call | tf_op jit(solution)/shard_map/prepare/pallas_call | solution.py:166
  17.7 0.0 copy-start.2
  17.7 0.0 copy-start.3
  17.7 0.0 copy-start.5
  17.7 0.0 copy-start.6
  17.7 0.0 copy-start.7
  17.7 0.0 copy-start.8
  17.7 1.7 %collective-permute-done.2.got_ref = bf16[8,2,8,256]{3,2,1,0:T(8,128)(2,1)S(1)} collective-permute-done((bf16[8,2,8,256]{3,2,1,0:T(8,128)(2,1)S(1)}, bf16[8,2,8,256]{3,2,1,0:T(8,128)(2,1)S(1)}, u32[]{:S(2)}, u32[]{:S(2)}) %collective-permute-start.2) | collective-permute-done | bytes 65568 | tf_op jit(solution)/shard_map/ppermute | solution.py:410
  19.4 2.7 %collective-permute-start.3 = (bf16[8,2,8,256]{3,2,1,0:T(8,128)(2,1)S(1)}, bf16[8,2,8,256]{3,2,1,0:T(8,128)(2,1)S(1)}, u32[]{:S(2)}, u32[]{:S(2)}) collective-permute-start(bf16[8,2,8,256]{3,2,1,0:T(8,128)(2,1)S(1)} %get-tuple-element.26), channel_id=1, source_target_pairs={{0,16},{2,18},{4,20},{6,22},{8,24},{10,26},{12,28},{14,30},{16,0},... | collective-permute-start | bytes 196616 | tf_op jit(solution)/shard_map/ppermute | solution.py:410
  22.1 2.6 %collective-permute-done.3.got_ref = bf16[8,2,8,256]{3,2,1,0:T(8,128)(2,1)S(1)} collective-permute-done((bf16[8,2,8,256]{3,2,1,0:T(8,128)(2,1)S(1)}, bf16[8,2,8,256]{3,2,1,0:T(8,128)(2,1)S(1)}, u32[]{:S(2)}, u32[]{:S(2)}) %collective-permute-start.3) | collective-permute-done | bytes 65568 | tf_op jit(solution)/shard_map/ppermute | solution.py:410
  24.7 0.3 mix.1.mine_ref
  24.9 1.6 %collective-permute-start.4 = (bf16[8,2,8,256]{3,2,1,0:T(8,128)(2,1)S(1)}, bf16[8,2,8,256]{3,2,1,0:T(8,128)(2,1)S(1)}, u32[]{:S(2)}, u32[]{:S(2)}) collective-permute-start(bf16[8,2,8,256]{3,2,1,0:T(8,128)(2,1)S(1)} %mix.1.mine_ref), channel_id=1, source_target_pairs={{0,8},{2,10},{4,12},{6,14},{8,0},{10,2},{12,4},{14,6},{16,24},{18,... | collective-permute-start | bytes 196616 | tf_op jit(solution)/shard_map/ppermute | solution.py:410
  26.6 2.7 %collective-permute-done.4.got_ref = bf16[8,2,8,256]{3,2,1,0:T(8,128)(2,1)S(1)} collective-permute-done((bf16[8,2,8,256]{3,2,1,0:T(8,128)(2,1)S(1)}, bf16[8,2,8,256]{3,2,1,0:T(8,128)(2,1)S(1)}, u32[]{:S(2)}, u32[]{:S(2)}) %collective-permute-start.4) | collective-permute-done | bytes 65568 | tf_op jit(solution)/shard_map/ppermute | solution.py:410
  29.3 1.6 %collective-permute-start.5 = (bf16[16,2,8,256]{3,2,1,0:T(8,128)(2,1)S(1)}, bf16[16,2,8,256]{3,2,1,0:T(8,128)(2,1)S(1)}, u32[]{:S(2)}, u32[]{:S(2)}) collective-permute-start(bf16[16,2,8,256]{3,2,1,0:T(8,128)(2,1)S(1)} %join.1.refs_0_), channel_id=1, source_target_pairs={{0,4},{2,6},{4,0},{6,2},{8,12},{10,14},{12,8},{14,10},{16,20},{18,... | collective-permute-start | bytes 393224 | tf_op jit(solution)/shard_map/ppermute | solution.py:410
  30.9 3.4 %collective-permute-done.5.refs_1_ = bf16[16,2,8,256]{3,2,1,0:T(8,128)(2,1)S(1)} collective-permute-done((bf16[16,2,8,256]{3,2,1,0:T(8,128)(2,1)S(1)}, bf16[16,2,8,256]{3,2,1,0:T(8,128)(2,1)S(1)}, u32[]{:S(2)}, u32[]{:S(2)}) %collective-permute-start.5) | collective-permute-done | bytes 131104 | tf_op jit(solution)/shard_map/ppermute | solution.py:410
  34.3 0.1 collective-permute-start.6
  34.4 1.5 %collective-permute-done.6.other_ref = bf16[2,256,256]{2,1,0:T(8,128)(2,1)S(1)} collective-permute-done((bf16[2,256,256]{2,1,0:T(8,128)(2,1)S(1)}, bf16[2,256,256]{2,1,0:T(8,128)(2,1)S(1)}, u32[]{:S(2)}, u32[]{:S(2)}) %collective-permute-start.6) | collective-permute-done | bytes 262176 | tf_op jit(solution)/shard_map/ppermute | solution.py:410
  36.0 0.0 copy-start.4
  36.0 20.4 %rows.2.rest_1_ = bf16[512,4,8,256]{3,2,1,0:T(8,128)(2,1)} custom-call(s32[4,9,6]{2,1,0:T(8,128)S(1)} %copy-done.8, s32[1]{0:T(128)} %bitcast.place_ref, bf16[512,4,8,256]{3,2,1,0:T(8,128)(2,1)S(1)} %copy-done, bf16[4096,256]{1,0:T(8,128)(2,1)S(1)} %get-tuple-element.16.inv_ref, f32[3,256]{1,0:T(4,128)S(1)} %copy-done.5, bf16[256,1024]{1,0:T(8,128)(2,1)S(1)} %copy-done.2, ...), custom_call_target="tpu_custom_call" | custom-call | flops 14495514624 | bytes 6291456 | tf_op jit(solution)/shard_map/rows/pallas_call | solution.py:366
  56.4 0.0 collective-permute-done.7.rest_0_
  56.4 8.1 %rows.3 = bf16[512,4,8,256]{3,2,1,0:T(8,128)(2,1)} custom-call(s32[4,9,2]{2,1,0:T(8,128)S(1)} %copy-done.4, s32[1]{0:T(128)} %bitcast.place_ref, bf16[512,4,8,256]{3,2,1,0:T(8,128)(2,1)S(1)} %copy-done, bf16[4096,256]{1,0:T(8,128)(2,1)S(1)} %get-tuple-element.16.inv_ref, f32[3,256]{1,0:T(4,128)S(1)} %copy-done.5, ...), custom_call_target="tpu_custom_call", output_to_operand_aliasing={{}: (12, {})} | custom-call | flops 4831838208 | bytes 2097152 | tf_op jit(solution)/shard_map/rows/pallas_call | solution.py:366
  (14 shorter events, 0.1 us)
Async XLA Ops:
  0.0 3.4 %copy-start = (bf16[512,4,8,256]{3,2,1,0:T(8,128)(2,1)S(1)}, bf16[512,4,8,256]{3,2,1,0:T(8,128)(2,1)}, u32[]{:S(2)}) copy-start(bf16[512,4,8,256]{3,2,1,0:T(8,128)(2,1)} %field_ref.5) | copy-start | bytes 25165828
  6.1 3.2 %collective-permute-start = (bf16[32,2,8,256]{3,2,1,0:T(8,128)(2,1)S(1)}, bf16[32,2,8,256]{3,2,1,0:T(8,128)(2,1)S(1)}, u32[]{:S(2)}, u32[]{:S(2)}) collective-permute-start(bf16[32,2,8,256]{3,2,1,0:T(8,128)(2,1)S(1)} %get-tuple-element.18.ahead_ref), channel_id=1, source_target_pairs={{0,2},{2,0},{4,6},{6,4},{8,10},{10,8},{12,14},{14,12},{16,18},{18,... | collective-permute-start | bytes 786440 | tf_op jit(solution)/shard_map/ppermute | solution.py:410
  6.6 10.1 %copy-start.1 = (bf16[16,2,256,256]{3,2,1,0:T(8,128)(2,1)S(1)}, bf16[16,2,256,256]{3,2,1,0:T(8,128)(2,1)}, u32[]{:S(2)}) copy-start(bf16[16,2,256,256]{3,2,1,0:T(8,128)(2,1)} %weight_ref.1) | copy-start | bytes 12582916
  6.7 49.6 %collective-permute-start.7 = (bf16[512,8,256]{2,1,0:T(8,128)(2,1)S(1)}, bf16[512,8,256]{2,1,0:T(8,128)(2,1)S(1)}, u32[]{:S(2)}, u32[]{:S(2)}) collective-permute-start(bf16[512,8,256]{2,1,0:T(8,128)(2,1)S(1)} %hold.1.refs_0_), channel_id=1, source_target_pairs={{0,1},{1,0},{2,3},{3,2},{4,5},{5,4},{6,7},{7,6},{8,9},{9,8},{10,11... | collective-permute-start | bytes 6291464 | tf_op jit(solution)/shard_map/ppermute | solution.py:427
  9.4 5.7 %collective-permute-start.1 = (bf16[16,2,8,256]{3,2,1,0:T(8,128)(2,1)S(1)}, bf16[16,2,8,256]{3,2,1,0:T(8,128)(2,1)S(1)}, u32[]{:S(2)}, u32[]{:S(2)}) collective-permute-start(bf16[16,2,8,256]{3,2,1,0:T(8,128)(2,1)S(1)} %get-tuple-element.21), channel_id=1, source_target_pairs={{0,4},{2,6},{4,0},{6,2},{8,12},{10,14},{12,8},{14,10},{16,20},{18,... | collective-permute-start | bytes 393224 | tf_op jit(solution)/shard_map/ppermute | solution.py:410
  15.1 4.3 %collective-permute-start.2 = (bf16[8,2,8,256]{3,2,1,0:T(8,128)(2,1)S(1)}, bf16[8,2,8,256]{3,2,1,0:T(8,128)(2,1)S(1)}, u32[]{:S(2)}, u32[]{:S(2)}) collective-permute-start(bf16[8,2,8,256]{3,2,1,0:T(8,128)(2,1)S(1)} %get-tuple-element.23), channel_id=1, source_target_pairs={{0,8},{2,10},{4,12},{6,14},{8,0},{10,2},{12,4},{14,6},{16,24},{18,... | collective-permute-start | bytes 196616 | tf_op jit(solution)/shard_map/ppermute | solution.py:410
  17.7 18.3 %copy-start.2 = (bf16[256,1024]{1,0:T(8,128)(2,1)S(1)}, bf16[256,1024]{1,0:T(8,128)(2,1)}, u32[]{:S(2)}) copy-start(bf16[256,1024]{1,0:T(8,128)(2,1)} %w_in_ref.3) | copy-start | bytes 1572868
  17.7 18.3 %copy-start.3 = (bf16[1024,256]{1,0:T(8,128)(2,1)S(1)}, bf16[1024,256]{1,0:T(8,128)(2,1)}, u32[]{:S(2)}) copy-start(bf16[1024,256]{1,0:T(8,128)(2,1)} %w_out_ref.3) | copy-start | bytes 1572868
  17.7 18.3 %copy-start.5 = (f32[3,256]{1,0:T(4,128)S(1)}, f32[3,256]{1,0:T(4,128)}, u32[]{:S(2)}) copy-start(f32[3,256]{1,0:T(4,128)} %taps_ref.3) | copy-start | bytes 9220
  17.7 18.2 %copy-start.6 = (f32[1024]{0:T(1024)S(1)}, f32[1024]{0:T(1024)}, u32[]{:S(2)}) copy-start(f32[1024]{0:T(1024)} %param.13) | copy-start | bytes 12292
  17.7 18.2 %copy-start.7 = (f32[256]{0:T(256)S(1)}, f32[256]{0:T(256)}, u32[]{:S(2)}) copy-start(f32[256]{0:T(256)} %param.15) | copy-start | bytes 3076
  17.7 18.2 %copy-start.8 = (s32[4,9,6]{2,1,0:T(8,128)S(1)}, s32[4,9,6]{2,1,0:T(8,128)}, u32[]{:S(2)}) copy-start(s32[4,9,6]{2,1,0:T(8,128)} %constant.25.clone.items_ref) | copy-start | bytes 2596
  19.4 5.2 %collective-permute-start.3 = (bf16[8,2,8,256]{3,2,1,0:T(8,128)(2,1)S(1)}, bf16[8,2,8,256]{3,2,1,0:T(8,128)(2,1)S(1)}, u32[]{:S(2)}, u32[]{:S(2)}) collective-permute-start(bf16[8,2,8,256]{3,2,1,0:T(8,128)(2,1)S(1)} %get-tuple-element.26), channel_id=1, source_target_pairs={{0,16},{2,18},{4,20},{6,22},{8,24},{10,26},{12,28},{14,30},{16,0},... | collective-permute-start | bytes 196616 | tf_op jit(solution)/shard_map/ppermute | solution.py:410
  24.9 4.3 %collective-permute-start.4 = (bf16[8,2,8,256]{3,2,1,0:T(8,128)(2,1)S(1)}, bf16[8,2,8,256]{3,2,1,0:T(8,128)(2,1)S(1)}, u32[]{:S(2)}, u32[]{:S(2)}) collective-permute-start(bf16[8,2,8,256]{3,2,1,0:T(8,128)(2,1)S(1)} %mix.1.mine_ref), channel_id=1, source_target_pairs={{0,8},{2,10},{4,12},{6,14},{8,0},{10,2},{12,4},{14,6},{16,24},{18,... | collective-permute-start | bytes 196616 | tf_op jit(solution)/shard_map/ppermute | solution.py:410
  29.3 5.0 %collective-permute-start.5 = (bf16[16,2,8,256]{3,2,1,0:T(8,128)(2,1)S(1)}, bf16[16,2,8,256]{3,2,1,0:T(8,128)(2,1)S(1)}, u32[]{:S(2)}, u32[]{:S(2)}) collective-permute-start(bf16[16,2,8,256]{3,2,1,0:T(8,128)(2,1)S(1)} %join.1.refs_0_), channel_id=1, source_target_pairs={{0,4},{2,6},{4,0},{6,2},{8,12},{10,14},{12,8},{14,10},{16,20},{18,... | collective-permute-start | bytes 393224 | tf_op jit(solution)/shard_map/ppermute | solution.py:410
  34.3 1.6 %collective-permute-start.6 = (bf16[2,256,256]{2,1,0:T(8,128)(2,1)S(1)}, bf16[2,256,256]{2,1,0:T(8,128)(2,1)S(1)}, u32[]{:S(2)}, u32[]{:S(2)}) collective-permute-start(bf16[2,256,256]{2,1,0:T(8,128)(2,1)S(1)} %stack.1.mine_ref), channel_id=1, source_target_pairs={{0,2},{2,0},{4,6},{6,4},{8,10},{10,8},{12,14},{14,12},{16,18},{18,... | collective-permute-start | bytes 786440 | tf_op jit(solution)/shard_map/ppermute | solution.py:410
  36.0 20.4 %copy-start.4 = (s32[4,9,2]{2,1,0:T(8,128)S(1)}, s32[4,9,2]{2,1,0:T(8,128)}, u32[]{:S(2)}) copy-start(s32[4,9,2]{2,1,0:T(8,128)} %constant.26.clone.items_ref) | copy-start | bytes 868
